TPU v7x, 32 devices: a whole 2x2x4 slice. The times are simulated.
32 devices in a mesh: shard: 2 (over core), ctx: 4 (over y, x), tp: 4 (over z).
Axes of the slice: x: 2, y: 2, z: 4, core: 2. Of those that a mesh axis runs over, the one named last changes fastest.
Arguments:
- hidden_in: bfloat16 [4, 1024, 2048], P('shard', 'ctx'), may hold values from -6 to 6
- lengths: int32 [4], P('shard'), may hold values from 256 to 1024, as said below
- cotangent: bfloat16 [4, 1024, 2048], P('shard', 'ctx'), may hold values from -6 to 6
- norm_gain: bfloat16 [2048], P('shard'), may hold values from 0.5 to 1.5
- in_weight: bfloat16 [2048, 2, 4096], P('shard', None, 'tp'), may hold values from -0.125 to 0.125
- conv_weight: bfloat16 [4, 4096], P(None, ('tp', 'shard')), may hold values from -3 to 3
- conv_bias: bfloat16 [4096], P(('tp', 'shard')), may hold values from -3 to 3
- low_weight: bfloat16 [160, 4096], P(None, ('tp', 'shard')), may hold values from -0.09375 to 0.09375
- step_weight: bfloat16 [128, 4096], P(None, ('tp', 'shard')), may hold values from -0.5 to 0.5
- step_bias: bfloat16 [4096], P(('tp', 'shard')), may hold values from -10 to -2
- decay_log: bfloat16 [16, 4096], P(None, ('tp', 'shard')), may hold values from -2 to 2
- skip_gain: bfloat16 [4096], P(('tp', 'shard')), may hold values from 0.25 to 1.75
- out_weight: bfloat16 [4096, 2048], P('tp', 'shard'), may hold values from -0.1875 to 0.1875
- ffn_gain: bfloat16 [2048], P('shard'), may hold values from 0.5 to 1.5
- gate_up: bfloat16 [2048, 2, 4096], P('shard', None, 'tp'), may hold values from -0.125 to 0.125
- down_weight: bfloat16 [4096, 2048], P('tp', 'shard'), may hold values from -0.09375 to 0.09375
Outputs:
- mixed_out: bfloat16 [4, 1024, 2048], P('shard', 'ctx')
- input_grad: float32 [4, 1024, 2048], P('shard', 'ctx')
- norm_gain_grad: float32 [2048], P(('shard', 'ctx'))
- in_weight_grad: float32 [2048, 2, 4096], P(('shard', 'ctx'), None, 'tp')
- conv_weight_grad: float32 [4, 4096], P(None, ('tp', 'shard', 'ctx'))
- conv_bias_grad: float32 [4096], P(('tp', 'shard', 'ctx'))
- low_weight_grad: float32 [160, 4096], P(None, ('tp', 'shard', 'ctx'))
- step_weight_grad: float32 [128, 4096], P(None, ('tp', 'shard', 'ctx'))
- step_bias_grad: float32 [4096], P(('tp', 'shard', 'ctx'))
- decay_log_grad: float32 [16, 4096], P(None, ('tp', 'shard', 'ctx'))
- skip_gain_grad: float32 [4096], P(('tp', 'shard', 'ctx'))
- out_weight_grad: float32 [4096, 2048], P('tp', ('shard', 'ctx'))
- ffn_gain_grad: float32 [2048], P(('shard', 'ctx'))
- gate_up_grad: float32 [2048, 2, 4096], P(('shard', 'ctx'), None, 'tp')
- down_grad: float32 [4096, 2048], P('tp', ('shard', 'ctx'))
Inputs may be any that keep to these rules, and one draw needn't show every extreme that they name: `lengths`: in each aligned group of 2 sequences one uses all 1024 slots; slots at or past a sequence's length are padding.
All inputs are finite; a program needn't handle non-finite values.
Results may differ from a plain program's by a relative error of at most 0.017.
Values may be sent and summed in bfloat16 or wider, within the bound.
A program may use at most 320 MiB of HBM per device.

v0:
```python
import jax
import jax.numpy as jnp
from jax import lax
from jax.sharding import PartitionSpec as P

epsilon = 1e-05
block_len = 8


def passed_along(value, axis, steps):
    count = lax.axis_size(axis)
    initial, last = (max(0, -steps), min(count, count - steps))
    return lax.ppermute(value, axis, [(source, source + steps) for source in range(initial, last)])


def prefix(shard, axis, combine, identity, reverse):
    count, here = (lax.axis_size(axis), lax.axis_index(axis))
    everything = jax.tree.map(lambda part: lax.all_gather(part, axis), shard)
    start = jax.tree.map(
        lambda part, zero: jnp.broadcast_to(jnp.asarray(zero, part.dtype), part.shape),
        shard,
        identity,
    )

    def turn(k, before):
        at = count - 1 - k if reverse else k
        reached = at > here if reverse else at < here
        new = combine(before, jax.tree.map(lambda part: part[at], everything))
        return jax.tree.map(lambda a, b: jnp.where(reached, a, b), new, before)

    return lax.fori_loop(0, count, turn, start)


def inner_rows(left, right):
    return lax.dot_general(
        left, right, (((0,), (0,)), ((), ())), preferred_element_type=jnp.float32
    )


def outer_cols(left, right):
    return lax.dot_general(
        left, right, (((1,), (1,)), ((), ())), preferred_element_type=jnp.float32
    )


def silu_grad(values):
    sig_val = jax.nn.sigmoid(values)
    return sig_val * (1.0 + values * (1.0 - sig_val))


def rms_scale(source):
    return lax.rsqrt(jnp.mean(source * source, axis=-1, keepdims=True) + epsilon)


def norm_back(upstream, source, inv_rms, gain_full):
    weighted = upstream * gain_full
    gain_grad = jnp.sum(upstream * source * inv_rms, axis=0)
    inv_cubed = inv_rms * inv_rms * inv_rms
    input_back = inv_rms * weighted - source * inv_cubed * jnp.mean(
        weighted * source, axis=-1, keepdims=True
    )
    return (input_back, gain_grad)


def chain_join(earlier, later):
    return (earlier[0] * later[0], later[0] * earlier[1] + later[1])


def run_forward(size_blk, drive_blk, b_blk, decay_rate, carried):
    states = []
    for slot_at in range(block_len):
        carried = (
            jnp.exp(size_blk[:, :, slot_at, None, :] * decay_rate) * carried
            + drive_blk[:, :, slot_at, None, :] * b_blk[:, :, slot_at, :, None]
        )
        states.append(carried)
    return states


def body(
    hidden_in,
    lengths,
    cotangent,
    norm_gain,
    in_weight,
    conv_weight,
    conv_bias,
    low_weight,
    step_weight,
    step_bias,
    decay_log,
    skip_gain,
    out_weight,
    ffn_gain,
    gate_up,
    down_weight,
):
    (
        norm_w,
        in_w,
        conv_w,
        conv_b,
        low_w,
        step_w,
        step_b,
        decay_w,
        skip_w,
        out_w,
        ffn_w,
        gate_w,
        down_w,
    ) = (
        lax.all_gather(norm_gain, "shard", axis=0, tiled=True),
        lax.all_gather(in_weight, "shard", axis=0, tiled=True),
        lax.all_gather(conv_weight, "shard", axis=1, tiled=True),
        lax.all_gather(conv_bias, "shard", axis=0, tiled=True),
        lax.all_gather(low_weight, "shard", axis=1, tiled=True),
        lax.all_gather(step_weight, "shard", axis=1, tiled=True),
        lax.all_gather(step_bias, "shard", axis=0, tiled=True),
        lax.all_gather(decay_log, "shard", axis=1, tiled=True),
        lax.all_gather(skip_gain, "shard", axis=0, tiled=True),
        lax.all_gather(out_weight, "shard", axis=1, tiled=True),
        lax.all_gather(ffn_gain, "shard", axis=0, tiled=True),
        lax.all_gather(gate_up, "shard", axis=0, tiled=True),
        lax.all_gather(down_weight, "shard", axis=1, tiled=True),
    )
    seq_count, local_len, model_width = hidden_in.shape
    row_count = seq_count * local_len
    inner_loc = in_w.shape[2]
    ffn_loc = gate_w.shape[2]
    kernel_len = conv_w.shape[0]
    rank_len = step_w.shape[0]
    state_len = decay_w.shape[0]
    block_count = local_len // block_len
    first_slot = lax.axis_index("ctx") * local_len
    positions = first_slot + jnp.arange(local_len, dtype=jnp.int32)
    pad_mask = (positions[None, :] < lengths[:, None]).astype(jnp.float32)
    source = hidden_in.reshape(row_count, model_width).astype(jnp.float32)
    inv_one = rms_scale(source)
    gain_one = norm_w.astype(jnp.float32)
    normed_one = (source * inv_one * gain_one).astype(jnp.bfloat16)
    project = jnp.dot(
        normed_one, in_w.reshape(model_width, 2 * inner_loc), preferred_element_type=jnp.float32
    )
    conv_in = project[:, :inner_loc].astype(jnp.bfloat16).reshape(seq_count, local_len, inner_loc)
    gate_z = project[:, inner_loc:]
    edge_in = passed_along(conv_in[:, local_len - kernel_len + 1 :], "ctx", 1)
    padded = jnp.concatenate([edge_in, conv_in], axis=1).astype(jnp.float32)
    kernel = conv_w.astype(jnp.float32)
    pre_act = conv_b.astype(jnp.float32) + sum(
        (
            kernel[kernel_at] * padded[:, kernel_at : kernel_at + local_len]
            for kernel_at in range(kernel_len)
        )
    )
    pre_act = pre_act.reshape(row_count, inner_loc)
    act_half = jax.nn.silu(pre_act).astype(jnp.bfloat16)
    act_full = act_half.astype(jnp.float32)
    low_all = lax.psum(outer_cols(act_half, low_w), "tp")
    step_low = low_all[:, :rank_len].astype(jnp.bfloat16)
    b_in = low_all[:, rank_len : rank_len + state_len]
    c_out = low_all[:, rank_len + state_len :]
    step_pre = jnp.dot(step_low, step_w, preferred_element_type=jnp.float32) + step_b.astype(
        jnp.float32
    )
    step_size = jax.nn.softplus(step_pre)
    decay_rate = -jnp.exp(decay_w.astype(jnp.float32))

    def blocked(values):
        return values.reshape((seq_count, block_count, block_len) + values.shape[1:])

    def unblock(pieces):
        return jnp.stack(pieces, axis=2).reshape((row_count,) + pieces[0].shape[2:])

    size_blk = blocked(step_size)
    act_blk = blocked(act_full)
    drive_blk = size_blk * act_blk
    b_blk = blocked(b_in)
    c_blk = blocked(c_out)
    zero_state = jnp.zeros((seq_count, block_count, state_len, inner_loc), jnp.float32)
    block_ends = run_forward(size_blk, drive_blk, b_blk, decay_rate, zero_state)[-1]
    block_sum = jnp.sum(size_blk, axis=2)
    block_decay = jnp.exp(block_sum[:, :, None, :] * decay_rate)
    inclusive = lax.associative_scan(chain_join, (block_decay, block_ends), axis=1)
    device_pair = (inclusive[0][:, -1], inclusive[1][:, -1])
    identity = (jnp.ones_like(device_pair[0]), jnp.zeros_like(device_pair[1]))
    entering = prefix(device_pair, "ctx", chain_join, identity, False)[1]
    before = jnp.cumsum(block_sum, axis=1) - block_sum
    shifted = jnp.concatenate([jnp.zeros_like(block_ends[:, :1]), inclusive[1][:, :-1]], axis=1)
    block_start = shifted + jnp.exp(before[:, :, None, :] * decay_rate) * entering[:, None]
    states = run_forward(size_blk, drive_blk, b_blk, decay_rate, block_start)
    scan_y = unblock(
        [
            jnp.sum(states[slot_at] * c_blk[:, :, slot_at, :, None], axis=2)
            for slot_at in range(block_len)
        ]
    )
    skip_full = skip_w.astype(jnp.float32)
    scan_out = scan_y + skip_full * act_full
    gate_act = jax.nn.silu(gate_z)
    gated_out = (scan_out * gate_act).astype(jnp.bfloat16)
    mixed_sum = lax.psum(jnp.dot(gated_out, out_w, preferred_element_type=jnp.float32), "tp")
    middle = source + mixed_sum
    inv_two = rms_scale(middle)
    gain_two = ffn_w.astype(jnp.float32)
    normed_two = (middle * inv_two * gain_two).astype(jnp.bfloat16)
    gate_flat = gate_w.reshape(model_width, 2 * ffn_loc)
    gate_val = jnp.dot(normed_two, gate_flat, preferred_element_type=jnp.float32)
    gate_lin = gate_val[:, :ffn_loc]
    up_lin = gate_val[:, ffn_loc:]
    hidden_ffn = (jax.nn.silu(gate_lin) * up_lin).astype(jnp.bfloat16)
    ffn_out = lax.psum(jnp.dot(hidden_ffn, down_w, preferred_element_type=jnp.float32), "tp")
    mixed_out = (middle + ffn_out).astype(jnp.bfloat16).reshape(hidden_in.shape)
    upstream = cotangent.reshape(row_count, model_width).astype(jnp.float32) * pad_mask.reshape(
        row_count, 1
    )
    ffn_grad = upstream.astype(jnp.bfloat16)
    down_grad = inner_rows(hidden_ffn, ffn_grad)
    hidden_grad = outer_cols(ffn_grad, down_w)
    gate_grad = hidden_grad * up_lin * silu_grad(gate_lin)
    up_grad = hidden_grad * jax.nn.silu(gate_lin)
    both_grad = jnp.concatenate([gate_grad, up_grad], axis=1).astype(jnp.bfloat16)
    gate_up_grad = inner_rows(normed_two, both_grad).reshape(gate_w.shape)
    normed_two_grad = lax.psum(outer_cols(both_grad, gate_flat), "tp")
    middle_back, ffn_gain_grad = norm_back(normed_two_grad, middle, inv_two, gain_two)
    middle_grad = upstream + middle_back
    mix_grad = middle_grad.astype(jnp.bfloat16)
    out_weight_grad = inner_rows(gated_out, mix_grad)
    gated_grad = outer_cols(mix_grad, out_w)
    scan_grad = gated_grad * gate_act
    z_grad = gated_grad * scan_out * silu_grad(gate_z)
    skip_gain_grad = jnp.sum(scan_grad * act_full, axis=0)
    grad_blk = blocked(scan_grad)

    def term_at(slot_at):
        return c_blk[:, :, slot_at, :, None] * grad_blk[:, :, slot_at, None, :]

    def decay_at(slot_at):
        return jnp.exp(size_blk[:, :, slot_at, None, :] * decay_rate)

    adjoint = zero_state
    for slot_at in reversed(range(block_len)):
        adjoint = decay_at(slot_at) * (term_at(slot_at) + adjoint)
    reverse_incl = lax.associative_scan(chain_join, (block_decay, adjoint), reverse=True, axis=1)
    device_back = (reverse_incl[0][:, 0], reverse_incl[1][:, 0])
    leaving = prefix(device_back, "ctx", chain_join, identity, True)[1]
    after_sum = jnp.sum(block_sum, axis=1, keepdims=True) - jnp.cumsum(block_sum, axis=1)
    later_sum = jnp.concatenate([reverse_incl[1][:, 1:], jnp.zeros_like(adjoint[:, :1])], axis=1)
    adjoint = later_sum + jnp.exp(after_sum[:, :, None, :] * decay_rate) * leaving[:, None]
    size_grads = [None] * block_len
    act_grads = [None] * block_len
    b_grads = [None] * block_len
    c_grads = [None] * block_len
    decay_acc = jnp.zeros_like(decay_rate)
    for slot_at in reversed(range(block_len)):
        decay_now = decay_at(slot_at)
        total_adj = term_at(slot_at) + adjoint
        prior_state = states[slot_at - 1] if slot_at > 0 else block_start
        c_grads[slot_at] = jnp.sum(states[slot_at] * grad_blk[:, :, slot_at, None, :], axis=3)
        b_grads[slot_at] = jnp.sum(total_adj * drive_blk[:, :, slot_at, None, :], axis=3)
        through_b = jnp.sum(total_adj * b_blk[:, :, slot_at, :, None], axis=2)
        through_decay = total_adj * prior_state * decay_now
        size_grads[slot_at] = act_blk[:, :, slot_at] * through_b + jnp.sum(
            through_decay * decay_rate, axis=2
        )
        act_grads[slot_at] = size_blk[:, :, slot_at] * through_b
        decay_acc = decay_acc + jnp.sum(
            through_decay * size_blk[:, :, slot_at, None, :], axis=(0, 1)
        )
        adjoint = decay_now * total_adj
    decay_log_grad = decay_acc * decay_rate
    step_grad = (unblock(size_grads) * jax.nn.sigmoid(step_pre)).astype(jnp.bfloat16)
    step_bias_grad = jnp.sum(step_grad.astype(jnp.float32), axis=0)
    step_weight_grad = inner_rows(step_low, step_grad)
    low_part = jnp.concatenate(
        [outer_cols(step_grad, step_w), unblock(b_grads), unblock(c_grads)], axis=1
    )
    low_grad = lax.psum(low_part, "tp").astype(jnp.bfloat16)
    low_weight_grad = inner_rows(low_grad, act_half)
    act_grad = (
        skip_full * scan_grad
        + unblock(act_grads)
        + jnp.dot(low_grad, low_w, preferred_element_type=jnp.float32)
    )
    pre_grad = (act_grad * silu_grad(pre_act)).reshape(seq_count, local_len, inner_loc)
    conv_bias_grad = jnp.sum(pre_grad, axis=(0, 1))
    conv_weight_grad = jnp.stack(
        [
            jnp.sum(pre_grad * padded[:, kernel_at : kernel_at + local_len], axis=(0, 1))
            for kernel_at in range(kernel_len)
        ]
    )
    padded_grad = sum(
        (
            jnp.pad(
                kernel[kernel_at] * pre_grad,
                ((0, 0), (kernel_at, kernel_len - 1 - kernel_at), (0, 0)),
            )
            for kernel_at in range(kernel_len)
        )
    )
    edge_back = passed_along(padded_grad[:, : kernel_len - 1], "ctx", -1)
    conv_grad = padded_grad[:, kernel_len - 1 :] + jnp.pad(
        edge_back, ((0, 0), (local_len - kernel_len + 1, 0), (0, 0))
    )
    project_grad = jnp.concatenate(
        [conv_grad.reshape(row_count, inner_loc), z_grad], axis=1
    ).astype(jnp.bfloat16)
    in_weight_grad = inner_rows(normed_one, project_grad).reshape(in_w.shape)
    normed_one_grad = lax.psum(
        outer_cols(project_grad, in_w.reshape(model_width, 2 * inner_loc)), "tp"
    )
    source_back, norm_gain_grad = norm_back(normed_one_grad, source, inv_one, gain_one)
    input_grad = (middle_grad + source_back).reshape(hidden_in.shape)
    weight_grads = (
        norm_gain_grad,
        in_weight_grad,
        conv_weight_grad,
        conv_bias_grad,
        low_weight_grad,
        step_weight_grad,
        step_bias_grad,
        decay_log_grad,
        skip_gain_grad,
        out_weight_grad,
        ffn_gain_grad,
        gate_up_grad,
        down_grad,
    )
    results = (
        lax.psum_scatter(weight_grads[0], ("shard", "ctx"), scatter_dimension=0, tiled=True),
        lax.psum_scatter(weight_grads[1], ("shard", "ctx"), scatter_dimension=0, tiled=True),
        lax.psum_scatter(weight_grads[2], ("shard", "ctx"), scatter_dimension=1, tiled=True),
        lax.psum_scatter(weight_grads[3], ("shard", "ctx"), scatter_dimension=0, tiled=True),
        lax.psum_scatter(weight_grads[4], ("shard", "ctx"), scatter_dimension=1, tiled=True),
        lax.psum_scatter(weight_grads[5], ("shard", "ctx"), scatter_dimension=1, tiled=True),
        lax.psum_scatter(weight_grads[6], ("shard", "ctx"), scatter_dimension=0, tiled=True),
        lax.psum_scatter(weight_grads[7], ("shard", "ctx"), scatter_dimension=1, tiled=True),
        lax.psum_scatter(weight_grads[8], ("shard", "ctx"), scatter_dimension=0, tiled=True),
        lax.psum_scatter(weight_grads[9], ("shard", "ctx"), scatter_dimension=1, tiled=True),
        lax.psum_scatter(weight_grads[10], ("shard", "ctx"), scatter_dimension=0, tiled=True),
        lax.psum_scatter(weight_grads[11], ("shard", "ctx"), scatter_dimension=0, tiled=True),
        lax.psum_scatter(weight_grads[12], ("shard", "ctx"), scatter_dimension=1, tiled=True),
    )
    return (
        mixed_out,
        input_grad,
        results[0],
        results[1],
        results[2],
        results[3],
        results[4],
        results[5],
        results[6],
        results[7],
        results[8],
        results[9],
        results[10],
        results[11],
        results[12],
    )


def solution(mesh):
    placed = (
        P("shard", "ctx", None),
        P("shard"),
        P("shard", "ctx", None),
        P("shard"),
        P("shard", None, "tp"),
        P(None, ("tp", "shard")),
        P(("tp", "shard")),
        P(None, ("tp", "shard")),
        P(None, ("tp", "shard")),
        P(("tp", "shard")),
        P(None, ("tp", "shard")),
        P(("tp", "shard")),
        P("tp", "shard"),
        P("shard"),
        P("shard", None, "tp"),
        P("tp", "shard"),
    )
    return jax.shard_map(
        body,
        mesh=mesh,
        in_specs=placed,
        out_specs=(
            P("shard", "ctx", None),
            P("shard", "ctx", None),
            P(("shard", "ctx")),
            P(("shard", "ctx"), None, "tp"),
            P(None, ("tp", "shard", "ctx")),
            P(("tp", "shard", "ctx")),
            P(None, ("tp", "shard", "ctx")),
            P(None, ("tp", "shard", "ctx")),
            P(("tp", "shard", "ctx")),
            P(None, ("tp", "shard", "ctx")),
            P(("tp", "shard", "ctx")),
            P("tp", ("shard", "ctx")),
            P(("shard", "ctx")),
            P(("shard", "ctx"), None, "tp"),
            P("tp", ("shard", "ctx")),
        ),
        check_vma=False,
    )
```

profile of v0, /device:TPU:0, one launch (start us, length us, event | category | flops | bytes accessed | tf_op | source)
XLA Modules:
  0.0 2029.6 jit_solution(9802803220888365158)
XLA Ops:
  14.8 17.4 all-gather.12.cloned.1.call-done
  74.4 24.7 %all-reduce.62.cloned.1.call-done = f32[512,160]{0,1:T(8,128)} async-done(((f32[512,160]{0,1:T(8,128)}), f32[512,160]{0,1:T(8,128)}) %all-reduce.62.cloned.1.call-update) | async-done | bytes 327696 | tf_op jit(solution)/shard_map/psum | solution.py:159
  221.5 12.2 pad.363
  267.1 18.7 pad.361
  287.3 18.5 pad.154
  340.6 13.7 multiply_reduce_fusion.43
  389.7 138.5 %all-reduce.64.cloned.1.call-done = f32[512,2048]{1,0:T(8,128)} async-done(((f32[512,2048]{1,0:T(8,128)}), f32[512,2048]{1,0:T(8,128)}) %all-reduce.64.cloned.1.call-update) | async-done | bytes 4194320 | tf_op jit(solution)/shard_map/psum | solution.py:202
  557.7 156.1 %all-reduce.66.cloned.1.call-done = f32[512,2048]{1,0:T(8,128)} async-done(((f32[512,2048]{1,0:T(8,128)}), f32[512,2048]{1,0:T(8,128)}) %all-reduce.66.cloned.1.call-update) | async-done | bytes 4194320 | tf_op jit(solution)/shard_map/psum | solution.py:224
  875.3 18.6 pad.365
  949.7 12.9 multiply_multiply_fusion.8
  983.5 14.3 multiply_reduce_fusion.5
  999.3 13.0 multiply_reduce_fusion.7
  1064.1 21.9 %all-reduce.71 = bf16[512,160]{0,1:T(8,128)(2,1)} all-reduce(f32[512,160]{0,1:T(8,128)S(1)} %pad_maximum_fusion.17), channel_id=1, replica_groups=mesh['shard'=2,'ctx'=4,'tp'=4] {'tp'}, use_global_device_ids=true, to_apply=%region_54.55 | all-reduce | flops 81920 | bytes 491520 | tf_op jit(solution)/shard_map/psum | solution.py:278
  1103.7 25.4 %copy.399 = f32[2048,2,1024]{2,1,0:T(2,128)} copy(f32[2048,2,1024]{0,2,1:T(8,128)} %bitcast.384) | data formatting | bytes 33554432 | tf_op jit(solution)/shard_map/reshape | solution.py:223
  1157.4 13.0 fusion.124
  1196.1 151.6 %all-reduce.68.cloned.1.call-done = f32[2048,2,1024]{2,1,0:T(2,128)} async-done(((f32[2048,2,1024]{2,1,0:T(2,128)}), f32[2048,2,1024]{2,1,0:T(2,128)}) %all-reduce.68.cloned.1.call-update) | async-done | bytes 16777232
  1351.4 291.0 %all-reduce.70.cloned.1.call-done = (f32[512,2048]{1,0:T(8,128)}, f32[512,2048]{1,0:T(8,128)}) async-done(((f32[512,2048]{1,0:T(8,128)}, f32[512,2048]{1,0:T(8,128)}), (f32[512,2048]{1,0:T(8,128)}, f32[512,2048]{1,0:T(8,128)})) %all-reduce.70.cloned.1.call-update) | async-done | bytes 8388624 | tf_op jit(solution)/shard_map/psum | solution.py:212
  1645.8 26.5 %all-reduce.53 = (f32[2048]{0:T(1024)S(1)}, f32[1024]{0:T(1024)S(1)}, f32[1024]{0:T(1024)S(1)}, f32[1024]{0:T(1024)S(1)}, f32[2048]{0:T(1024)S(1)}) all-reduce(f32[2048]{0:T(1024)S(1)} %get-tuple-element.357, f32[1024]{0:T(1024)S(1)} %get-tuple-element.587, ...), channel_id=6, replica_groups=mesh['shard'=2,'ctx'=4,'tp'=4] {'shard','ctx'}, use_global_device_ids=true, to_apply=%region_58.59.clone | all-reduce | flops 7168 | bytes 57344
  1685.5 75.4 %reduce-scatter.10.cloned.1.call-done = f32[256,2,1024]{2,0,1:T(8,128)} async-done(((f32[2048,2,1024]{2,0,1:T(8,128)}), f32[256,2,1024]{2,0,1:T(8,128)}) %reduce-scatter.10.cloned.1.call-update) | async-done | bytes 2097168 | tf_op jit(solution)/shard_map/reduce_scatter | solution.py:332
  1765.5 30.4 %reduce-scatter.16.cloned.1.call-done = f32[16,128]{1,0:T(8,128)} async-done(((f32[16,1024]{1,0:T(8,128)}), f32[16,128]{1,0:T(8,128)}) %reduce-scatter.16.cloned.1.call-update) | async-done | bytes 8208 | tf_op jit(solution)/shard_map/reduce_scatter | solution.py:338
  1795.8 38.1 %reduce-scatter.14.cloned.1.call-done = f32[128,128]{1,0:T(8,128)} async-done(((f32[128,1024]{1,0:T(8,128)}), f32[128,128]{1,0:T(8,128)}) %reduce-scatter.14.cloned.1.call-update) | async-done | bytes 65552 | tf_op jit(solution)/shard_map/reduce_scatter | solution.py:336
  1834.0 38.1 %reduce-scatter.12.cloned.1.call-done = f32[160,128]{1,0:T(8,128)} async-done(((f32[160,1024]{1,0:T(8,128)}), f32[160,128]{1,0:T(8,128)}) %reduce-scatter.12.cloned.1.call-update) | async-done | bytes 81936 | tf_op jit(solution)/shard_map/reduce_scatter | solution.py:335
  1872.1 75.2 %reduce-scatter.20.cloned.1.call-done = f32[1024,256]{1,0:T(8,128)} async-done(((f32[1024,2048]{1,0:T(8,128)}), f32[1024,256]{1,0:T(8,128)}) %reduce-scatter.20.cloned.1.call-update) | async-done | bytes 1048592 | tf_op jit(solution)/shard_map/reduce_scatter | solution.py:343
  1947.3 75.6 %reduce-scatter.18.cloned.1.call-done = f32[1024,256]{1,0:T(8,128)} async-done(((f32[1024,2048]{1,0:T(8,128)}), f32[1024,256]{1,0:T(8,128)}) %reduce-scatter.18.cloned.1.call-update) | async-done | bytes 1048592 | tf_op jit(solution)/shard_map/reduce_scatter | solution.py:340
  (806 shorter events, 698.8 us)
Async XLA Ops:
  7.2 25.0 %all-gather.12.cloned.1.call-start = ((), (), s32[]{:S(2)}) async-start(), calls=%async_computation.7 | async-start | bytes 12582912 | tf_op jit(solution)/shard_map/all_gather | solution.py:114
  7.9 91.2 %all-reduce.62.cloned.1.call-start = ((), (), s32[]{:S(2)}) async-start(), calls=%async_computation.8 | async-start | bytes 655360 | tf_op jit(solution)/shard_map/psum | solution.py:159
  49.7 7.5 collective-permute-start
  62.8 304.4 %all-gather.14.cloned.1.call-start = ((), (), s32[]{:S(2)}) async-start(), calls=%async_computation.9 | async-start | bytes 6291456 | tf_op jit(solution)/shard_map/all_gather | solution.py:122
  63.5 315.8 %all-gather.16.cloned.1.call-start = ((), (), s32[]{:S(2)}) async-start(), calls=%async_computation.11 | async-start | bytes 12582912 | tf_op jit(solution)/shard_map/all_gather | solution.py:124
  64.1 464.1 %all-reduce.64.cloned.1.call-start = ((), (), s32[]{:S(2)}) async-start(), calls=%async_computation.10 | async-start | bytes 8388608 | tf_op jit(solution)/shard_map/psum | solution.py:202
  72.1 292.4 %copy-start.210 = (f32[2,1,512]{2,1,0:T(1,128)}, f32[2,1,512]{2,1,0:T(1,128)S(1)}, u32[]{:S(2)}) copy-start(f32[2,1,512]{2,1,0:T(1,128)S(1)} %convert_element_type.146) | copy-start | bytes 12292
  374.6 167.7 %all-gather.18.cloned.1.call-start = ((), (), s32[]{:S(2)}) async-start(), calls=%async_computation.12 | async-start | bytes 6291456 | tf_op jit(solution)/shard_map/all_gather | solution.py:125
  375.2 338.6 %all-reduce.66.cloned.1.call-start = ((), (), s32[]{:S(2)}) async-start(), calls=%async_computation.13 | async-start | bytes 8388608 | tf_op jit(solution)/shard_map/psum | solution.py:224
  557.5 637.1 %reduce-scatter.22.cloned.1.call-start = ((), (), s32[]{:S(2)}) async-start(), calls=%async_computation.20 | async-start | bytes 589824
  1092.7 255.1 %all-reduce.68.cloned.1.call-start = ((), (), s32[]{:S(2)}) async-start(), calls=%async_computation.21 | async-start | bytes 33554432
  1129.1 513.2 %all-reduce.70.cloned.1.call-start = ((), (), s32[]{:S(2)}) async-start(), calls=%async_computation.22 | async-start | bytes 16777216 | tf_op jit(solution)/shard_map/psum | solution.py:212
  1138.3 6.9 collective-permute-start.1
  1152.7 608.2 %reduce-scatter.10.cloned.1.call-start = ((), (), s32[]{:S(2)}) async-start(), calls=%async_computation.14 | async-start | bytes 18874368 | tf_op jit(solution)/shard_map/reduce_scatter | solution.py:332
  1170.5 625.3 %reduce-scatter.16.cloned.1.call-start = ((), (), s32[]{:S(2)}) async-start(), calls=%async_computation.17 | async-start | bytes 73728 | tf_op jit(solution)/shard_map/reduce_scatter | solution.py:338
  1172.2 661.8 %reduce-scatter.14.cloned.1.call-start = ((), (), s32[]{:S(2)}) async-start(), calls=%async_computation.16 | async-start | bytes 589824 | tf_op jit(solution)/shard_map/reduce_scatter | solution.py:336
  1173.4 698.7 %reduce-scatter.12.cloned.1.call-start = ((), (), s32[]{:S(2)}) async-start(), calls=%async_computation.15 | async-start | bytes 737280 | tf_op jit(solution)/shard_map/reduce_scatter | solution.py:335
  1174.7 772.6 %reduce-scatter.20.cloned.1.call-start = ((), (), s32[]{:S(2)}) async-start(), calls=%async_computation.19 | async-start | bytes 9437184 | tf_op jit(solution)/shard_map/reduce_scatter | solution.py:343
  1182.6 840.3 %reduce-scatter.18.cloned.1.call-start = ((), (), s32[]{:S(2)}) async-start(), calls=%async_computation.18 | async-start | bytes 9437184 | tf_op jit(solution)/shard_map/reduce_scatter | solution.py:340
  1192.0 450.3 %copy-start.9 = (bf16[2,256,2048]{2,1,0:T(8,128)(2,1)S(1)}, bf16[2,256,2048]{2,1,0:T(8,128)(2,1)}, u32[]{:S(2)}) copy-start(bf16[2,256,2048]{2,1,0:T(8,128)(2,1)} %param.20) | copy-start | bytes 6291460
  1192.0 450.3 %copy-start.193 = (f32[2048]{0:T(1024)S(1)}, f32[2048]{0:T(1024)}, u32[]{:S(2)}) copy-start(f32[2048]{0:T(1024)} %copy-done.192) | copy-start | bytes 24580
  1351.4 294.4 %copy-start.208 = (f32[2048]{0:T(1024)S(1)}, f32[2048]{0:T(1024)}, u32[]{:S(2)}) copy-start(f32[2048]{0:T(1024)} %get-tuple-element.355) | copy-start | bytes 24580
  1351.4 294.4 %copy-start.209 = (f32[1024]{0:T(1024)S(1)}, f32[1024]{0:T(1024)}, u32[]{:S(2)}) copy-start(f32[1024]{0:T(1024)} %get-tuple-element.447) | copy-start | bytes 12292
  1351.4 294.5 %copy-start.219 = (f32[1024]{0:T(1024)S(1)}, f32[1024]{0:T(1024)}, u32[]{:S(2)}) copy-start(f32[1024]{0:T(1024)} %get-tuple-element.445) | copy-start | bytes 12292
  (233 other events, 3173.5 us)
Sparse Core Ops, SparseCore 0:
  9.6 22.5 all-gather.11
  62.9 36.2 all-reduce.61
  100.7 13.4 all-gather.13
  115.6 21.0 all-gather.15
  374.7 153.3 all-reduce.63
  529.6 12.6 all-gather.17
  557.6 156.1 all-reduce.65
  1092.8 32.4 reduce-scatter.21
  1129.5 218.1 all-reduce.67
  1350.8 291.5 all-reduce.69
  1645.9 114.9 reduce-scatter.9
  1764.4 31.4 reduce-scatter.15
  1799.8 34.1 reduce-scatter.13
  1837.5 34.5 reduce-scatter.11
  1876.0 71.2 reduce-scatter.19
  1951.6 71.2 reduce-scatter.17
where the time goes:
time: 2050 us; the launch traced here: 2030 us
  waiting for transfers between devices  1120 us (55%)
  local copies, waits for them, and re-layouts  417 us (20%)
  other arithmetic  257 us (13%)
  blocking collectives  110 us (5%)
  matrix products  100 us (5%)
    psum x1, waiting for transfers between devices, body(): lax.psum(jnp.dot(hidden_ffn, down_w, preferred_element_type=jnp.float32),...  291 us
    psum x1, waiting for transfers between devices, body(): normed_two_grad = lax.psum(outer_cols(both_grad, gate_flat), 'tp')  156 us
    unnamed x18, waiting for transfers between devices  154 us
    unnamed x520, local copies, waits for them, and re-layouts  139 us
    psum x1, waiting for transfers between devices, body(): lax.psum(jnp.dot(gated_out, out_w, preferred_element_type=jnp.float32), '...  138 us
    pad x14, local copies, waits for them, and re-layouts, body(): lax.associative_scan(chain_join, (block_decay, block_ends), axis=1)  103 us
    pad x14, local copies, waits for them, and re-layouts, body(): lax.associative_scan(chain_join, (block_decay, adjoint), reverse=True, ax...  92.6 us
    reduce_scatter x1, waiting for transfers between devices, body(): lax.psum_scatter(weight_grads[9], ('shard', 'ctx'), scatter_dimension=1,...  75.6 us
  transfers between devices with their start and end apart: 18, of which 14 were waited for; matrix products, arithmetic and copies ran while one was open for 19% of the time, Pallas kernels for 0%

commit v1 on v0

v1 whole, which is shorter than its diff:
```python
import functools

import jax
import jax.numpy as jnp
from jax import lax
from jax.experimental import pallas as pl
from jax.experimental.pallas import tpu as pltpu
from jax.sharding import PartitionSpec as P

MESH = pl.DeviceIdType.MESH
epsilon = 1e-05
log2e = 1.4426950408889634
bf16 = jnp.bfloat16
f32 = jnp.float32
VMEM = pl.BlockSpec(memory_space=pltpu.VMEM)
HBM = pl.BlockSpec(memory_space=pl.ANY)


def inner_rows(left, right):
    return lax.dot_general(left, right, (((0,), (0,)), ((), ())), preferred_element_type=f32)


def outer_cols(left, right):
    return lax.dot_general(left, right, (((1,), (1,)), ((), ())), preferred_element_type=f32)


def silu_grad(values):
    sig_val = jax.nn.sigmoid(values)
    return sig_val * (1.0 + values * (1.0 - sig_val))


def rms_scale(source):
    return lax.rsqrt(jnp.mean(source * source, axis=-1, keepdims=True) + epsilon)


def tp_sum(partial, epilogue, extras, extra_outs, chunk, ident, out_dtype=bf16):
    rows, width = partial.shape
    count = rows // chunk
    n_ex, n_out = len(extras), len(extra_outs)

    def kernel(*refs):
        p_ref = refs[0]
        ins = refs[1 : 1 + n_ex]
        out_ref = refs[1 + n_ex]
        outs = refs[2 + n_ex : 2 + n_ex + n_out]
        got_a, pair, got_b, a_send, a_recv, b_send, b_recv, c_send, c_recv = refs[2 + n_ex + n_out :]
        me = lax.axis_index("tp")
        mate = me + 1 - 2 * (me % 2)
        across = 3 - me
        middle = jnp.logical_or(me == 1, me == 2)
        barrier = pltpu.get_barrier_semaphore()

        def at(c):
            return pl.ds(pl.multiple_of(c * chunk, chunk), chunk)

        def copy_a(c):
            return pltpu.make_async_remote_copy(
                p_ref.at[at(c)], got_a.at[at(c)], a_send.at[c], a_recv.at[c], device_id={"tp": mate}, device_id_type=MESH
            )

        def copy_b(c):
            return pltpu.make_async_remote_copy(
                pair.at[at(c)], got_b.at[at(c)], b_send.at[c], b_recv.at[c], device_id={"tp": across}, device_id_type=MESH
            )

        def copy_c(c):
            return pltpu.make_async_remote_copy(
                out_ref.at[at(c)], out_ref.at[at(c)], c_send.at[c], c_recv.at[c], device_id={"tp": mate}, device_id_type=MESH
            )

        pl.semaphore_signal(barrier, inc=1, device_id={"tp": mate}, device_id_type=MESH)

        @pl.when(middle)
        def _():
            pl.semaphore_signal(barrier, inc=1, device_id={"tp": across}, device_id_type=MESH)
            pl.semaphore_wait(barrier, 2)

            def first(c):
                copy_a(c).wait_recv()
                pair[at(c), :] = (p_ref[at(c), :].astype(f32) + got_a[at(c), :].astype(f32)).astype(bf16)
                copy_b(c).start()

            def second(c):
                copy_b(c).wait_recv()
                total = pair[at(c), :].astype(f32) + got_b[at(c), :].astype(f32)
                epilogue(c, at(c), total, ins, out_ref, outs)
                copy_c(c).start()

            first(0)

            def turn(c, _):
                first(c)
                second(c - 1)
                return 0

            lax.fori_loop(1, count, turn, 0)
            second(count - 1)

            def drain(c, _):
                copy_b(c).wait_send()
                copy_c(c).wait_send()
                return 0

            lax.fori_loop(0, count, drain, 0)

        @pl.when(jnp.logical_not(middle))
        def _():
            pl.semaphore_wait(barrier, 1)

            def send(c, _):
                copy_a(c).start()
                return 0

            lax.fori_loop(0, count, send, 0)

            def take(c, _):
                copy_c(c).wait_recv()
                copy_a(c).wait_send()
                return 0

            lax.fori_loop(0, count, take, 0)

    return pl.pallas_call(
        kernel,
        out_shape=[jax.ShapeDtypeStruct((rows, width), out_dtype)] + list(extra_outs),
        in_specs=[VMEM] * (1 + n_ex),
        out_specs=[VMEM] * (1 + n_out),
        scratch_shapes=[pltpu.VMEM((rows, width), bf16)] * 3 + [pltpu.SemaphoreType.DMA((count,))] * 6,
        compiler_params=pltpu.CompilerParams(
            collective_id=ident, has_side_effects=True, vmem_limit_bytes=48 << 20
        ),
    )(partial, *extras)


def plain_end(c, rows, total, ins, out_ref, outs):
    out_ref[rows, :] = total.astype(out_ref.dtype)


def norm_end(c, rows, total, ins, out_ref, outs):
    source_ref, gain_ref = ins
    middle = source_ref[rows, :].astype(f32) + total
    outs[0][rows, :] = middle
    out_ref[rows, :] = (middle * rms_scale(middle) * gain_ref[...]).astype(bf16)


def add_end(c, rows, total, ins, out_ref, outs):
    out_ref[rows, :] = (ins[0][rows, :] + total).astype(bf16)


def norm_back_end(c, rows, total, ins, out_ref, outs):
    source = ins[0][rows, :].astype(f32)
    inv = rms_scale(source)
    weighted = total * ins[1][...]
    back = inv * weighted - source * (inv * inv * inv) * jnp.mean(weighted * source, axis=-1, keepdims=True)
    result = ins[2][rows, :] + back
    if outs:
        outs[0][rows, :] = result
    out_ref[rows, :] = result.astype(bf16)


def shard_gather(arrays, dims, ident):
    shards = lax.axis_size("shard")
    n = len(arrays)

    def kernel(*refs):
        ins, outs, (send, recv, own) = refs[:n], refs[n : 2 * n], refs[2 * n :]
        me = lax.axis_index("shard")
        barrier = pltpu.get_barrier_semaphore()
        for step in range(1, shards):
            pl.semaphore_signal(barrier, inc=1, device_id={"shard": lax.rem(me + step, shards)}, device_id_type=MESH)
        pl.semaphore_wait(barrier, shards - 1)
        copies = []
        for i in range(n):
            size = arrays[i].shape[dims[i]]
            spot = pl.ds(pl.multiple_of(me * size, size), size)
            place = outs[i].at[tuple(spot if k == dims[i] else slice(None) for k in range(arrays[i].ndim))]
            for step in range(1, shards):
                peer = lax.rem(me + step, shards)
                copies.append(
                    pltpu.make_async_remote_copy(
                        ins[i], place, send.at[i, step], recv.at[i, step], device_id={"shard": peer}, device_id_type=MESH
                    )
                )
                copies[-1].start()
            copies.append(pltpu.make_async_copy(ins[i], place, own.at[i]))
            copies[-1].start()
        for copy in copies:
            copy.wait()

    def full(array, dim):
        return jax.ShapeDtypeStruct(
            tuple(s * shards if k == dim else s for k, s in enumerate(array.shape)), array.dtype
        )

    return pl.pallas_call(
        kernel,
        out_shape=[full(a, d) for a, d in zip(arrays, dims)],
        in_specs=[VMEM] * n,
        out_specs=[HBM] * n,
        scratch_shapes=[
            pltpu.SemaphoreType.DMA((n, shards)),
            pltpu.SemaphoreType.DMA((n, shards)),
            pltpu.SemaphoreType.DMA((n,)),
        ],
        compiler_params=pltpu.CompilerParams(
            collective_id=ident, has_side_effects=True, vmem_limit_bytes=32 << 20
        ),
    )(*arrays)


piece = 32
unroll = 4


def spread(flat_ref, natural, first):
    for j in range(8):
        flat_ref[pl.ds(first * 8 + j, 8, stride=8), :] = natural[:, j * 128 : (j + 1) * 128]


def unspread(flat_ref, first):
    return jnp.concatenate([flat_ref[pl.ds(first * 8 + j, 8, stride=8), :] for j in range(8)], axis=1)


def tile(ref, t):
    return ref[pl.ds(pl.multiple_of(t * 8, 8), 8), :]


def row(ref, t, n, states):
    return ref[pl.ds(t * states + n, 8, stride=0), :]


def exchange(ends, got, send, recv, seq, width):
    me = lax.axis_index("ctx")
    copies = []
    for step in range(1, width):
        copies.append(
            pltpu.make_async_remote_copy(
                ends.at[seq],
                got.at[me, seq],
                send.at[seq, step],
                recv.at[seq, step],
                device_id={"ctx": lax.rem(me + step, width)},
                device_id_type=MESH,
            )
        )
        copies[-1].start()
    return copies


def ctx_barrier(width):
    me = lax.axis_index("ctx")
    barrier = pltpu.get_barrier_semaphore()
    for step in range(1, width):
        pl.semaphore_signal(barrier, inc=1, device_id={"ctx": lax.rem(me + step, width)}, device_id_type=MESH)
    pl.semaphore_wait(barrier, width - 1)


def entering(got, seq, rate_ref, states, width, reverse):
    me = lax.axis_index("ctx")
    result = []
    for n in range(states):
        value = jnp.zeros((8, 128), f32)
        for k in reversed(range(width)) if reverse else range(width):
            new = jnp.exp2(got[k, seq, states] * rate_ref[n]) * value + got[k, seq, n]
            value = jnp.where(me < k if reverse else me > k, new, value)
        result.append(value)
    return result


def scan_forward(size, act, b_row, c_row, rate, seqs, ident):
    rows, channels = size.shape
    local = rows // seqs
    states = rate.shape[0]
    width = lax.axis_size("ctx")
    pieces = local // piece

    def kernel(
        size_ref, act_ref, b_ref, c_ref, rate_ref, y_ref, kept_ref, enter_ref, size3, drive3,
        y3, ends, got, held, send, recv, out_sem,
    ):
        ctx_barrier(width)

        def lay(i, _):
            first = pl.multiple_of(i * 8, 8)
            block = size_ref[pl.ds(first, 8), :]
            spread(size3, block, first)
            spread(drive3, block * act_ref[pl.ds(first, 8), :], first)
            return 0

        lax.fori_loop(0, rows // 8, lay, 0)
        copies = []
        for seq in range(seqs):

            def first_pass(i, carried):
                values, total = list(carried[:-1]), carried[-1]
                for u in range(unroll):
                    t = seq * local + i * unroll + u
                    s, d = tile(size3, t), tile(drive3, t)
                    total = total + s
                    for n in range(states):
                        values[n] = jnp.exp2(s * rate_ref[n]) * values[n] + d * row(b_ref, t, n, states)
                return tuple(values) + (total,)

            zero = tuple(jnp.zeros((8, 128), f32) for _ in range(states + 1))
            done = lax.fori_loop(0, local // unroll, first_pass, zero)
            for n in range(states + 1):
                ends[seq, n] = done[n]
            copies.append(exchange(ends, got, send, recv, seq, width))
        me = lax.axis_index("ctx")
        for seq in range(seqs):
            for copy in copies[seq]:
                copy.wait()
            got[me, seq] = ends[seq]
            start = entering(got, seq, rate_ref, states, width, False)
            for n in range(states):
                enter_ref[seq, n] = start[n]

            def save(k, slot):
                return pltpu.make_async_copy(
                    held.at[slot], kept_ref.at[pl.ds(seq * local + k * piece, piece)], out_sem.at[slot]
                )

            def one_piece(k, carried):
                slot = lax.rem(k, 2)

                @pl.when(k >= 2)
                def _():
                    save(k - 2, slot).wait()

                def second_pass(i, values):
                    values = list(values)
                    for u in range(unroll):
                        inside = i * unroll + u
                        t = seq * local + k * piece + inside
                        s, d = tile(size3, t), tile(drive3, t)
                        acc = [None] * 4
                        for n in range(states):
                            values[n] = jnp.exp2(s * rate_ref[n]) * values[n] + d * row(b_ref, t, n, states)
                            held[slot, inside, n] = values[n]
                            part = values[n] * row(c_ref, t, n, states)
                            acc[n % 4] = part if acc[n % 4] is None else acc[n % 4] + part
                        y3[pl.ds(pl.multiple_of(t * 8, 8), 8), :] = (acc[0] + acc[1]) + (acc[2] + acc[3])
                    return tuple(values)

                carried = lax.fori_loop(0, piece // unroll, second_pass, carried)
                save(k, slot).start()
                return carried

            lax.fori_loop(0, pieces, one_piece, tuple(start))
            for k in (pieces - 2, pieces - 1):
                save(k, k % 2).wait()

        def back(i, _):
            first = pl.multiple_of(i * 8, 8)
            y_ref[pl.ds(first, 8), :] = unspread(y3, first)
            return 0

        lax.fori_loop(0, rows // 8, back, 0)

    flat = jax.ShapeDtypeStruct((rows * 8, 128), f32)
    return pl.pallas_call(
        kernel,
        out_shape=[
            jax.ShapeDtypeStruct((rows, channels), f32),
            jax.ShapeDtypeStruct((rows, states, 8, 128), f32),
            jax.ShapeDtypeStruct((seqs, states, 8, 128), f32),
            flat,
            flat,
        ],
        in_specs=[VMEM] * 5,
        out_specs=[VMEM, HBM, VMEM, VMEM, VMEM],
        scratch_shapes=[
            pltpu.VMEM((rows * 8, 128), f32),
            pltpu.VMEM((seqs, states + 1, 8, 128), f32),
            pltpu.VMEM((width, seqs, states + 1, 8, 128), f32),
            pltpu.VMEM((2, piece, states, 8, 128), f32),
            pltpu.SemaphoreType.DMA((seqs, width)),
            pltpu.SemaphoreType.DMA((seqs, width)),
            pltpu.SemaphoreType.DMA((2,)),
        ],
        compiler_params=pltpu.CompilerParams(
            collective_id=ident, has_side_effects=True, vmem_limit_bytes=48 << 20
        ),
    )(size, act, b_row, c_row, rate)


def sublane_sums(parts):
    at = lax.broadcasted_iota(jnp.int32, (8, 128), 0)
    for shift in (4, 2, 1):
        low = (at // shift) % 2 == 0
        half = len(parts) // 2
        merged = []
        for one, two in zip(parts[:half], parts[half:]):
            merged.append(
                jnp.where(low, one + pltpu.roll(one, 8 - shift, 0), two + pltpu.roll(two, shift, 0))
            )
        parts = merged
    return parts[0]


def scan_backward(size3, drive3, grad, b_row, c_row, rate, kept, enter, seqs, ident):
    rows, channels = grad.shape
    local = rows // seqs
    states = rate.shape[0]
    width = lax.axis_size("ctx")
    pieces = local // piece
    unroll_b = 2

    def kernel(
        size_ref, drive_ref, grad_ref, b_ref, c_ref, rate_ref, kept_ref, enter_ref,
        tb_ref, sd_ref, bg_ref, cg_ref, dec_ref,
        grad3, tb3, sd3, ends, got, held, bpart, cpart, prior, send, recv, in_sem,
    ):
        ctx_barrier(width)

        def lay(i, _):
            first = pl.multiple_of(i * 8, 8)
            spread(grad3, grad_ref[pl.ds(first, 8), :], first)
            return 0

        lax.fori_loop(0, rows // 8, lay, 0)

        def fetch(seq, k, slot):
            return pltpu.make_async_copy(
                kept_ref.at[pl.ds(seq * local + k * piece, piece)], held.at[slot], in_sem.at[slot]
            )

        copies = []
        for seq in range(seqs):

            def first_pass(i, carried):
                values, total = list(carried[:-1]), carried[-1]
                for u in range(unroll):
                    t = seq * local + local - 1 - (i * unroll + u)
                    s, g = tile(size_ref, t), tile(grad3, t)
                    total = total + s
                    for n in range(states):
                        values[n] = jnp.exp2(s * rate_ref[n]) * (values[n] + g * row(c_ref, t, n, states))
                return tuple(values) + (total,)

            zero = tuple(jnp.zeros((8, 128), f32) for _ in range(states + 1))
            done = lax.fori_loop(0, local // unroll, first_pass, zero)
            for n in range(states + 1):
                ends[seq, n] = done[n]
            copies.append(exchange(ends, got, send, recv, seq, width))
        me = lax.axis_index("ctx")
        for n in range(states):
            dec_ref[n] = jnp.zeros((8, 128), f32)
        for seq in range(seqs):
            fetch(seq, pieces - 1, (pieces - 1) % 2).start()
            for copy in copies[seq]:
                copy.wait()
            got[me, seq] = ends[seq]
            start = entering(got, seq, rate_ref, states, width, True)
            fetch(seq, pieces - 1, (pieces - 1) % 2).wait()

            def one_slot(slot, k, inside, adjoint, decays, prior_at):
                t = seq * local + k * piece + inside
                s, d, g = tile(size_ref, t), tile(drive_ref, t), tile(grad3, t)
                tb, sd = [None] * 2, [None] * 2
                b_parts, c_parts = [], []
                for n in range(states):
                    total = adjoint[n] + g * row(c_ref, t, n, states)
                    c_parts.append(held[slot, inside, n] * g)
                    b_parts.append(total * d)
                    through = total * row(b_ref, t, n, states)
                    adjoint[n] = jnp.exp2(s * rate_ref[n]) * total
                    kept_part = adjoint[n] * prior_at(n)
                    through_size = kept_part * rate_ref[n]
                    decays[n] = decays[n] + kept_part * s
                    tb[n % 2] = through if tb[n % 2] is None else tb[n % 2] + through
                    sd[n % 2] = through_size if sd[n % 2] is None else sd[n % 2] + through_size
                here = pl.ds(pl.multiple_of(t * 8, 8), 8)
                tb3[here, :] = tb[0] + tb[1]
                sd3[here, :] = sd[0] + sd[1]
                for h in range(states // 8):
                    spot = pl.ds(pl.multiple_of(inside * states + h * 8, 8), 8)
                    bpart[spot, :] = sublane_sums(b_parts[h * 8 : h * 8 + 8])
                    cpart[spot, :] = sublane_sums(c_parts[h * 8 : h * 8 + 8])

            def one_piece(back_k, carried):
                k = pieces - 1 - back_k
                slot = lax.rem(k, 2)

                @pl.when(k > 0)
                def _():
                    fetch(seq, k - 1, 1 - slot).start()

                def slots(i, carried):
                    adjoint, decays = list(carried[:states]), list(carried[states:])
                    for u in range(unroll_b):
                        inside = piece - 1 - (i * unroll_b + u)
                        one_slot(slot, k, inside, adjoint, decays, lambda n: held[slot, inside - 1, n])
                    return tuple(adjoint) + tuple(decays)

                carried = lax.fori_loop(0, piece // unroll_b - 1, slots, carried)
                adjoint, decays = list(carried[:states]), list(carried[states:])
                for inside in reversed(range(1, unroll_b)):
                    one_slot(slot, k, inside, adjoint, decays, lambda n: held[slot, inside - 1, n])

                @pl.when(k > 0)
                def _():
                    fetch(seq, k - 1, 1 - slot).wait()
                    prior[...] = held[1 - slot, piece - 1]

                @pl.when(k == 0)
                def _():
                    prior[...] = enter_ref[seq]

                one_slot(slot, k, 0, adjoint, decays, lambda n: prior[n])
                ones = jnp.ones((8, 128), bf16)
                for part, out in ((bpart, bg_ref), (cpart, cg_ref)):
                    sums = outer_cols(ones, part[...].astype(bf16))
                    out[pl.ds(seq * pieces + k, 1)] = sums[None]
                return tuple(adjoint) + tuple(decays)

            zero = tuple(jnp.zeros((8, 128), f32) for _ in range(states))
            carried = lax.fori_loop(0, pieces, one_piece, tuple(start) + zero)
            for n in range(states):
                dec_ref[n] = dec_ref[n] + carried[states + n]

        def back(i, _):
            first = pl.multiple_of(i * 8, 8)
            tb_ref[pl.ds(first, 8), :] = unspread(tb3, first)
            sd_ref[pl.ds(first, 8), :] = unspread(sd3, first)
            return 0

        lax.fori_loop(0, rows // 8, back, 0)

    nat = jax.ShapeDtypeStruct((rows, channels), f32)
    sums = jax.ShapeDtypeStruct((rows // piece, 8, piece * states), f32)
    return pl.pallas_call(
        kernel,
        out_shape=[nat, nat, sums, sums, jax.ShapeDtypeStruct((states, 8, 128), f32)],
        in_specs=[VMEM] * 6 + [HBM, VMEM],
        out_specs=[VMEM] * 5,
        scratch_shapes=[pltpu.VMEM((rows * 8, 128), f32)] * 3
        + [
            pltpu.VMEM((seqs, states + 1, 8, 128), f32),
            pltpu.VMEM((width, seqs, states + 1, 8, 128), f32),
            pltpu.VMEM((2, piece, states, 8, 128), f32),
            pltpu.VMEM((piece * states, 128), f32),
            pltpu.VMEM((piece * states, 128), f32),
            pltpu.VMEM((states, 8, 128), f32),
            pltpu.SemaphoreType.DMA((seqs, width)),
            pltpu.SemaphoreType.DMA((seqs, width)),
            pltpu.SemaphoreType.DMA((2,)),
        ],
        compiler_params=pltpu.CompilerParams(
            collective_id=ident, has_side_effects=True, vmem_limit_bytes=52 << 20
        ),
    )(size3, drive3, grad, b_row, c_row, rate, kept, enter)


def body(
    hidden_in, lengths, cotangent, norm_gain, in_weight, conv_weight, conv_bias, low_weight, step_weight,
    step_bias, decay_log, skip_gain, out_weight, ffn_gain, gate_up, down_weight,
):
    seqs, local, width = hidden_in.shape
    rows = seqs * local
    shards, pieces = lax.axis_size("shard"), lax.axis_size("ctx")
    inner = in_weight.shape[2]
    taps = conv_weight.shape[0]
    rank = step_weight.shape[0]
    states = decay_log.shape[0]
    low_len = low_weight.shape[0]

    small = jnp.concatenate(
        [low_weight, step_weight, decay_log, conv_weight, conv_bias[None], step_bias[None], skip_gain[None]], axis=0
    )
    small = jnp.pad(small, ((0, -small.shape[0] % 16), (0, 0)))
    gains = jnp.stack([norm_gain, ffn_gain])
    gains = jnp.pad(gains, ((0, 14), (0, 0)))
    in_half = in_weight.transpose(1, 0, 2)
    small, gains, in_w = shard_gather([small, gains, in_half], [1, 1, 1], 0)
    out_parts = lax.all_gather(out_weight, "shard")
    gate_half = gate_up.transpose(1, 0, 2)
    gate_w = [lax.all_gather(gate_half[c], "shard", axis=0, tiled=True) for c in range(2)]
    down_parts = lax.all_gather(down_weight, "shard")
    part = width // shards

    low_w = small[:low_len]
    step_w = small[low_len : low_len + rank]
    at = low_len + rank
    decay_w = small[at : at + states].astype(f32)
    kernel = small[at + states : at + states + taps].astype(f32)
    conv_b = small[at + states + taps].astype(f32)
    step_b = small[at + states + taps + 1].astype(f32)
    skip_full = small[at + states + taps + 2].astype(f32)
    gain_one, gain_two = gains[0:1].astype(f32), gains[1:2].astype(f32)

    first_slot = lax.axis_index("ctx") * local
    positions = first_slot + jnp.arange(local, dtype=jnp.int32)
    pad_mask = (positions[None, :] < lengths[:, None]).astype(f32)

    ahead = lax.ppermute(hidden_in[:, local - taps + 1 :], "ctx", [(k, k + 1) for k in range(pieces - 1)])
    longer = jnp.concatenate([ahead, hidden_in], axis=1).astype(f32)
    normed_all = (longer * rms_scale(longer) * gain_one).astype(bf16)
    source = hidden_in.reshape(rows, width).astype(f32)
    normed_one = normed_all[:, taps - 1 :].reshape(rows, width)
    normed_edge = normed_all[:, : taps - 1].reshape(seqs * (taps - 1), width)
    edge_in = jnp.dot(normed_edge, in_w[0], preferred_element_type=f32).astype(bf16)
    conv_in = jnp.dot(normed_one, in_w[0], preferred_element_type=f32).astype(bf16)
    gate_z = jnp.dot(normed_one, in_w[1], preferred_element_type=f32)
    padded = jnp.concatenate(
        [edge_in.reshape(seqs, taps - 1, inner), conv_in.reshape(seqs, local, inner)], axis=1
    ).astype(f32)
    pre_act = conv_b + sum(kernel[k] * padded[:, k : k + local] for k in range(taps))
    pre_act = pre_act.reshape(rows, inner)
    act_half = jax.nn.silu(pre_act).astype(bf16)
    act_full = act_half.astype(f32)

    low_part = outer_cols(low_w, act_half).astype(bf16)
    low_all = tp_sum(low_part, plain_end, [], [], 80, 1, f32)[0]
    step_low = low_all[:rank].astype(bf16)
    b_in, c_out = low_all[rank : rank + states], low_all[rank + states :]
    b_row, c_row = (
        jnp.broadcast_to(v.T[:, :, None], (rows, states, 128)).reshape(rows * states, 128) for v in (b_in, c_out)
    )
    step_pre = inner_rows(step_low, step_w) + step_b
    step_size = jax.nn.softplus(step_pre)
    decay_rate = -jnp.exp(decay_w)
    rate = (decay_rate * log2e).reshape(states, 8, 128)
    scan_y, kept, enter, size3, drive3 = scan_forward(step_size, act_full, b_row, c_row, rate, seqs, 2)
    scan_out = scan_y + skip_full * act_full
    gate_act = jax.nn.silu(gate_z)
    gated_out = (scan_out * gate_act).astype(bf16)
    mixed_part = jnp.concatenate(
        [jnp.dot(gated_out, out_parts[k], preferred_element_type=f32) for k in range(shards)], axis=1
    ).astype(bf16)
    wide = jax.ShapeDtypeStruct((rows, width), f32)
    hidden_rows = hidden_in.reshape(rows, width)
    normed_two, middle = tp_sum(mixed_part, norm_end, [hidden_rows, gain_two], [wide], 32, 3)
    gate_lin, up_lin = (jnp.dot(normed_two, gate_w[c], preferred_element_type=f32) for c in range(2))
    hidden_ffn = (jax.nn.silu(gate_lin) * up_lin).astype(bf16)
    ffn_part = jnp.concatenate(
        [jnp.dot(hidden_ffn, down_parts[k], preferred_element_type=f32) for k in range(shards)], axis=1
    ).astype(bf16)
    mixed_out = tp_sum(ffn_part, add_end, [middle], [], 32, 4)[0].reshape(hidden_in.shape)

    upstream = cotangent.reshape(rows, width).astype(f32) * pad_mask.reshape(rows, 1)
    ffn_grad = upstream.astype(bf16)
    down_grad = inner_rows(hidden_ffn, ffn_grad)
    hidden_grad = sum(outer_cols(ffn_grad[:, k * part : (k + 1) * part], down_parts[k]) for k in range(shards))
    gate_grad = (hidden_grad * up_lin * silu_grad(gate_lin)).astype(bf16)
    up_grad = (hidden_grad * jax.nn.silu(gate_lin)).astype(bf16)
    both_grad = jnp.concatenate([gate_grad, up_grad], axis=1)
    gate_up_grad = inner_rows(normed_two, both_grad)
    back_part = (outer_cols(gate_grad, gate_w[0]) + outer_cols(up_grad, gate_w[1])).astype(bf16)
    mix_grad, middle_grad = tp_sum(back_part, norm_back_end, [middle, gain_two, upstream], [wide], 32, 5)
    ffn_gain_grad = jnp.sum(back_part.astype(f32) * normed_two.astype(f32), axis=0) / gain_two[0]

    out_weight_grad = inner_rows(gated_out, mix_grad)
    gated_grad = sum(outer_cols(mix_grad[:, k * part : (k + 1) * part], out_parts[k]) for k in range(shards))
    scan_grad = gated_grad * gate_act
    z_grad = gated_grad * scan_out * silu_grad(gate_z)
    skip_gain_grad = jnp.sum(scan_grad * act_full, axis=0)
    through_b, through_decay, b_sums, c_sums, decay_sum = scan_backward(
        size3, drive3, scan_grad, b_row, c_row, rate, kept, enter, seqs, 6
    )
    decay_log_grad = decay_sum.reshape(states, inner) * decay_rate
    size_grad = act_full * through_b + through_decay * (1.0 / log2e)
    step_grad = (size_grad * jax.nn.sigmoid(step_pre)).astype(bf16)
    step_bias_grad = jnp.sum(step_grad.astype(f32), axis=0)
    step_weight_grad = jnp.dot(step_low, step_grad, preferred_element_type=f32)
    low_back = jnp.concatenate(
        [
            outer_cols(step_w, step_grad),
            b_sums[:, 0].reshape(rows, states).T,
            c_sums[:, 0].reshape(rows, states).T,
        ],
        axis=0,
    ).astype(bf16)
    low_grad = tp_sum(low_back, plain_end, [], [], 80, 7)[0]
    low_weight_grad = jnp.dot(low_grad, act_half, preferred_element_type=f32)
    act_grad = skip_full * scan_grad + step_size * through_b + inner_rows(low_grad, low_w)
    pre_grad = (act_grad * silu_grad(pre_act)).reshape(seqs, local, inner)
    conv_bias_grad = jnp.sum(pre_grad, axis=(0, 1))
    conv_weight_grad = jnp.stack(
        [jnp.sum(pre_grad * padded[:, k : k + local], axis=(0, 1)) for k in range(taps)]
    )
    behind = lax.ppermute(pre_grad[:, : taps - 1], "ctx", [(k + 1, k) for k in range(pieces - 1)])
    pre_long = jnp.concatenate([pre_grad, behind], axis=1)
    conv_grad = sum(kernel[k] * pre_long[:, taps - 1 - k : taps - 1 - k + local] for k in range(taps))
    conv_grad = conv_grad.reshape(rows, inner).astype(bf16)
    z_half = z_grad.astype(bf16)
    project_grad = jnp.concatenate([conv_grad, z_half], axis=1)
    in_weight_grad = inner_rows(normed_one, project_grad)
    first_part = (outer_cols(conv_grad, in_w[0]) + outer_cols(z_half, in_w[1])).astype(bf16)
    norm_gain_grad = jnp.sum(first_part.astype(f32) * source * rms_scale(source), axis=0)
    input_grad = tp_sum(first_part, norm_back_end, [hidden_rows, gain_one, middle_grad], [], 32, 8)[0]
    input_grad = input_grad.astype(f32).reshape(hidden_in.shape)

    both = ("shard", "ctx")
    scatter = functools.partial(lax.psum_scatter, axis_name=both, tiled=True)
    small_grads = jnp.concatenate(
        [low_weight_grad, step_weight_grad, decay_log_grad, conv_weight_grad, conv_bias_grad[None],
         step_bias_grad[None], skip_gain_grad[None]], axis=0,
    )
    small_out = scatter(small_grads, scatter_dimension=1)
    at = low_len + rank
    gain_out = lax.psum(scatter(jnp.stack([norm_gain_grad, ffn_gain_grad]), scatter_dimension=1), "tp")
    in_out = scatter(in_weight_grad, scatter_dimension=0)
    gate_out = scatter(gate_up_grad, scatter_dimension=0)
    return (
        mixed_out,
        input_grad,
        gain_out[0],
        in_out.reshape((-1,) + in_weight.shape[1:]),
        small_out[at + states : at + states + taps],
        small_out[at + states + taps],
        small_out[:low_len],
        small_out[low_len : low_len + rank],
        small_out[at + states + taps + 1],
        small_out[at : at + states],
        small_out[at + states + taps + 2],
        scatter(out_weight_grad, scatter_dimension=1),
        gain_out[1],
        gate_out.reshape((-1,) + gate_up.shape[1:]),
        scatter(down_grad, scatter_dimension=1),
    )


def solution(mesh):
    placed = (
        P("shard", "ctx", None),
        P("shard"),
        P("shard", "ctx", None),
        P("shard"),
        P("shard", None, "tp"),
        P(None, ("tp", "shard")),
        P(("tp", "shard")),
        P(None, ("tp", "shard")),
        P(None, ("tp", "shard")),
        P(("tp", "shard")),
        P(None, ("tp", "shard")),
        P(("tp", "shard")),
        P("tp", "shard"),
        P("shard"),
        P("shard", None, "tp"),
        P("tp", "shard"),
    )
    return jax.shard_map(
        body,
        mesh=mesh,
        in_specs=placed,
        out_specs=(
            P("shard", "ctx", None),
            P("shard", "ctx", None),
            P(("shard", "ctx")),
            P(("shard", "ctx"), None, "tp"),
            P(None, ("tp", "shard", "ctx")),
            P(("tp", "shard", "ctx")),
            P(None, ("tp", "shard", "ctx")),
            P(None, ("tp", "shard", "ctx")),
            P(("tp", "shard", "ctx")),
            P(None, ("tp", "shard", "ctx")),
            P(("tp", "shard", "ctx")),
            P("tp", ("shard", "ctx")),
            P(("shard", "ctx")),
            P(("shard", "ctx"), None, "tp"),
            P("tp", ("shard", "ctx")),
        ),
        check_vma=False,
    )
```

time: 2050 us -> 865 us (0.42)
  waiting for transfers between devices: 1120 us -> 289 us
  local copies, waits for them, and re-layouts: 417 us -> 63.1 us
  Pallas kernels: 0 us -> 347 us
  other arithmetic: 257 us -> 21.6 us
  blocking collectives: 110 us -> 9.73 us
    psum x4 -> x0, waiting for transfers between devices: 610 us -> none  [the longest x1 291 us: body(): lax.psum(jnp.dot(hidden_ffn, down_w, preferred_element_type=jnp.float32),...]
    pallas_call x0 -> x9, Pallas kernels: none -> 347 us  [the longest x6 250 us: tp_sum(): pl.pallas_call(kernel, out_shape=[jax.ShapeDtypeStruct((rows, width), out...]
    pad x28 -> x1, local copies, waits for them, and re-layouts: 196 us -> 0.03 us  [body(): small = jnp.pad(small, ((0, -small.shape[0] % 16), (0, 0)))]
    unnamed x18 -> x11, waiting for transfers between devices: 154 us -> 1.51 us
    unnamed x520 -> x116, local copies, waits for them, and re-layouts: 139 us -> 32.1 us
    reduce_sum x11 -> x2, other arithmetic: 86.4 us -> 5.92 us  [the longest x1 4.18 us: body(): step_bias_grad = jnp.sum(step_grad.astype(f32), axis=0)]
    add x36 -> x2, other arithmetic: 72.8 us -> 0.96 us  [the longest x1 0.96 us: body(): conv_b + sum((kernel[k] * padded[:, k:k + local] for k in range(taps)))]
    all_gather x13 -> x0, blocking collectives: 61.4 us -> none  [the longest x4 43.8 us: prefix(): everything = jax.tree.map(lambda part: lax.all_gather(part, axis), shard)]
  transfers between devices with their start and end apart: 18 -> 12, of which waited for: 14 -> 5; matrix products, arithmetic and copies ran while one was open for 19% -> 15% of each run, Pallas kernels for 0% -> 26%
where the time goes in v1:
time: 865 us; the launch traced here: 855 us
  Pallas kernels  347 us (40%)
  waiting for transfers between devices  289 us (33%)
  matrix products  102 us (12%)
  local copies, waits for them, and re-layouts  63.1 us (7%)
  other arithmetic  21.6 us (2%)
  between operations  15.5 us (2%)
  blocking collectives  9.73 us (1%)
    pallas_call x6, Pallas kernels, tp_sum(): pl.pallas_call(kernel, out_shape=[jax.ShapeDtypeStruct((rows, width), out...  250 us
    reduce_scatter x1, waiting for transfers between devices, body(): in_out = scatter(in_weight_grad, scatter_dimension=0)  116 us
    reduce_scatter x1, waiting for transfers between devices, body(): scatter(down_grad, scatter_dimension=1)  75.2 us
    reduce_scatter x1, waiting for transfers between devices, body(): scatter(out_weight_grad, scatter_dimension=1)  71.8 us
    pallas_call x1, Pallas kernels, scan_backward(): pl.pallas_call(kernel, out_shape=[nat, nat, sums, sums, jax.ShapeDtypeStr...  53.7 us
    dot_general x6, matrix products, inner_rows(): lax.dot_general(left, right, (((0,), (0,)), ((), ())), preferred_element_...  38 us
    pallas_call x1, Pallas kernels, scan_forward(): pl.pallas_call(kernel, out_shape=[jax.ShapeDtypeStruct((rows, channels),...  35.6 us
    unnamed x116, local copies, waits for them, and re-layouts  32.1 us
  transfers between devices with their start and end apart: 12, of which 5 were waited for; matrix products, arithmetic and copies ran while one was open for 15% of the time, Pallas kernels for 26%

profile of v1, /device:TPU:0, one launch (start us, length us, event | category | flops | bytes accessed | tf_op | source)
XLA Modules:
  0.0 855.2 jit_solution(11903699678238101187)
XLA Ops:
  21.4 6.4 copy.54
  30.1 7.8 shard_map.271
  49.5 6.6 fusion.90
  64.4 17.8 %shard_map.272 = f32[160,512]{1,0:T(8,128)S(1)} custom-call(bf16[160,512]{1,0:T(8,128)(2,1)S(1)} %convolution_convert_fusion.refs_0_), custom_call_target="tpu_custom_call" | custom-call | tf_op jit(solution)/shard_map/pallas_call | solution.py:123
  91.3 35.6 %shard_map.273 = (f32[512,1024]{1,0:T(8,128)S(1)}, f32[512,16,8,128]{3,2,1,0:T(8,128)}, f32[2,16,8,128]{3,2,1,0:T(8,128)S(1)}, f32[4096,128]{1,0:T(8,128)S(1)}, f32[4096,128]{1,0:T(8,128)}) custom-call(f32[512,1024]{1,0:T(8,128)} %get-tuple-element.83.size_ref, f32[512,1024]{1,0:T(8,128)} %get-tuple-element.57.act_ref, f32[8192,128]{1,0:T(8,128)} %broadcast_in_dim.47.b_ref, ...), custom_call_target="tpu_custom_call" | custom-call | tf_op jit(solution)/shard_map/pallas_call | solution.py:361
  129.6 5.9 multiply_convert_fusion.5
  140.4 57.7 %shard_map.274 = (bf16[512,2048]{1,0:T(8,128)(2,1)S(1)}, f32[512,2048]{1,0:T(8,128)}) custom-call(bf16[512,2048]{1,0:T(8,128)(2,1)S(1)} %pad_maximum_fusion.2.refs_0_, bf16[512,2048]{1,0:T(8,128)(2,1)} %bitcast.166, f32[1,2048]{1,0:T(1,128)S(1)} %get-tuple-element.75.refs_2_), custom_call_target="tpu_custom_call" | custom-call | tf_op jit(solution)/shard_map/pallas_call | solution.py:123
  204.5 5.9 fusion.5
  210.4 7.7 multiply_convert_fusion.3
  223.6 57.9 %shard_map.276 = (bf16[512,2048]{1,0:T(8,128)(2,1)S(1)}, f32[512,2048]{1,0:T(8,128)}) custom-call(bf16[512,2048]{1,0:T(8,128)(2,1)S(1)} %get-tuple-element.88.refs_0_, f32[512,2048]{1,0:T(8,128)} %get-tuple-element.37.refs_1_, f32[1,2048]{1,0:T(1,128)S(1)} %get-tuple-element.75.refs_2_, f32[512,2048]{1,0:T(8,128)} %get-tuple-element.65.refs_3_), custom_call_target="tpu_custom_call" | custom-call | tf_op jit(solution)/shard_map/pallas_call | solution.py:123
  288.4 53.7 %shard_map.277 = (f32[512,1024]{1,0:T(8,128)}, f32[512,1024]{1,0:T(8,128)}, f32[16,8,512]{2,1,0:T(8,128)S(1)}, f32[16,8,512]{2,1,0:T(8,128)S(1)}, f32[16,8,128]{2,1,0:T(8,128)S(1)}) custom-call(f32[4096,128]{1,0:T(8,128)} %copy-done.1, f32[4096,128]{1,0:T(8,128)} %get-tuple-element.40.drive_ref, f32[512,1024]{1,0:T(8,128)} %get-tuple-element.54.grad_ref, ...), custom_call_target="tpu_custom_call" | custom-call | tf_op jit(solution)/shard_map/pallas_call | solution.py:532
  347.5 10.5 %shard_map.278 = bf16[160,512]{1,0:T(8,128)(2,1)S(1)} custom-call(bf16[160,512]{1,0:T(8,128)(2,1)S(1)} %pad_maximum_fusion.4.refs_0_), custom_call_target="tpu_custom_call" | custom-call | tf_op jit(solution)/shard_map/pallas_call | solution.py:123
  380.4 5.8 concatenate.41
  386.3 9.8 %fusion.43 = f32[2048,2048]{1,0:T(8,128)} fusion(bf16[512,2048]{1,0:T(8,128)(2,1)S(1)} %get-tuple-element.36, bf16[512,1024]{1,0:T(8,128)(2,1)} %copy-done.47, bf16[512,1024]{1,0:T(8,128)(2,1)} %copy-done.46), kind=kOutput, calls=%fused_computation.56 | convolution fusion | flops 4299161600 | bytes 20971520 | tf_op jit(solution)/shard_map/dot_general | solution.py:20
  397.9 9.4 %fusion.39 = f32[2048,2048]{1,0:T(8,128)} fusion(bf16[512,2048]{1,0:T(8,128)(2,1)S(1)} %bitcast.174, bf16[512,1024]{1,0:T(8,128)(2,1)} %get-tuple-element.59, bf16[512,1024]{1,0:T(8,128)(2,1)S(1)} %bitcast.176), kind=kOutput, calls=%fused_computation.52 | convolution fusion | flops 4299161600 | bytes 20971520 | tf_op jit(solution)/shard_map/dot_general | solution.py:20
  409.2 5.6 fusion.124
  416.7 5.6 fusion.125
  426.9 56.8 %shard_map.275 = bf16[512,2048]{1,0:T(8,128)(2,1)S(1)} custom-call(bf16[512,2048]{1,0:T(8,128)(2,1)S(1)} %pad_maximum_fusion.3.refs_0_, f32[512,2048]{1,0:T(8,128)} %get-tuple-element.37.refs_1_), custom_call_target="tpu_custom_call" | custom-call | tf_op jit(solution)/shard_map/pallas_call | solution.py:123
  483.7 49.7 %shard_map.279 = bf16[512,2048]{1,0:T(8,128)(2,1)S(1)} custom-call(bf16[512,2048]{1,0:T(8,128)(2,1)S(1)} %copy-done.3, bf16[512,2048]{1,0:T(8,128)(2,1)} %bitcast.167, f32[1,2048]{1,0:T(1,128)S(1)} %copy-done.5, f32[512,2048]{1,0:T(8,128)} %get-tuple-element.47.refs_3_), custom_call_target="tpu_custom_call" | custom-call | tf_op jit(solution)/shard_map/pallas_call | solution.py:123
  536.9 9.7 %psum.7 = f32[2,256]{1,0:T(2,128)S(1)} all-reduce(f32[2,256]{1,0:T(2,128)S(1)} %copy.45), channel_id=1, replica_groups=mesh['shard'=2,'ctx'=4,'tp'=4] {'tp'}, use_global_device_ids=true, to_apply=%region_5.6 | all-reduce | flops 512 | bytes 4096 | tf_op jit(solution)/shard_map/psum | solution.py:702
  554.1 21.6 %reduce-scatter.15.cloned.1.call-done = f32[256,2048]{1,0:T(8,128)} async-done(((f32[2048,2048]{1,0:T(8,128)}), f32[256,2048]{1,0:T(8,128)}) %reduce-scatter.15.cloned.1.call-update) | async-done | bytes 2097168 | tf_op jit(solution)/shard_map/reduce_scatter | solution.py:704
  579.7 116.0 %reduce-scatter.9.cloned.1.call-done = f32[256,2048]{1,0:T(8,128)} async-done(((f32[2048,2048]{1,0:T(8,128)}), f32[256,2048]{1,0:T(8,128)}) %reduce-scatter.9.cloned.1.call-update) | async-done | bytes 2097168 | tf_op jit(solution)/shard_map/reduce_scatter | solution.py:703
  699.6 71.8 %reduce-scatter.13.cloned.1.call-done = f32[1024,256]{1,0:T(8,128)} async-done(((f32[1024,2048]{1,0:T(8,128)}), f32[1024,256]{1,0:T(8,128)}) %reduce-scatter.13.cloned.1.call-update) | async-done | bytes 1048592 | tf_op jit(solution)/shard_map/reduce_scatter | solution.py:717
  771.4 75.2 %reduce-scatter.17.cloned.1.call-done = f32[1024,256]{1,0:T(8,128)} async-done(((f32[1024,2048]{1,0:T(8,128)}), f32[1024,256]{1,0:T(8,128)}) %reduce-scatter.17.cloned.1.call-update) | async-done | bytes 1048592 | tf_op jit(solution)/shard_map/reduce_scatter | solution.py:720
  (227 shorter events, 129.2 us)
Async XLA Ops:
  7.2 128.3 %all-gather.9.cloned.1.call-start = ((), (), s32[]{:S(2)}) async-start(), calls=%async_computation.11 | async-start | bytes 6291456 | tf_op jit(solution)/shard_map/all_gather | solution.py:576
  7.9 190.2 %all-gather.15.cloned.1.call-start = ((), (), s32[]{:S(2)}) async-start(), calls=%async_computation.14 | async-start | bytes 6291456 | tf_op jit(solution)/shard_map/all_gather | solution.py:579
  8.7 195.9 %all-gather.13.cloned.1.call-start = ((), (), s32[]{:S(2)}) async-start(), calls=%async_computation.13 | async-start | bytes 6291456 | tf_op jit(solution)/shard_map/all_gather | solution.py:578
  14.7 195.7 %all-gather.11.cloned.1.call-start = ((), (), s32[]{:S(2)}) async-start(), calls=%async_computation.12 | async-start | bytes 6291456 | tf_op jit(solution)/shard_map/all_gather | solution.py:578
  16.3 30.7 %collective-permute-start = (bf16[2,3,2048]{2,1,0:T(4,128)(2,1)S(1)}, bf16[2,3,2048]{2,1,0:T(4,128)(2,1)S(1)}, u32[]{:S(2)}, u32[]{:S(2)}) collective-permute-start(bf16[2,3,2048]{2,1,0:T(4,128)(2,1)S(1)} %slice.172), channel_id=1, source_target_pairs={{0,4},{4,8},{8,12},{1,5},{5,9},{9,13},{2,6},{6,10},{10,14},{3,7},{... | collective-permute-start | bytes 73736 | tf_op jit(solution)/shard_map/ppermute | solution.py:596
  21.2 514.8 %reduce-scatter.19.cloned.1.call-start = ((), (), s32[]{:S(2)}) async-start(), calls=%async_computation.15 | async-start | bytes 1179648
  63.9 22.1 %copy-start.14 = (bf16[512,1024]{1,0:T(8,128)(2,1)}, bf16[512,1024]{1,0:T(8,128)(2,1)S(1)}, u32[]{:S(2)}) copy-start(bf16[512,1024]{1,0:T(8,128)(2,1)S(1)} %get-tuple-element.58) | copy-start | bytes 3145732
  88.6 41.1 %slice-start = ((s8[8388608]{0:T(1024)(128)(4,1)}), s8[4194304]{0:T(1024)(128)(4,1)S(1)}, s32[]{:S(2)}) async-start(s8[8388608]{0:T(1024)(128)(4,1)} %bitcast.158), calls=%async_computation.16 | async-start | bytes 8388608
  91.3 38.3 %slice-start.1 = ((s8[8388608]{0:T(1024)(128)(4,1)}), s8[4194304]{0:T(1024)(128)(4,1)S(1)}, s32[]{:S(2)}) async-start(s8[8388608]{0:T(1024)(128)(4,1)} %bitcast.158), calls=%async_computation.17 | async-start | bytes 8388608
  91.3 38.3 %copy-start.15 = (bf16[512,1024]{1,0:T(8,128)(2,1)S(1)}, bf16[512,1024]{1,0:T(8,128)(2,1)}, u32[]{:S(2)}) copy-start(bf16[512,1024]{1,0:T(8,128)(2,1)} %copy-done.14) | copy-start | bytes 3145732
  210.4 7.7 copy-start.41
  223.6 57.9 %copy-start.40 = (bf16[2048,1024]{1,0:T(8,128)(2,1)S(1)}, bf16[2048,1024]{1,0:T(8,128)(2,1)}, u32[]{:S(2)}) copy-start(bf16[2048,1024]{1,0:T(8,128)(2,1)} %all-gather.9.cloned.1.call-done) | copy-start | bytes 12582916
  342.7 15.2 %copy-start.13 = (f32[2,259,1024]{2,1,0:T(8,128)S(1)}, f32[2,259,1024]{2,1,0:T(8,128)}, u32[]{:S(2)}) copy-start(f32[2,259,1024]{2,1,0:T(8,128)} %copy-done.12) | copy-start | bytes 6365188
  342.7 21.0 %slice-start.2 = ((s8[8388608]{0:T(1024)(128)(4,1)}), s8[4194304]{0:T(1024)(128)(4,1)S(1)}, s32[]{:S(2)}) async-start(s8[8388608]{0:T(1024)(128)(4,1)} %bitcast.160), calls=%async_computation.18 | async-start | bytes 8388608
  346.9 11.0 %copy-start.20 = (f32[2,256,1024]{2,1,0:T(8,128)S(1)}, f32[2,256,1024]{2,1,0:T(8,128)}, u32[]{:S(2)}) copy-start(f32[2,256,1024]{2,1,0:T(8,128)} %copy-done.19) | copy-start | bytes 6291460
  362.3 9.7 %copy-start.18 = (f32[512,1024]{1,0:T(8,128)}, f32[512,1024]{1,0:T(8,128)S(1)}, u32[]{:S(2)}) copy-start(f32[512,1024]{1,0:T(8,128)S(1)} %get-tuple-element.91) | copy-start | bytes 6291460
  366.2 5.8 collective-permute-start.1
  378.5 168.7 %reduce-scatter.11.cloned.1.call-start = ((), (), s32[]{:S(2)}) async-start(), calls=%async_computation.7 | async-start | bytes 1437696 | tf_op jit(solution)/shard_map/reduce_scatter | solution.py:700
  386.2 189.5 %reduce-scatter.15.cloned.1.call-start = ((), (), s32[]{:S(2)}) async-start(), calls=%async_computation.9 | async-start | bytes 18874368 | tf_op jit(solution)/shard_map/reduce_scatter | solution.py:704
  396.1 299.6 %reduce-scatter.9.cloned.1.call-start = ((), (), s32[]{:S(2)}) async-start(), calls=%async_computation.6 | async-start | bytes 18874368 | tf_op jit(solution)/shard_map/reduce_scatter | solution.py:703
  407.4 364.0 %reduce-scatter.13.cloned.1.call-start = ((), (), s32[]{:S(2)}) async-start(), calls=%async_computation.8 | async-start | bytes 9437184 | tf_op jit(solution)/shard_map/reduce_scatter | solution.py:717
  414.9 431.7 %reduce-scatter.17.cloned.1.call-start = ((), (), s32[]{:S(2)}) async-start(), calls=%async_computation.10 | async-start | bytes 9437184 | tf_op jit(solution)/shard_map/reduce_scatter | solution.py:720
  426.9 56.8 %copy-start.3 = (bf16[512,2048]{1,0:T(8,128)(2,1)S(1)}, bf16[512,2048]{1,0:T(8,128)(2,1)}, u32[]{:S(2)}) copy-start(bf16[512,2048]{1,0:T(8,128)(2,1)} %get-tuple-element.90.refs_0_) | copy-start | bytes 6291460
  426.9 56.8 %copy-start.5 = (f32[1,2048]{1,0:T(1,128)S(1)}, f32[1,2048]{1,0:T(1,128)}, u32[]{:S(2)}) copy-start(f32[1,2048]{1,0:T(1,128)} %copy-done.4) | copy-start | bytes 24580
  (42 other events, 154.7 us)
Sparse Core Ops, SparseCore 0:
  9.6 16.3 all-gather.8
  27.5 14.8 all-gather.14
  43.9 14.8 all-gather.12
  60.2 14.8 all-gather.10
  378.7 36.3 reduce-scatter.18
  418.8 36.8 reduce-scatter.10
  459.7 115.9 reduce-scatter.14
  579.7 115.9 reduce-scatter.8
  700.1 71.2 reduce-scatter.12
  775.3 71.2 reduce-scatter.16

commit v2 on v1

--- a/solution.py
+++ b/solution.py
@@ -33,103 +33,300 @@
     return lax.rsqrt(jnp.mean(source * source, axis=-1, keepdims=True) + epsilon)
 
 
-def tp_sum(partial, epilogue, extras, extra_outs, chunk, ident, out_dtype=bf16):
+class Line:
+    lag = 3
+    ahead = 4
+
+    def __init__(self, shape, chunk, epilogue, extras, out_dtype):
+        self.shape, self.chunk, self.epilogue, self.out_dtype = shape, chunk, epilogue, out_dtype
+        self.count = shape[0] // chunk
+        self.extras = [(e.shape, e.dtype) for e in extras]
+
+    def scratch(self):
+        return (
+            [pltpu.VMEM(self.shape, bf16)] * 4
+            + [pltpu.SemaphoreType.DMA((self.count,))] * 6
+            + [pltpu.VMEM(shape, dtype) for shape, dtype in self.extras]
+            + [pltpu.SemaphoreType.DMA((1 + len(self.extras),))]
+        )
+
+    def bind(self, p_ref, ins, out_ref, outs, scratch):
+        self.p_ref, self.given, self.out_ref, self.outs = p_ref, ins, out_ref, outs
+        (self.p, self.got_a, self.pair, self.got_b, self.a_send, self.a_recv, self.b_send, self.b_recv,
+         self.c_send, self.c_recv) = scratch[:10]
+        self.ins, self.in_sem = scratch[10:-1], scratch[-1]
+        me = lax.axis_index("tp")
+        self.mate = me + 1 - 2 * (me % 2)
+        self.across = 3 - me
+        self.middle = jnp.logical_or(me == 1, me == 2)
+
+    def at(self, c):
+        return pl.ds(pl.multiple_of(c * self.chunk, self.chunk), self.chunk)
+
+    def remote(self, source, target, send, recv, c, to):
+        return pltpu.make_async_remote_copy(
+            source.at[self.at(c)], target.at[self.at(c)], send.at[c], recv.at[c], device_id={"tp": to}, device_id_type=MESH
+        )
+
+    def copy_a(self, c):
+        return self.remote(self.p_ref, self.got_a, self.a_send, self.a_recv, c, self.mate)
+
+    def copy_b(self, c):
+        return self.remote(self.pair, self.got_b, self.b_send, self.b_recv, c, self.across)
+
+    def copy_c(self, c):
+        return self.remote(self.out_ref, self.out_ref, self.c_send, self.c_recv, c, self.mate)
+
+    def loads(self):
+        pairs = [(self.p_ref, self.p)] + list(zip(self.given, self.ins))
+        return [pltpu.make_async_copy(a, b, self.in_sem.at[i]) for i, (a, b) in enumerate(pairs)]
+
+    def begin(self, barrier, met, ends_meet=False):
+        pl.semaphore_signal(barrier, inc=1, device_id={"tp": self.mate}, device_id_type=MESH)
+
+        @pl.when(self.middle)
+        def _():
+            pl.semaphore_signal(barrier, inc=1, device_id={"tp": self.across}, device_id_type=MESH)
+            for load in self.loads():
+                load.start()
+            pl.semaphore_wait(barrier, met + 2)
+            for load in self.loads():
+                load.wait()
+
+        @pl.when(jnp.logical_not(self.middle))
+        def _():
+            if ends_meet:
+                pl.semaphore_signal(barrier, inc=1, device_id={"tp": self.across}, device_id_type=MESH)
+            pl.semaphore_wait(barrier, met + 2 if ends_meet else met + 1)
+
+            for c in range(min(self.ahead, self.count)):
+                self.copy_a(c).start()
+
+    def first(self, c):
+        at = self.at(c)
+        self.copy_a(c).wait_recv()
+        self.pair[at, :] = (self.p[at, :].astype(f32) + self.got_a[at, :].astype(f32)).astype(bf16)
+        self.copy_b(c).start()
+
+    def second(self, c):
+        at = self.at(c)
+        self.copy_b(c).wait_recv()
+        total = self.pair[at, :].astype(f32) + self.got_b[at, :].astype(f32)
+        self.epilogue(c, at, total, self.ins, self.out_ref, self.outs)
+        self.copy_c(c).start()
+
+    def tick(self, c):
+        lag = min(self.lag, self.count)
+
+        @pl.when(jnp.logical_and(self.middle, c < self.count))
+        def _():
+            self.first(c)
+
+        @pl.when(jnp.logical_and(self.middle, jnp.logical_and(c >= lag, c < self.count + lag)))
+        def _():
+            self.second(c - lag)
+
+        @pl.when(jnp.logical_and(jnp.logical_not(self.middle), c + self.ahead < self.count))
+        def _():
+            self.copy_a(c + self.ahead).start()
+
+    def ticks(self):
+        return self.count + min(self.lag, self.count)
+
+    def finish(self):
+        @pl.when(self.middle)
+        def _():
+            def drain(c, _):
+                self.copy_b(c).wait_send()
+                self.copy_c(c).wait_send()
+                return 0
+
+            lax.fori_loop(0, self.count, drain, 0)
+
+        @pl.when(jnp.logical_not(self.middle))
+        def _():
+            def take(c, _):
+                self.copy_c(c).wait_recv()
+                self.copy_a(c).wait_send()
+                return 0
+
+            lax.fori_loop(0, self.count, take, 0)
+
+
+share_lag = 2
+share_ahead = 2
+
+
+def halving(count, axis):
+    return [(axis, 1 << k) for k in reversed(range(count.bit_length() - 1))]
+
+
+def tp_sum(partial, epilogue, extras, extra_outs, chunk, ident, out_dtype=bf16, scatters=(), line_too=False):
     rows, width = partial.shape
-    count = rows // chunk
-    n_ex, n_out = len(extras), len(extra_outs)
+    line = Line(partial.shape, chunk, epilogue, extras, out_dtype)
+    n_line = len(line.scratch())
+    n_ex, n_out, n_sc = len(extras), len(extra_outs), len(scatters)
+    shards, pieces = lax.axis_size("shard"), lax.axis_size("ctx")
+    bits = halving(shards, "shard") + halving(pieces, "ctx")
+    depth = len(bits)
+    head = shards.bit_length() - 1
+    dims = list(range(depth))
+    orders = (dims, dims[:head] + dims[head:][::-1])
+    step_rows = 16
+    blocks = [g.shape[0] // (shards * pieces) for g in scatters]
+    parts = [r // step_rows for r in blocks]
+    folded = [g.reshape((2,) * depth + (r, g.shape[1])) for g, r in zip(scatters, blocks)]
 
     def kernel(*refs):
-        p_ref = refs[0]
-        ins = refs[1 : 1 + n_ex]
-        out_ref = refs[1 + n_ex]
-        outs = refs[2 + n_ex : 2 + n_ex + n_out]
-        got_a, pair, got_b, a_send, a_recv, b_send, b_recv, c_send, c_recv = refs[2 + n_ex + n_out :]
-        me = lax.axis_index("tp")
-        mate = me + 1 - 2 * (me % 2)
-        across = 3 - me
-        middle = jnp.logical_or(me == 1, me == 2)
+        refs = list(refs)
+
+        def take_refs(n):
+            taken = refs[:n]
+            del refs[:n]
+            return taken
+
+        (p_ref,) = take_refs(1)
+        ins = take_refs(n_ex)
+        full = take_refs(n_sc)
+        (out_ref,) = take_refs(1)
+        outs = take_refs(n_out)
+        shares = take_refs(n_sc)
+        line.bind(p_ref, ins, out_ref, outs, take_refs(n_line))
+        own = take_refs(n_sc)
+        landed = [take_refs(n_sc) for _ in range(depth if n_sc else 0)]
+        r_send, r_recv, own_sem = take_refs(3) if n_sc else (None, None, None)
+        tail, tail_send, tail_recv = take_refs(3) if line_too else (None, None, None)
         barrier = pltpu.get_barrier_semaphore()
-
-        def at(c):
-            return pl.ds(pl.multiple_of(c * chunk, chunk), chunk)
-
-        def copy_a(c):
+        mine, partner = [], []
+        for axis, bit in bits if n_sc else []:
+            here = lax.axis_index(axis)
+            mine.append((here // bit) % 2)
+            partner.append({axis: here + bit - 2 * bit * ((here // bit) % 2)})
+
+        def spot(c):
+            return pl.ds(pl.multiple_of(c * step_rows, step_rows), step_rows)
+
+        def pick(remaining, dim, index, c):
+            return tuple(index if d == dim else slice(None) for d in remaining) + (spot(c), slice(None))
+
+        def rest(order, j):
+            return [d for d in dims if d not in order[:j]]
+
+        def share_copy(j, a, c, order):
+            source = full[a] if j == 0 else landed[j - 1][a]
+            d = order[j]
             return pltpu.make_async_remote_copy(
-                p_ref.at[at(c)], got_a.at[at(c)], a_send.at[c], a_recv.at[c], device_id={"tp": mate}, device_id_type=MESH
+                source.at[pick(rest(order, j), d, 1 - mine[d], c)],
+                landed[j][a].at[pick(rest(order, j + 1), None, None, c)],
+                r_send.at[j, a, c],
+                r_recv.at[j, a, c],
+                device_id=partner[d],
+                device_id_type=MESH,
             )
 
-        def copy_b(c):
-            return pltpu.make_async_remote_copy(
-                pair.at[at(c)], got_b.at[at(c)], b_send.at[c], b_recv.at[c], device_id={"tp": across}, device_id_type=MESH
+        def own_copy(a, c, order):
+            return pltpu.make_async_copy(
+                full[a].at[pick(dims, order[0], mine[order[0]], c)],
+                own[a].at[pick(rest(order, 1), None, None, c)],
+                own_sem.at[a, c],
             )
 
-        def copy_c(c):
-            return pltpu.make_async_remote_copy(
-                out_ref.at[at(c)], out_ref.at[at(c)], c_send.at[c], c_recv.at[c], device_id={"tp": mate}, device_id_type=MESH
-            )
-
-        pl.semaphore_signal(barrier, inc=1, device_id={"tp": mate}, device_id_type=MESH)
-
-        @pl.when(middle)
-        def _():
-            pl.semaphore_signal(barrier, inc=1, device_id={"tp": across}, device_id_type=MESH)
-            pl.semaphore_wait(barrier, 2)
-
-            def first(c):
-                copy_a(c).wait_recv()
-                pair[at(c), :] = (p_ref[at(c), :].astype(f32) + got_a[at(c), :].astype(f32)).astype(bf16)
-                copy_b(c).start()
-
-            def second(c):
-                copy_b(c).wait_recv()
-                total = pair[at(c), :].astype(f32) + got_b[at(c), :].astype(f32)
-                epilogue(c, at(c), total, ins, out_ref, outs)
-                copy_c(c).start()
-
-            first(0)
-
-            def turn(c, _):
-                first(c)
-                second(c - 1)
+        def share_step(j, a, c, order):
+            share_copy(j, a, c, order).wait_recv()
+            where = pick(rest(order, j + 1), None, None, c)
+            d = order[j]
+            if j == 0:
+                own_copy(a, c, order).wait()
+                kept = own[a][where]
+            else:
+                kept = landed[j - 1][a][pick(rest(order, j), d, mine[d], c)]
+            total = kept.astype(f32) + landed[j][a][where].astype(f32)
+            if j == depth - 1:
+                shares[a][spot(c), :] = total
+            else:
+                landed[j][a][where] = total.astype(bf16)
+                share_copy(j + 1, a, c, order).start()
+
+        def each_part(i, fn):
+            for parity in (0, 1):
+                c = 2 * i + parity
+                for a in range(n_sc):
+
+                    @pl.when(jnp.logical_and(c >= 0, c < parts[a]))
+                    def _():
+                        fn(a, c, orders[parity])
+
+        for who in partner:
+            pl.semaphore_signal(barrier, inc=1, device_id=who, device_id_type=MESH)
+        line.begin(barrier, len(partner), line_too)
+
+        def begin(a, c, order):
+            share_copy(0, a, c, order).start()
+            own_copy(a, c, order).start()
+
+        pairs = (max(parts, default=0) + 1) // 2
+        if n_sc:
+
+            for i in range(share_ahead):
+                each_part(i, begin)
+
+        def turn(i, _):
+            for parity in (0, 1):
+                line.tick(2 * i + parity)
+            each_part(i + share_ahead, begin)
+            for j in range(depth if n_sc else 0):
+                each_part(i - share_lag * j, functools.partial(share_step, j))
+            return 0
+
+        turns = (line.ticks() + 1) // 2
+        if n_sc:
+            turns = max(turns, pairs + share_lag * (depth - 1))
+        lax.fori_loop(0, turns, turn, 0)
+        if line_too:
+            top = shares[-1].at[pl.ds(0, 8)]
+            for k, to in enumerate((line.mate, line.across)):
+                copy = pltpu.make_async_remote_copy(
+                    top if k == 0 else tail.at[2], tail.at[k], tail_send.at[k], tail_recv.at[k],
+                    device_id={"tp": to}, device_id_type=MESH,
+                )
+                copy.start()
+                copy.wait()
+                if k == 0:
+                    tail[2] = top[...] + tail[0]
+            shares[-1][pl.ds(0, 8), :] = tail[2] + tail[1]
+        line.finish()
+
+        if n_sc:
+
+            def sent(i, _):
+                for j in range(depth):
+                    each_part(i, lambda a, c, order: share_copy(j, a, c, order).wait_send())
                 return 0
 
-            lax.fori_loop(1, count, turn, 0)
-            second(count - 1)
-
-            def drain(c, _):
-                copy_b(c).wait_send()
-                copy_c(c).wait_send()
-                return 0
-
-            lax.fori_loop(0, count, drain, 0)
-
-        @pl.when(jnp.logical_not(middle))
-        def _():
-            pl.semaphore_wait(barrier, 1)
-
-            def send(c, _):
-                copy_a(c).start()
-                return 0
-
-            lax.fori_loop(0, count, send, 0)
-
-            def take(c, _):
-                copy_c(c).wait_recv()
-                copy_a(c).wait_send()
-                return 0
-
-            lax.fori_loop(0, count, take, 0)
-
+            lax.fori_loop(0, pairs, sent, 0)
+
+    buffers = []
+    if n_sc:
+        buffers += [pltpu.VMEM((2,) * (depth - 1) + g.shape[depth:], bf16) for g in folded]
+        for j in range(depth):
+            buffers += [pltpu.VMEM((2,) * (depth - 1 - j) + g.shape[depth:], bf16) for g in folded]
+        sem = pltpu.SemaphoreType.DMA((depth, n_sc, max(parts)))
+        buffers += [sem, sem, pltpu.SemaphoreType.DMA((n_sc, max(parts)))]
+    if line_too:
+        pair_sem = pltpu.SemaphoreType.DMA((2,))
+        buffers += [pltpu.VMEM((3, 8, folded[-1].shape[-1]), f32), pair_sem, pair_sem]
     return pl.pallas_call(
         kernel,
-        out_shape=[jax.ShapeDtypeStruct((rows, width), out_dtype)] + list(extra_outs),
-        in_specs=[VMEM] * (1 + n_ex),
-        out_specs=[VMEM] * (1 + n_out),
-        scratch_shapes=[pltpu.VMEM((rows, width), bf16)] * 3 + [pltpu.SemaphoreType.DMA((count,))] * 6,
+        out_shape=[jax.ShapeDtypeStruct((rows, width), out_dtype)]
+        + list(extra_outs)
+        + [jax.ShapeDtypeStruct(g.shape[depth:], f32) for g in folded],
+        in_specs=[HBM] * (1 + n_ex + n_sc),
+        out_specs=[VMEM] * (1 + n_out + n_sc),
+        scratch_shapes=line.scratch() + buffers,
         compiler_params=pltpu.CompilerParams(
-            collective_id=ident, has_side_effects=True, vmem_limit_bytes=48 << 20
+            collective_id=ident, has_side_effects=True, vmem_limit_bytes=56 << 20
         ),
-    )(partial, *extras)
+    )(partial, *extras, *folded)
 
 
 def plain_end(c, rows, total, ins, out_ref, outs):
@@ -247,12 +444,12 @@
     return copies
 
 
-def ctx_barrier(width):
+def ctx_greet(width):
     me = lax.axis_index("ctx")
     barrier = pltpu.get_barrier_semaphore()
     for step in range(1, width):
         pl.semaphore_signal(barrier, inc=1, device_id={"ctx": lax.rem(me + step, width)}, device_id_type=MESH)
-    pl.semaphore_wait(barrier, width - 1)
+    return barrier
 
 
 def entering(got, seq, rate_ref, states, width, reverse):
@@ -278,7 +475,7 @@
         size_ref, act_ref, b_ref, c_ref, rate_ref, y_ref, kept_ref, enter_ref, size3, drive3,
         y3, ends, got, held, send, recv, out_sem,
     ):
-        ctx_barrier(width)
+        pl.semaphore_wait(ctx_greet(width), width - 1)
 
         def lay(i, _):
             first = pl.multiple_of(i * 8, 8)
@@ -398,20 +595,23 @@
     return parts[0]
 
 
-def scan_backward(size3, drive3, grad, b_row, c_row, rate, kept, enter, seqs, ident):
+def scan_backward(size3, drive3, grad, b_row, c_row, rate, kept, enter, seqs, ident, partial, epilogue, extras, chunk):
     rows, channels = grad.shape
     local = rows // seqs
     states = rate.shape[0]
     width = lax.axis_size("ctx")
     pieces = local // piece
+    early = 2
     unroll_b = 2
-
-    def kernel(
-        size_ref, drive_ref, grad_ref, b_ref, c_ref, rate_ref, kept_ref, enter_ref,
-        tb_ref, sd_ref, bg_ref, cg_ref, dec_ref,
-        grad3, tb3, sd3, ends, got, held, bpart, cpart, prior, send, recv, in_sem,
-    ):
-        ctx_barrier(width)
+    line = Line(partial.shape, chunk, epilogue, extras, bf16)
+    n_line, n_ex = len(line.scratch()), len(extras)
+
+    def kernel(*refs):
+        size_ref, drive_ref, grad_ref, b_ref, c_ref, rate_ref, kept_ref, enter_ref, p_ref = refs[:9]
+        tb_ref, sd_ref, bg_ref, cg_ref, dec_ref, sum_ref = refs[9 + n_ex : 15 + n_ex]
+        grad3, tb3, sd3, ends, got, held, bpart, cpart, prior, send, recv, in_sem = refs[15 + n_ex : 27 + n_ex]
+        line.bind(p_ref, refs[9 : 9 + n_ex], sum_ref, [], refs[27 + n_ex :])
+        line.begin(ctx_greet(width), width - 1)
 
         def lay(i, _):
             first = pl.multiple_of(i * 8, 8)
@@ -439,7 +639,11 @@
                 return tuple(values) + (total,)
 
             zero = tuple(jnp.zeros((8, 128), f32) for _ in range(states + 1))
-            done = lax.fori_loop(0, local // unroll, first_pass, zero)
+            done = zero
+            for half in range(early):
+                span = local // unroll // early
+                done = lax.fori_loop(half * span, (half + 1) * span, first_pass, done)
+                line.tick(seq * early + half)
             for n in range(states + 1):
                 ends[seq, n] = done[n]
             copies.append(exchange(ends, got, send, recv, seq, width))
@@ -512,6 +716,7 @@
                 for part, out in ((bpart, bg_ref), (cpart, cg_ref)):
                     sums = outer_cols(ones, part[...].astype(bf16))
                     out[pl.ds(seq * pieces + k, 1)] = sums[None]
+                line.tick(seqs * early + seq * pieces + back_k)
                 return tuple(adjoint) + tuple(decays)
 
             zero = tuple(jnp.zeros((8, 128), f32) for _ in range(states))
@@ -526,14 +731,18 @@
             return 0
 
         lax.fori_loop(0, rows // 8, back, 0)
+        for c in range(seqs * (early + pieces), line.ticks()):
+            line.tick(c)
+        line.finish()
 
     nat = jax.ShapeDtypeStruct((rows, channels), f32)
     sums = jax.ShapeDtypeStruct((rows // piece, 8, piece * states), f32)
     return pl.pallas_call(
         kernel,
-        out_shape=[nat, nat, sums, sums, jax.ShapeDtypeStruct((states, 8, 128), f32)],
-        in_specs=[VMEM] * 6 + [HBM, VMEM],
-        out_specs=[VMEM] * 5,
+        out_shape=[nat, nat, sums, sums, jax.ShapeDtypeStruct((states, 8, 128), f32),
+                   jax.ShapeDtypeStruct(partial.shape, bf16)],
+        in_specs=[VMEM] * 6 + [HBM, VMEM] + [HBM] * (1 + n_ex),
+        out_specs=[VMEM] * 6,
         scratch_shapes=[pltpu.VMEM((rows * 8, 128), f32)] * 3
         + [
             pltpu.VMEM((seqs, states + 1, 8, 128), f32),
@@ -545,11 +754,12 @@
             pltpu.SemaphoreType.DMA((seqs, width)),
             pltpu.SemaphoreType.DMA((seqs, width)),
             pltpu.SemaphoreType.DMA((2,)),
-        ],
+        ]
+        + line.scratch(),
         compiler_params=pltpu.CompilerParams(
-            collective_id=ident, has_side_effects=True, vmem_limit_bytes=52 << 20
+            collective_id=ident, has_side_effects=True, vmem_limit_bytes=58 << 20
         ),
-    )(size3, drive3, grad, b_row, c_row, rate, kept, enter)
+    )(size3, drive3, grad, b_row, c_row, rate, kept, enter, partial, *extras)
 
 
 def body(
@@ -636,28 +846,29 @@
     ffn_part = jnp.concatenate(
         [jnp.dot(hidden_ffn, down_parts[k], preferred_element_type=f32) for k in range(shards)], axis=1
     ).astype(bf16)
-    mixed_out = tp_sum(ffn_part, add_end, [middle], [], 32, 4)[0].reshape(hidden_in.shape)
 
     upstream = cotangent.reshape(rows, width).astype(f32) * pad_mask.reshape(rows, 1)
     ffn_grad = upstream.astype(bf16)
-    down_grad = inner_rows(hidden_ffn, ffn_grad)
+    down_grad = inner_rows(ffn_grad, hidden_ffn).astype(bf16)
     hidden_grad = sum(outer_cols(ffn_grad[:, k * part : (k + 1) * part], down_parts[k]) for k in range(shards))
     gate_grad = (hidden_grad * up_lin * silu_grad(gate_lin)).astype(bf16)
     up_grad = (hidden_grad * jax.nn.silu(gate_lin)).astype(bf16)
-    both_grad = jnp.concatenate([gate_grad, up_grad], axis=1)
-    gate_up_grad = inner_rows(normed_two, both_grad)
+    gate_up_grad = [inner_rows(normed_two, g).astype(bf16) for g in (gate_grad, up_grad)]
     back_part = (outer_cols(gate_grad, gate_w[0]) + outer_cols(up_grad, gate_w[1])).astype(bf16)
-    mix_grad, middle_grad = tp_sum(back_part, norm_back_end, [middle, gain_two, upstream], [wide], 32, 5)
+    mix_grad, middle_grad, *ffn_shares = tp_sum(
+        back_part, norm_back_end, [middle, gain_two, ffn_grad], [wide], 32, 5, scatters=gate_up_grad + [down_grad]
+    )
     ffn_gain_grad = jnp.sum(back_part.astype(f32) * normed_two.astype(f32), axis=0) / gain_two[0]
 
-    out_weight_grad = inner_rows(gated_out, mix_grad)
+    out_weight_grad = inner_rows(mix_grad, gated_out).astype(bf16)
     gated_grad = sum(outer_cols(mix_grad[:, k * part : (k + 1) * part], out_parts[k]) for k in range(shards))
     scan_grad = gated_grad * gate_act
     z_grad = gated_grad * scan_out * silu_grad(gate_z)
     skip_gain_grad = jnp.sum(scan_grad * act_full, axis=0)
-    through_b, through_decay, b_sums, c_sums, decay_sum = scan_backward(
-        size3, drive3, scan_grad, b_row, c_row, rate, kept, enter, seqs, 6
+    through_b, through_decay, b_sums, c_sums, decay_sum, mixed_out = scan_backward(
+        size3, drive3, scan_grad, b_row, c_row, rate, kept, enter, seqs, 6, ffn_part, add_end, [middle], 32
     )
+    mixed_out = mixed_out.reshape(hidden_in.shape)
     decay_log_grad = decay_sum.reshape(states, inner) * decay_rate
     size_grad = act_full * through_b + through_decay * (1.0 / log2e)
     step_grad = (size_grad * jax.nn.sigmoid(step_pre)).astype(bf16)
@@ -684,29 +895,35 @@
     conv_grad = sum(kernel[k] * pre_long[:, taps - 1 - k : taps - 1 - k + local] for k in range(taps))
     conv_grad = conv_grad.reshape(rows, inner).astype(bf16)
     z_half = z_grad.astype(bf16)
-    project_grad = jnp.concatenate([conv_grad, z_half], axis=1)
-    in_weight_grad = inner_rows(normed_one, project_grad)
+    in_weight_grad = [inner_rows(normed_one, g).astype(bf16) for g in (conv_grad, z_half)]
     first_part = (outer_cols(conv_grad, in_w[0]) + outer_cols(z_half, in_w[1])).astype(bf16)
     norm_gain_grad = jnp.sum(first_part.astype(f32) * source * rms_scale(source), axis=0)
-    input_grad = tp_sum(first_part, norm_back_end, [hidden_rows, gain_one, middle_grad], [], 32, 8)[0]
-    input_grad = input_grad.astype(f32).reshape(hidden_in.shape)
-
-    both = ("shard", "ctx")
-    scatter = functools.partial(lax.psum_scatter, axis_name=both, tiled=True)
     small_grads = jnp.concatenate(
         [low_weight_grad, step_weight_grad, decay_log_grad, conv_weight_grad, conv_bias_grad[None],
          step_bias_grad[None], skip_gain_grad[None]], axis=0,
     )
-    small_out = scatter(small_grads, scatter_dimension=1)
+    places = shards * pieces
+    lines, lane = small_grads.shape[0], inner // places
+    small_blocks = small_grads.reshape(lines, places, lane).transpose(1, 0, 2).reshape(places, lines * lane)
+    small_rows = -(-lines * lane // (16 * inner)) * 16
+    small_blocks = jnp.pad(small_blocks, ((0, 0), (0, small_rows * inner - lines * lane)))
+    small_blocks = small_blocks.reshape(places * small_rows, inner).astype(bf16)
+    share = width // places
+    gain_blocks = jnp.concatenate([norm_gain_grad.reshape(places, share), ffn_gain_grad.reshape(places, share)], axis=1)
+    gain_blocks = jnp.pad(gain_blocks[:, None], ((0, 0), (0, 15), (0, inner - 2 * share))).astype(bf16)
+    input_grad, in_share, z_share, out_share, small_share, gain_share = tp_sum(
+        first_part, norm_back_end, [hidden_rows, gain_one, middle_grad], [], 32, 8,
+        scatters=in_weight_grad + [out_weight_grad, small_blocks, gain_blocks.reshape(places * 16, inner)],
+        line_too=True,
+    )
+    input_grad = input_grad.astype(f32).reshape(hidden_in.shape)
+    small_out = small_share.reshape(-1)[: lines * lane].reshape(lines, lane)
     at = low_len + rank
-    gain_out = lax.psum(scatter(jnp.stack([norm_gain_grad, ffn_gain_grad]), scatter_dimension=1), "tp")
-    in_out = scatter(in_weight_grad, scatter_dimension=0)
-    gate_out = scatter(gate_up_grad, scatter_dimension=0)
     return (
         mixed_out,
         input_grad,
-        gain_out[0],
-        in_out.reshape((-1,) + in_weight.shape[1:]),
+        gain_share[0, :share],
+        jnp.stack([in_share, z_share], axis=1),
         small_out[at + states : at + states + taps],
         small_out[at + states + taps],
         small_out[:low_len],
@@ -714,10 +931,10 @@
         small_out[at + states + taps + 1],
         small_out[at : at + states],
         small_out[at + states + taps + 2],
-        scatter(out_weight_grad, scatter_dimension=1),
-        gain_out[1],
-        gate_out.reshape((-1,) + gate_up.shape[1:]),
-        scatter(down_grad, scatter_dimension=1),
+        out_share.T,
+        gain_share[0, share : 2 * share],
+        jnp.stack(ffn_shares[:2], axis=1),
+        ffn_shares[2].T,
     )
 
 

time: 865 us -> 585 us (0.68)
  waiting for transfers between devices: 289 us -> 1.44 us
  local copies, waits for them, and re-layouts: 63.1 us -> 73.6 us
  Pallas kernels: 347 us -> 357 us
  blocking collectives: 9.73 us -> 0 us
    reduce_scatter x5 -> x0, waiting for transfers between devices: 284 us -> none  [the longest x1 116 us: body(): in_out = scatter(in_weight_grad, scatter_dimension=0)]
    pallas_call x1, Pallas kernels: 53.7 us -> 73 us  [scan_backward(): pl.pallas_call(kernel, out_shape=[nat, nat, sums, sums, jax.ShapeDtypeStr...]
    unnamed x116 -> x152, local copies, waits for them, and re-layouts: 32.1 us -> 43.2 us
    pallas_call x6 -> x5, Pallas kernels: 250 us -> 240 us  [tp_sum(): pl.pallas_call(kernel, out_shape=[jax.ShapeDtypeStruct((rows, width), out...]
    psum x1 -> x0, blocking collectives: 9.73 us -> none  [body(): lax.psum(scatter(jnp.stack([norm_gain_grad, ffn_gain_grad]), scatter_dime...]
    dot_general x6 -> x8, matrix products: 38 us -> 36 us  [inner_rows(): lax.dot_general(left, right, (((0,), (0,)), ((), ())), preferred_element_...]
  transfers between devices with their start and end apart: 12 -> 6, of which waited for: 5 -> 0; matrix products, arithmetic and copies ran while one was open for 15% -> 16% of each run, Pallas kernels for 26% -> 21%
where the time goes in v2:
time: 585 us; the launch traced here: 581 us
  Pallas kernels  357 us (61%)
  matrix products  102 us (17%)
  local copies, waits for them, and re-layouts  73.6 us (13%)
  other arithmetic  25.2 us (4%)
  between operations  15 us (3%)
  starting transfers between devices  6.63 us (1%)
    pallas_call x5, Pallas kernels, tp_sum(): pl.pallas_call(kernel, out_shape=[jax.ShapeDtypeStruct((rows, width), out...  240 us
    pallas_call x1, Pallas kernels, scan_backward(): pl.pallas_call(kernel, out_shape=[nat, nat, sums, sums, jax.ShapeDtypeStr...  73 us
    unnamed x152, local copies, waits for them, and re-layouts  43.2 us
    dot_general x8, matrix products, inner_rows(): lax.dot_general(left, right, (((0,), (0,)), ((), ())), preferred_element_...  36 us
    pallas_call x1, Pallas kernels, scan_forward(): pl.pallas_call(kernel, out_shape=[jax.ShapeDtypeStruct((rows, channels),...  35.5 us
    dot_general x10, matrix products, outer_cols(): lax.dot_general(left, right, (((1,), (1,)), ((), ())), preferred_element_...  29.4 us
    dot_general x2, matrix products, body(): jnp.dot(normed_two, gate_w[c], preferred_element_type=f32)  13.7 us
  transfers between devices with their start and end apart: 6, of which 0 were waited for; matrix products, arithmetic and copies ran while one was open for 16% of the time, Pallas kernels for 21%

profile of v2, /device:TPU:0, one launch (start us, length us, event | category | flops | bytes accessed | tf_op | source)
XLA Modules:
  0.0 580.5 jit_solution(16012609023228008197)
XLA Ops:
  16.3 4.8 collective-permute-start
  22.0 6.2 %copy.113 = bf16[1024,2,1024]{2,0,1:T(8,128)(2,1)} copy(bf16[1024,2,1024]{2,1,0:T(2,128)(2,1)} %param.20) | data formatting | bytes 8388608 | tf_op args[4]
  31.1 7.8 %shard_map.271 = (bf16[320,1024]{1,0:T(8,128)(2,1)S(1)}, bf16[16,2048]{1,0:T(8,128)(2,1)S(1)}, bf16[2,2048,1024]{2,1,0:T(8,128)(2,1)S(1)}) custom-call(bf16[320,512]{1,0:T(8,128)(2,1)S(1)} %pad.18.refs_0_, bf16[16,1024]{1,0:T(8,128)(2,1)S(1)} %fusion.103.refs_1_, bf16[2,1024,1024]{2,1,0:T(8,128)(2,1)S(1)} %bitcast.202), custom_call_target="tpu_custom_call" | custom-call | tf_op jit(solution)/shard_map/pallas_call | solution.py:392
  50.9 4.2 fusion
  67.2 6.0 %fusion.83 = bf16[512,1024]{1,0:T(8,128)(2,1)S(1)} fusion(bf16[512,2048]{1,0:T(8,128)(2,1)} %bitcast.230, bf16[2,2048,1024]{2,1,0:T(8,128)(2,1)} %copy-done.1), kind=kOutput, calls=%fused_computation.110 | convolution fusion | flops 2148007936 | bytes 7340032 | tf_op jit(solution)/shard_map/dot_general | solution.py:813
  78.1 18.4 %shard_map.272 = f32[160,512]{1,0:T(8,128)} custom-call(bf16[160,512]{1,0:T(8,128)(2,1)} %convolution_convert_fusion.7.refs_0_), custom_call_target="tpu_custom_call" | custom-call | tf_op jit(solution)/shard_map/pallas_call | solution.py:318
  108.0 35.5 %shard_map.273 = (f32[512,1024]{1,0:T(8,128)S(1)}, f32[512,16,8,128]{3,2,1,0:T(8,128)}, f32[2,16,8,128]{3,2,1,0:T(8,128)S(1)}, f32[4096,128]{1,0:T(8,128)S(1)}, f32[4096,128]{1,0:T(8,128)}) custom-call(f32[512,1024]{1,0:T(8,128)} %get-tuple-element.146.size_ref, f32[512,1024]{1,0:T(8,128)} %get-tuple-element.122.act_ref, ...), custom_call_target="tpu_custom_call" | custom-call | tf_op jit(solution)/shard_map/pallas_call | solution.py:558
  145.5 5.9 %multiply_convert_fusion.5 = (bf16[512,1024]{1,0:T(8,128)(2,1)}, f32[512,1024]{1,0:T(8,128)}) fusion(f32[512,1024]{1,0:T(8,128)S(1)} %get-tuple-element.47, bf16[512,1024]{1,0:T(8,128)(2,1)S(1)} %copy-done.11, f32[1024]{0:T(1024)S(1)} %bitcast.263, bf16[512,2048]{1,0:T(8,128)(2,1)} %bitcast.231, bf16[2,2048,1024]{2,1,0:T(8,128)(2,1)S(1)} %bitcast.204), kind=kOutput, calls=%fused_computation.83 | convolution fusion | flops 2152202240 | bytes 12587008 | tf_op jit(solution)/shard_map/dot_general | solution.py:814
  157.6 59.1 %shard_map.274 = (bf16[512,2048]{1,0:T(8,128)(2,1)}, f32[512,2048]{1,0:T(8,128)}) custom-call(bf16[512,2048]{1,0:T(8,128)(2,1)} %pad_maximum_fusion.2.refs_0_, bf16[512,2048]{1,0:T(8,128)(2,1)} %bitcast.211, f32[1,2048]{1,0:T(1,128)} %get-tuple-element.140.refs_2_), custom_call_target="tpu_custom_call" | custom-call | tf_op jit(solution)/shard_map/pallas_call | solution.py:318
  223.2 6.5 %fusion.6 = f32[512,1024]{1,0:T(8,128)} fusion(bf16[512,2048]{1,0:T(8,128)(2,1)} %get-tuple-element.48, bf16[1,2048,1024]{2,1,0:T(8,128)(2,1)} %all-gather.15.cloned.1.call-done), kind=kOutput, calls=%fused_computation.11 | convolution fusion | flops 2147483648 | bytes 8388608 | tf_op jit(solution)/shard_map/dot_general | solution.py:844
  229.7 7.2 %multiply_convert_fusion.2 = (bf16[512,1024]{1,0:T(8,128)(2,1)S(1)}, bf16[512,1024]{1,0:T(8,128)(2,1)S(1)}, bf16[512,1024]{1,0:T(8,128)(2,1)S(1)}) fusion(f32[512,1024]{1,0:T(8,128)} %fusion.6, f32[512,1024]{1,0:T(8,128)} %fusion.65, bf16[512,2048]{1,0:T(8,128)(2,1)} %get-tuple-element.48, bf16[1,2048,1024]{2,1,0:T(8,128)(2,1)} %all-gather.13.cloned.1.call-done), kind=kOutput, calls=%fused_computation.78 | convolution fusion | flops 2155347968 | bytes 13631488 | tf_op jit(solution)/shard_map/dot_general | solution.py:844
  236.9 4.4 convolution_convert_fusion.2
  241.3 4.5 convolution_convert_fusion.3
  245.8 4.8 convolution_convert_fusion.4
  262.4 68.4 %shard_map.275 = (bf16[512,2048]{1,0:T(8,128)(2,1)}, f32[512,2048]{1,0:T(8,128)}, f32[256,1024]{1,0:T(8,128)}, f32[256,1024]{1,0:T(8,128)}, f32[256,1024]{1,0:T(8,128)}) custom-call(bf16[512,2048]{1,0:T(8,128)(2,1)} %get-tuple-element.152.refs_0_, f32[512,2048]{1,0:T(8,128)} %get-tuple-element.49.refs_1_.refs_9_, f32[1,2048]{1,0:T(1,128)} %get-tuple-element.140.refs_2_, ...), custom_call_target="tpu_custom_call" | custom-call | tf_op jit(solution)/shard_map/pallas_call | solution.py:318
  339.1 73.0 %shard_map.276 = (f32[512,1024]{1,0:T(8,128)}, f32[512,1024]{1,0:T(8,128)}, f32[16,8,512]{2,1,0:T(8,128)}, f32[16,8,512]{2,1,0:T(8,128)}, f32[16,8,128]{2,1,0:T(8,128)}, /*index=5*/bf16[512,2048]{1,0:T(8,128)(2,1)}) custom-call(f32[4096,128]{1,0:T(8,128)} %copy-done.2, f32[4096,128]{1,0:T(8,128)} %get-tuple-element.46.refs_1_, ...), custom_call_target="tpu_custom_call" | custom-call | tf_op jit(solution)/shard_map/pallas_call | solution.py:740
  416.9 4.4 convolution_convert_fusion
  421.2 4.4 convolution_convert_fusion.1
  425.7 4.4 fusion.12
  432.4 11.8 %shard_map.277 = bf16[160,512]{1,0:T(8,128)(2,1)} custom-call(bf16[160,512]{1,0:T(8,128)(2,1)} %pad_maximum_fusion.6.refs_0_), custom_call_target="tpu_custom_call" | custom-call | tf_op jit(solution)/shard_map/pallas_call | solution.py:318
  444.2 5.8 multiply_reduce_fusion.4
  462.0 4.5 bitcast_convert_fusion
  467.5 4.2 multiply_reduce_fusion.1
  472.4 82.8 %shard_map.278 = (bf16[512,2048]{1,0:T(8,128)(2,1)}, f32[256,1024]{1,0:T(8,128)}, f32[256,1024]{1,0:T(8,128)}, f32[256,1024]{1,0:T(8,128)}, f32[48,1024]{1,0:T(8,128)}, /*index=5*/f32[16,1024]{1,0:T(8,128)}) custom-call(bf16[512,2048]{1,0:T(8,128)(2,1)} %get-tuple-element.154.refs_0_, bf16[512,2048]{1,0:T(8,128)(2,1)} %bitcast.212, f32[1,2048]{1,0:T(1,128)} %copy-done.34, ...), custom_call_target="tpu_custom_call" | custom-call | tf_op jit(solution)/shard_map/pallas_call | solution.py:318
  (269 shorter events, 126.6 us)
Async XLA Ops:
  7.2 144.2 %all-gather.11.cloned.1.call-start = ((), (), s32[]{:S(2)}) async-start(), calls=%async_computation.1 | async-start | bytes 6291456 | tf_op jit(solution)/shard_map/all_gather | solution.py:786
  7.9 208.8 %all-gather.9.cloned.1.call-start = ((), (), s32[]{:S(2)}) async-start(), calls=%async_computation | async-start | bytes 6291456 | tf_op jit(solution)/shard_map/all_gather | solution.py:789
  8.7 214.5 %all-gather.15.cloned.1.call-start = ((), (), s32[]{:S(2)}) async-start(), calls=%async_computation.3 | async-start | bytes 6291456 | tf_op jit(solution)/shard_map/all_gather | solution.py:788
  14.7 215.0 %all-gather.13.cloned.1.call-start = ((), (), s32[]{:S(2)}) async-start(), calls=%async_computation.2 | async-start | bytes 6291456 | tf_op jit(solution)/shard_map/all_gather | solution.py:788
  16.3 33.1 %collective-permute-start = (bf16[2,3,2048]{2,0,1:T(2,128)(2,1)S(1)}, bf16[2,3,2048]{2,0,1:T(2,128)(2,1)S(1)}, u32[]{:S(2)}, u32[]{:S(2)}) collective-permute-start(bf16[2,3,2048]{2,0,1:T(2,128)(2,1)S(1)} %copy.94), channel_id=1, source_target_pairs={{0,4},{4,8},{8,12},{1,5},{5,9},{9,13},{2,6},{6,10},{10,14},{3,7},{... | collective-permute-start | bytes 73736 | tf_op jit(solution)/shard_map/ppermute | solution.py:806
  22.0 6.2 %copy-start.32 = (bf16[160,512]{1,0:T(8,128)(2,1)S(1)}, bf16[160,512]{1,0:T(8,128)(2,1)}, u32[]{:S(2)}) copy-start(bf16[160,512]{1,0:T(8,128)(2,1)} %param.23) | copy-start | bytes 491524
  22.0 6.2 %copy-start.33 = (bf16[128,512]{1,0:T(8,128)(2,1)S(1)}, bf16[128,512]{1,0:T(8,128)(2,1)}, u32[]{:S(2)}) copy-start(bf16[128,512]{1,0:T(8,128)(2,1)} %param.24) | copy-start | bytes 393220
  22.0 6.2 %copy-start.36 = (bf16[16,512]{1,0:T(8,128)(2,1)S(1)}, bf16[16,512]{1,0:T(8,128)(2,1)}, u32[]{:S(2)}) copy-start(bf16[16,512]{1,0:T(8,128)(2,1)} %param.26) | copy-start | bytes 49156
  22.0 6.2 %copy-start.37 = (bf16[4,512]{1,0:T(4,128)(2,1)S(1)}, bf16[4,512]{1,0:T(4,128)(2,1)}, u32[]{:S(2)}) copy-start(bf16[4,512]{1,0:T(4,128)(2,1)} %param.21) | copy-start | bytes 12292
  31.1 11.2 %copy-start.47 = (s32[2]{0:T(128)S(1)}, s32[2]{0:T(128)}, u32[]{:S(2)}) copy-start(s32[2]{0:T(128)} %param.17) | copy-start | bytes 28
  42.9 12.1 %copy-start.34 = (f32[1,2048]{1,0:T(1,128)}, f32[1,2048]{1,0:T(1,128)S(1)}, u32[]{:S(2)}) copy-start(f32[1,2048]{1,0:T(1,128)S(1)} %get-tuple-element.141.refs_2_) | copy-start | bytes 24580
  49.4 58.6 %copy-start.3 = (f32[2,8,8,128]{3,2,1,0:T(8,128)}, f32[2,8,8,128]{3,2,1,0:T(8,128)S(1)}, u32[]{:S(2)}) copy-start(f32[2,8,8,128]{3,2,1,0:T(8,128)S(1)} %copy.97) | copy-start | bytes 196612
  76.9 22.5 %copy-start.10 = (bf16[512,1024]{1,0:T(8,128)(2,1)}, bf16[512,1024]{1,0:T(8,128)(2,1)S(1)}, u32[]{:S(2)}) copy-start(bf16[512,1024]{1,0:T(8,128)(2,1)S(1)} %get-tuple-element.123) | copy-start | bytes 3145732
  105.2 40.2 %slice-start = ((s8[8388608]{0:T(1024)(128)(4,1)}), s8[4194304]{0:T(1024)(128)(4,1)S(1)}, s32[]{:S(2)}) async-start(s8[8388608]{0:T(1024)(128)(4,1)} %bitcast.203), calls=%async_computation.4 | async-start | bytes 8388608
  108.0 37.5 %slice-start.1 = ((s8[8388608]{0:T(1024)(128)(4,1)}), s8[4194304]{0:T(1024)(128)(4,1)S(1)}, s32[]{:S(2)}) async-start(s8[8388608]{0:T(1024)(128)(4,1)} %bitcast.203), calls=%async_computation.5 | async-start | bytes 8388608
  108.0 37.5 %copy-start.11 = (bf16[512,1024]{1,0:T(8,128)(2,1)S(1)}, bf16[512,1024]{1,0:T(8,128)(2,1)}, u32[]{:S(2)}) copy-start(bf16[512,1024]{1,0:T(8,128)(2,1)} %copy-done.10) | copy-start | bytes 3145732
  229.7 7.2 %copy-start.20 = (bf16[512,2048]{1,0:T(8,128)(2,1)S(1)}, bf16[512,2048]{1,0:T(8,128)(2,1)}, u32[]{:S(2)}) copy-start(bf16[512,2048]{1,0:T(8,128)(2,1)} %fusion.3.refs_3_) | copy-start | bytes 6291460
  339.1 73.0 %copy-start.25 = (f32[512,1024]{1,0:T(8,128)S(1)}, f32[512,1024]{1,0:T(8,128)}, u32[]{:S(2)}) copy-start(f32[512,1024]{1,0:T(8,128)} %get-tuple-element.147) | copy-start | bytes 6291460
  416.9 8.8 %slice-start.2 = ((s8[8388608]{0:T(1024)(128)(4,1)}), s8[4194304]{0:T(1024)(128)(4,1)S(1)}, s32[]{:S(2)}) async-start(s8[8388608]{0:T(1024)(128)(4,1)} %bitcast.205), calls=%async_computation.6 | async-start | bytes 8388608
  425.6 18.5 %copy-start.6 = (f32[2,259,1024]{2,1,0:T(8,128)S(1)}, f32[2,259,1024]{2,1,0:T(8,128)}, u32[]{:S(2)}) copy-start(f32[2,259,1024]{2,1,0:T(8,128)} %copy-done.5) | copy-start | bytes 6365188
  444.2 8.0 %copy-start.28 = (f32[256,1024]{1,0:T(8,128)S(1)}, f32[256,1024]{1,0:T(8,128)}, u32[]{:S(2)}) copy-start(f32[256,1024]{1,0:T(8,128)} %get-tuple-element.67) | copy-start | bytes 3145732
  450.5 10.5 %collective-permute-start.1 = (f32[2,3,1024]{2,1,0:T(4,128)S(1)}, f32[2,3,1024]{2,1,0:T(4,128)S(1)}, u32[]{:S(2)}, u32[]{:S(2)}) collective-permute-start(f32[2,3,1024]{2,1,0:T(4,128)S(1)} %slice.281), channel_id=1, source_target_pairs={{4,0},{8,4},{12,8},{5,1},{9,5},{13,9},{6,2},{10,6},{14,10},{7,3},{... | collective-permute-start | bytes 73736 | tf_op jit(solution)/shard_map/ppermute | solution.py:893
  459.6 6.9 %slice-start.4 = ((s8[8388608]{0:T(1024)(128)(4,1)}), s8[4194304]{0:T(1024)(128)(4,1)S(1)}, s32[]{:S(2)}) async-start(s8[8388608]{0:T(1024)(128)(4,1)} %bitcast.207), calls=%async_computation.8 | async-start | bytes 8388608
  555.3 11.5 %copy-start.22 = (bf16[512,2048]{1,0:T(8,128)(2,1)S(1)}, bf16[512,2048]{1,0:T(8,128)(2,1)}, u32[]{:S(2)}) copy-start(bf16[512,2048]{1,0:T(8,128)(2,1)} %get-tuple-element.60) | copy-start | bytes 6291460
  (50 other events, 153.6 us)
Sparse Core Ops, SparseCore 0:
  9.6 16.3 all-gather.10
  27.5 14.8 all-gather.8
  43.9 14.8 all-gather.14
  60.2 14.8 all-gather.12

commit v3 on v2

--- a/solution.py
+++ b/solution.py
@@ -102,6 +102,24 @@
             for c in range(min(self.ahead, self.count)):
                 self.copy_a(c).start()
 
+    def greet(self, barrier, met):
+        pl.semaphore_signal(barrier, inc=1, device_id={"tp": self.mate}, device_id_type=MESH)
+
+        @pl.when(self.middle)
+        def _():
+            pl.semaphore_signal(barrier, inc=1, device_id={"tp": self.across}, device_id_type=MESH)
+            pl.semaphore_wait(barrier, met + 2)
+
+        @pl.when(jnp.logical_not(self.middle))
+        def _():
+            pl.semaphore_wait(barrier, met + 1)
+
+    def start(self):
+        @pl.when(jnp.logical_not(self.middle))
+        def _():
+            for c in range(min(self.ahead, self.count)):
+                self.copy_a(c).start()
+
     def first(self, c):
         at = self.at(c)
         self.copy_a(c).wait_recv()
@@ -157,25 +175,138 @@
 share_ahead = 2
 
 
-def halving(count, axis):
-    return [(axis, 1 << k) for k in reversed(range(count.bit_length() - 1))]
+class Halving:
+    def __init__(self, arrays, step_rows=16):
+        self.step_rows = step_rows
+        shards, pieces = lax.axis_size("shard"), lax.axis_size("ctx")
+        self.n = len(arrays)
+        self.bits = [
+            (axis, 1 << k)
+            for axis, size in (("shard", shards), ("ctx", pieces))
+            for k in reversed(range(size.bit_length() - 1))
+        ]
+        self.depth = len(self.bits)
+        head = shards.bit_length() - 1
+        self.dims = list(range(self.depth))
+        self.orders = (self.dims, self.dims[:head] + self.dims[head:][::-1])
+        self.parts = [g.shape[0] // (shards * pieces) // step_rows for g in arrays]
+        self.folded = [g.reshape((2,) * self.depth + (p * step_rows, g.shape[1])) for g, p in zip(arrays, self.parts)]
+        self.tails = [g.shape[self.depth :] for g in self.folded]
+        self.pairs = (max(self.parts, default=0) + 1) // 2
+        self.turns = self.pairs + share_lag * (self.depth - 1)
+
+    def results(self):
+        return [jax.ShapeDtypeStruct(tail, f32) for tail in self.tails]
+
+    def scratch(self):
+        if not self.n:
+            return []
+        held = [pltpu.VMEM((2,) * (self.depth - 1) + tail, bf16) for tail in self.tails]
+        for j in range(self.depth):
+            held += [pltpu.VMEM((2,) * (self.depth - 1 - j) + tail, bf16) for tail in self.tails]
+        sem = pltpu.SemaphoreType.DMA((self.depth, self.n, max(self.parts)))
+        return held + [sem, sem, pltpu.SemaphoreType.DMA((self.n, max(self.parts)))]
+
+    def bind(self, full, shares, scratch):
+        n = self.n
+        self.partner, self.mine = [], []
+        if not n:
+            return
+        self.full, self.shares, self.own = full, shares, scratch[:n]
+        self.landed = [scratch[n * (j + 1) : n * (j + 2)] for j in range(self.depth)]
+        self.send, self.recv, self.own_sem = scratch[n * (self.depth + 1) :]
+        for axis, bit in self.bits:
+            here = lax.axis_index(axis)
+            self.mine.append((here // bit) % 2)
+            self.partner.append({axis: here + bit - 2 * bit * ((here // bit) % 2)})
+
+    def greet(self, barrier):
+        for who in self.partner:
+            pl.semaphore_signal(barrier, inc=1, device_id=who, device_id_type=MESH)
+        return len(self.partner)
+
+    def spot(self, c):
+        return pl.ds(pl.multiple_of(c * self.step_rows, self.step_rows), self.step_rows)
+
+    def pick(self, remaining, dim, index, c):
+        return tuple(index if d == dim else slice(None) for d in remaining) + (self.spot(c), slice(None))
+
+    def rest(self, order, j):
+        return [d for d in self.dims if d not in order[:j]]
+
+    def copy(self, j, a, c, order):
+        source = self.full[a] if j == 0 else self.landed[j - 1][a]
+        d = order[j]
+        return pltpu.make_async_remote_copy(
+            source.at[self.pick(self.rest(order, j), d, 1 - self.mine[d], c)],
+            self.landed[j][a].at[self.pick(self.rest(order, j + 1), None, None, c)],
+            self.send.at[j, a, c],
+            self.recv.at[j, a, c],
+            device_id=self.partner[d],
+            device_id_type=MESH,
+        )
+
+    def own_copy(self, a, c, order):
+        return pltpu.make_async_copy(
+            self.full[a].at[self.pick(self.dims, order[0], self.mine[order[0]], c)],
+            self.own[a].at[self.pick(self.rest(order, 1), None, None, c)],
+            self.own_sem.at[a, c],
+        )
+
+    def begin(self, a, c, order):
+        self.copy(0, a, c, order).start()
+        self.own_copy(a, c, order).start()
+
+    def step(self, j, a, c, order):
+        self.copy(j, a, c, order).wait_recv()
+        where = self.pick(self.rest(order, j + 1), None, None, c)
+        d = order[j]
+        if j == 0:
+            self.own_copy(a, c, order).wait()
+            kept = self.own[a][where]
+        else:
+            kept = self.landed[j - 1][a][self.pick(self.rest(order, j), d, self.mine[d], c)]
+        total = kept.astype(f32) + self.landed[j][a][where].astype(f32)
+        if j == self.depth - 1:
+            self.shares[a][self.spot(c), :] = total
+        else:
+            self.landed[j][a][where] = total.astype(bf16)
+            self.copy(j + 1, a, c, order).start()
+
+    def each(self, i, fn):
+        for parity in (0, 1):
+            c = 2 * i + parity
+            for a in range(self.n):
+
+                @pl.when(jnp.logical_and(c >= 0, c < self.parts[a]))
+                def _():
+                    fn(a, c, self.orders[parity])
+
+    def start(self):
+        for i in range(share_ahead if self.n else 0):
+            self.each(i, self.begin)
+
+    def tick(self, i):
+        if self.n:
+            self.each(i + share_ahead, self.begin)
+            for j in range(self.depth):
+                self.each(i - share_lag * j, functools.partial(self.step, j))
+
+    def finish(self):
+        def sent(i, _):
+            for j in range(self.depth):
+                self.each(i, lambda a, c, order: self.copy(j, a, c, order).wait_send())
+            return 0
+
+        if self.n:
+            lax.fori_loop(0, self.pairs, sent, 0)
 
 
 def tp_sum(partial, epilogue, extras, extra_outs, chunk, ident, out_dtype=bf16, scatters=(), line_too=False):
-    rows, width = partial.shape
     line = Line(partial.shape, chunk, epilogue, extras, out_dtype)
-    n_line = len(line.scratch())
+    share = Halving(scatters)
     n_ex, n_out, n_sc = len(extras), len(extra_outs), len(scatters)
-    shards, pieces = lax.axis_size("shard"), lax.axis_size("ctx")
-    bits = halving(shards, "shard") + halving(pieces, "ctx")
-    depth = len(bits)
-    head = shards.bit_length() - 1
-    dims = list(range(depth))
-    orders = (dims, dims[:head] + dims[head:][::-1])
-    step_rows = 16
-    blocks = [g.shape[0] // (shards * pieces) for g in scatters]
-    parts = [r // step_rows for r in blocks]
-    folded = [g.reshape((2,) * depth + (r, g.shape[1])) for g, r in zip(scatters, blocks)]
+    n_line, n_share = len(line.scratch()), len(share.scratch())
 
     def kernel(*refs):
         refs = list(refs)
@@ -192,141 +323,50 @@
         outs = take_refs(n_out)
         shares = take_refs(n_sc)
         line.bind(p_ref, ins, out_ref, outs, take_refs(n_line))
-        own = take_refs(n_sc)
-        landed = [take_refs(n_sc) for _ in range(depth if n_sc else 0)]
-        r_send, r_recv, own_sem = take_refs(3) if n_sc else (None, None, None)
+        share.bind(full, shares, take_refs(n_share))
         tail, tail_send, tail_recv = take_refs(3) if line_too else (None, None, None)
         barrier = pltpu.get_barrier_semaphore()
-        mine, partner = [], []
-        for axis, bit in bits if n_sc else []:
-            here = lax.axis_index(axis)
-            mine.append((here // bit) % 2)
-            partner.append({axis: here + bit - 2 * bit * ((here // bit) % 2)})
-
-        def spot(c):
-            return pl.ds(pl.multiple_of(c * step_rows, step_rows), step_rows)
-
-        def pick(remaining, dim, index, c):
-            return tuple(index if d == dim else slice(None) for d in remaining) + (spot(c), slice(None))
-
-        def rest(order, j):
-            return [d for d in dims if d not in order[:j]]
-
-        def share_copy(j, a, c, order):
-            source = full[a] if j == 0 else landed[j - 1][a]
-            d = order[j]
-            return pltpu.make_async_remote_copy(
-                source.at[pick(rest(order, j), d, 1 - mine[d], c)],
-                landed[j][a].at[pick(rest(order, j + 1), None, None, c)],
-                r_send.at[j, a, c],
-                r_recv.at[j, a, c],
-                device_id=partner[d],
-                device_id_type=MESH,
-            )
-
-        def own_copy(a, c, order):
-            return pltpu.make_async_copy(
-                full[a].at[pick(dims, order[0], mine[order[0]], c)],
-                own[a].at[pick(rest(order, 1), None, None, c)],
-                own_sem.at[a, c],
-            )
-
-        def share_step(j, a, c, order):
-            share_copy(j, a, c, order).wait_recv()
-            where = pick(rest(order, j + 1), None, None, c)
-            d = order[j]
-            if j == 0:
-                own_copy(a, c, order).wait()
-                kept = own[a][where]
-            else:
-                kept = landed[j - 1][a][pick(rest(order, j), d, mine[d], c)]
-            total = kept.astype(f32) + landed[j][a][where].astype(f32)
-            if j == depth - 1:
-                shares[a][spot(c), :] = total
-            else:
-                landed[j][a][where] = total.astype(bf16)
-                share_copy(j + 1, a, c, order).start()
-
-        def each_part(i, fn):
-            for parity in (0, 1):
-                c = 2 * i + parity
-                for a in range(n_sc):
-
-                    @pl.when(jnp.logical_and(c >= 0, c < parts[a]))
-                    def _():
-                        fn(a, c, orders[parity])
-
-        for who in partner:
-            pl.semaphore_signal(barrier, inc=1, device_id=who, device_id_type=MESH)
-        line.begin(barrier, len(partner), line_too)
-
-        def begin(a, c, order):
-            share_copy(0, a, c, order).start()
-            own_copy(a, c, order).start()
-
-        pairs = (max(parts, default=0) + 1) // 2
-        if n_sc:
-
-            for i in range(share_ahead):
-                each_part(i, begin)
+        line.begin(barrier, share.greet(barrier), line_too)
+        share.start()
 
         def turn(i, _):
             for parity in (0, 1):
                 line.tick(2 * i + parity)
-            each_part(i + share_ahead, begin)
-            for j in range(depth if n_sc else 0):
-                each_part(i - share_lag * j, functools.partial(share_step, j))
+            share.tick(i)
             return 0
 
         turns = (line.ticks() + 1) // 2
-        if n_sc:
-            turns = max(turns, pairs + share_lag * (depth - 1))
-        lax.fori_loop(0, turns, turn, 0)
+        lax.fori_loop(0, max(turns, share.turns) if n_sc else turns, turn, 0)
         if line_too:
-            top = shares[-1].at[pl.ds(0, 8)]
+            height = shares[-1].shape[0]
+            last = pl.ds(height - 8, 8)
             for k, to in enumerate((line.mate, line.across)):
                 copy = pltpu.make_async_remote_copy(
-                    top if k == 0 else tail.at[2], tail.at[k], tail_send.at[k], tail_recv.at[k],
+                    shares[-1].at[last] if k == 0 else tail.at[2], tail.at[k], tail_send.at[k], tail_recv.at[k],
                     device_id={"tp": to}, device_id_type=MESH,
                 )
                 copy.start()
                 copy.wait()
                 if k == 0:
-                    tail[2] = top[...] + tail[0]
-            shares[-1][pl.ds(0, 8), :] = tail[2] + tail[1]
+                    tail[2] = shares[-1][last, :] + tail[0]
+            shares[-1][last, :] = tail[2] + tail[1]
         line.finish()
-
-        if n_sc:
-
-            def sent(i, _):
-                for j in range(depth):
-                    each_part(i, lambda a, c, order: share_copy(j, a, c, order).wait_send())
-                return 0
-
-            lax.fori_loop(0, pairs, sent, 0)
+        share.finish()
 
     buffers = []
-    if n_sc:
-        buffers += [pltpu.VMEM((2,) * (depth - 1) + g.shape[depth:], bf16) for g in folded]
-        for j in range(depth):
-            buffers += [pltpu.VMEM((2,) * (depth - 1 - j) + g.shape[depth:], bf16) for g in folded]
-        sem = pltpu.SemaphoreType.DMA((depth, n_sc, max(parts)))
-        buffers += [sem, sem, pltpu.SemaphoreType.DMA((n_sc, max(parts)))]
     if line_too:
         pair_sem = pltpu.SemaphoreType.DMA((2,))
-        buffers += [pltpu.VMEM((3, 8, folded[-1].shape[-1]), f32), pair_sem, pair_sem]
+        buffers += [pltpu.VMEM((3, 8, scatters[-1].shape[-1]), f32), pair_sem, pair_sem]
     return pl.pallas_call(
         kernel,
-        out_shape=[jax.ShapeDtypeStruct((rows, width), out_dtype)]
-        + list(extra_outs)
-        + [jax.ShapeDtypeStruct(g.shape[depth:], f32) for g in folded],
+        out_shape=[jax.ShapeDtypeStruct(partial.shape, out_dtype)] + list(extra_outs) + share.results(),
         in_specs=[HBM] * (1 + n_ex + n_sc),
         out_specs=[VMEM] * (1 + n_out + n_sc),
-        scratch_shapes=line.scratch() + buffers,
+        scratch_shapes=line.scratch() + share.scratch() + buffers,
         compiler_params=pltpu.CompilerParams(
             collective_id=ident, has_side_effects=True, vmem_limit_bytes=56 << 20
         ),
-    )(partial, *extras, *folded)
+    )(partial, *extras, *share.folded)
 
 
 def plain_end(c, rows, total, ins, out_ref, outs):
@@ -355,54 +395,196 @@
     out_ref[rows, :] = result.astype(bf16)
 
 
-def shard_gather(arrays, dims, ident):
-    shards = lax.axis_size("shard")
-    n = len(arrays)
-
-    def kernel(*refs):
-        ins, outs, (send, recv, own) = refs[:n], refs[n : 2 * n], refs[2 * n :]
-        me = lax.axis_index("shard")
+halo = 16
+tile_cols = 256
+
+
+def front(hidden, in_half, small, gains, seqs, at_conv, taps, low_len, ident):
+    rows, width = hidden.shape
+    local = rows // seqs
+    part, inner = in_half.shape[1:]
+    shards, pieces = lax.axis_size("shard"), lax.axis_size("ctx")
+    long = local + halo
+    tiles = inner // tile_cols
+    line = Line((low_len, rows), 80, plain_end, [], f32)
+    n_line = len(line.scratch())
+
+    def kernel(
+        hid_ref, tail_ref, in_ref, small_ref, gain_ref,
+        in_out, small_out, gain_out, normed_out, z_out, ext_out, pre_out, act_out, low_out,
+        own_w, got_w, edge, normed, ext_n, acc, z_val, conv_f, ext_c, pre, act, low_acc, small_all, gain_all,
+        send, recv, edge_sem, own_sem, out_sem, *rest
+    ):
+        me, ctx = lax.axis_index("shard"), lax.axis_index("ctx")
         barrier = pltpu.get_barrier_semaphore()
+        line.bind(rest[0], [], low_out, [], list(rest))
         for step in range(1, shards):
             pl.semaphore_signal(barrier, inc=1, device_id={"shard": lax.rem(me + step, shards)}, device_id_type=MESH)
-        pl.semaphore_wait(barrier, shards - 1)
-        copies = []
-        for i in range(n):
-            size = arrays[i].shape[dims[i]]
-            spot = pl.ds(pl.multiple_of(me * size, size), size)
-            place = outs[i].at[tuple(spot if k == dims[i] else slice(None) for k in range(arrays[i].ndim))]
+        pl.semaphore_signal(barrier, inc=1, device_id={"ctx": lax.rem(ctx + pieces - 1, pieces)}, device_id_type=MESH)
+        load = pltpu.make_async_copy(in_ref, own_w, own_sem.at[0])
+        load.start()
+        small_size, gain_size = small_ref.shape[1], gain_ref.shape[1]
+        small_at = pl.ds(pl.multiple_of(me * small_size, small_size), small_size)
+        gain_at = pl.ds(pl.multiple_of(me * gain_size, gain_size), gain_size)
+        small_all[:, small_at] = small_ref[...]
+        gain_all[:, gain_at] = gain_ref[...]
+        line.greet(barrier, shards)
+        edge_copy = pltpu.make_async_remote_copy(
+            tail_ref, edge, edge_sem.at[0], edge_sem.at[1],
+            device_id={"ctx": lax.rem(ctx + 1, pieces)}, device_id_type=MESH,
+        )
+        copies = {}
+        for step in range(1, shards):
+            peer = {"shard": lax.rem(me + step, shards)}
+            moves = [(gain_ref, gain_all.at[:, gain_at]), (small_ref, small_all.at[:, small_at])]
+            moves += [(in_ref.at[c], got_w.at[step - 1, c]) for c in range(2)]
+            for k, (source, target) in enumerate(moves):
+                copies[step, k] = pltpu.make_async_remote_copy(
+                    source, target, send.at[step, k], recv.at[step, k], device_id=peer, device_id_type=MESH
+                )
+        for k in range(4):
             for step in range(1, shards):
-                peer = lax.rem(me + step, shards)
-                copies.append(
-                    pltpu.make_async_remote_copy(
-                        ins[i], place, send.at[i, step], recv.at[i, step], device_id={"shard": peer}, device_id_type=MESH
-                    )
-                )
-                copies[-1].start()
-            copies.append(pltpu.make_async_copy(ins[i], place, own.at[i]))
-            copies[-1].start()
-        for copy in copies:
-            copy.wait()
-
-    def full(array, dim):
-        return jax.ShapeDtypeStruct(
-            tuple(s * shards if k == dim else s for k, s in enumerate(array.shape)), array.dtype
-        )
-
+                copies[step, k].start()
+            if k == 0:
+                edge_copy.start()
+        for step in range(1, shards):
+            copies[step, 0].wait_recv()
+        gain = gain_all[0:1, :].astype(f32)
+
+        def norm_rows(i, _):
+            at = pl.ds(pl.multiple_of(i * 16, 16), 16)
+            source = hid_ref[at, :].astype(f32)
+            value = (source * rms_scale(source) * gain).astype(bf16)
+            normed[at, :] = value
+            seq = i // (local // 16)
+            ext_n[pl.ds(pl.multiple_of(i * 16 + (seq + 1) * halo, 16), 16), :] = value
+            return 0
+
+        lax.fori_loop(0, rows // 16, norm_rows, 0)
+        edge_copy.wait_recv()
+        for seq in range(seqs):
+            source = edge[seq].astype(f32)
+            value = source * rms_scale(source) * gain * (ctx > 0).astype(f32)
+            ext_n[seq * long : seq * long + halo, :] = value.astype(bf16)
+        outs = [(normed, normed_out)]
+        pltpu.make_async_copy(normed, normed_out, out_sem.at[0]).start()
+
+        def cols(c, j):
+            return pl.ds(pl.multiple_of(c * inner + j * tile_cols, tile_cols), tile_cols)
+
+        def finish_conv(j):
+            here = pl.ds(pl.multiple_of(j * tile_cols, tile_cols), tile_cols)
+            value = acc[:, cols(0, j)].astype(bf16)
+            ext_c[:, here] = value
+            conv_f[...] = value.astype(f32)
+            weights = small_all[at_conv : at_conv + 16, here].astype(f32)
+            for seq in range(seqs):
+                for k in range(local // 64):
+                    first = seq * long + halo + k * 64
+                    total = weights[taps : taps + 1]
+                    for tap in range(taps):
+                        total = total + weights[tap : tap + 1] * conv_f[first - taps + 1 + tap : first - taps + 1 + tap + 64, :]
+                    to = slice(seq * local + k * 64, seq * local + (k + 1) * 64)
+                    pre[to, here] = total
+                    act[to, here] = jax.nn.silu(total).astype(bf16)
+            low = outer_cols(small_all[0:low_len, here], act[:, here])
+            low_acc[...] = low_acc[...] + low
+
+        def finish_gate(j):
+            here = pl.ds(pl.multiple_of(j * tile_cols, tile_cols), tile_cols)
+            for seq in range(seqs):
+                z_val[seq * local : (seq + 1) * local, here] = acc[seq * long + halo : (seq + 1) * long, cols(1, j)]
+
+        low_acc[...] = jnp.zeros_like(low_acc)
+        own_place = pl.ds(pl.multiple_of(me * part, part), part)
+        load.wait()
+        own_save = pltpu.make_async_copy(own_w, in_out.at[:, own_place], own_sem.at[1])
+        own_save.start()
+        saves = []
+        for step in range(shards):
+            owner = lax.rem(me - step + shards, shards)
+            place = pl.ds(pl.multiple_of(owner * part, part), part)
+            last = step == shards - 1
+            if last:
+                for other in range(1, shards):
+                    copies[other, 1].wait_recv()
+            for c in range(2):
+                weight = own_w.at[c] if step == 0 else got_w.at[step - 1, c]
+                if step > 0:
+                    copies[step, 2 + c].wait_recv()
+
+                def matmul(j, _):
+                    here = pl.ds(pl.multiple_of(j * tile_cols, tile_cols), tile_cols)
+                    value = jnp.dot(ext_n[:, place], weight[:, here], preferred_element_type=f32)
+                    acc[:, cols(c, j)] = value if step == 0 else acc[:, cols(c, j)] + value
+                    if last:
+                        (finish_conv, finish_gate)[c](j)
+                    return 0
+
+                lax.fori_loop(0, tiles, matmul, 0)
+            if step > 0:
+                saves.append(pltpu.make_async_copy(got_w.at[step - 1], in_out.at[:, place], own_sem.at[1 + step]))
+                saves[-1].start()
+        line.p[...] = low_acc[...].astype(bf16)
+        outs += [(z_val, z_out), (ext_c, ext_out), (pre, pre_out), (act, act_out), (small_all, small_out), (gain_all, gain_out)]
+        for k, (source, target) in enumerate(outs):
+            if k:
+                pltpu.make_async_copy(source, target, out_sem.at[k]).start()
+        line.start()
+        for c in range(line.ticks()):
+            line.tick(c)
+        line.finish()
+        for save in saves + [own_save]:
+            save.wait()
+        for k, (source, target) in enumerate(outs):
+            pltpu.make_async_copy(source, target, out_sem.at[k]).wait()
+        for copy in copies.values():
+            copy.wait_send()
+        edge_copy.wait_send()
+
+    sds = jax.ShapeDtypeStruct
+    tails = hidden.reshape(seqs, local, width)[:, local - halo :]
     return pl.pallas_call(
         kernel,
-        out_shape=[full(a, d) for a, d in zip(arrays, dims)],
-        in_specs=[VMEM] * n,
-        out_specs=[HBM] * n,
+        out_shape=[
+            sds((2, shards * part, inner), bf16),
+            sds((small.shape[0], small.shape[1] * shards), bf16),
+            sds((gains.shape[0], gains.shape[1] * shards), bf16),
+            sds((rows, width), bf16),
+            sds((rows, inner), f32),
+            sds((seqs * long, inner), bf16),
+            sds((rows, inner), f32),
+            sds((rows, inner), bf16),
+            sds((low_len, rows), f32),
+        ],
+        in_specs=[VMEM, HBM, HBM, VMEM, VMEM],
+        out_specs=[HBM] * 8 + [VMEM],
         scratch_shapes=[
-            pltpu.SemaphoreType.DMA((n, shards)),
-            pltpu.SemaphoreType.DMA((n, shards)),
-            pltpu.SemaphoreType.DMA((n,)),
-        ],
+            pltpu.VMEM((2, part, inner), bf16),
+            pltpu.VMEM((max(shards - 1, 1), 2, part, inner), bf16),
+            pltpu.VMEM((seqs, halo, width), bf16),
+            pltpu.VMEM((rows, width), bf16),
+            pltpu.VMEM((seqs * long, width), bf16),
+            pltpu.VMEM((seqs * long, 2 * inner), f32),
+            pltpu.VMEM((rows, inner), f32),
+            pltpu.VMEM((seqs * long, tile_cols), f32),
+            pltpu.VMEM((seqs * long, inner), bf16),
+            pltpu.VMEM((rows, inner), f32),
+            pltpu.VMEM((rows, inner), bf16),
+            pltpu.VMEM((low_len, rows), f32),
+            pltpu.VMEM((small.shape[0], small.shape[1] * shards), bf16),
+            pltpu.VMEM((gains.shape[0], gains.shape[1] * shards), bf16),
+            pltpu.SemaphoreType.DMA((shards, 4)),
+            pltpu.SemaphoreType.DMA((shards, 4)),
+            pltpu.SemaphoreType.DMA((2,)),
+            pltpu.SemaphoreType.DMA((shards + 1,)),
+            pltpu.SemaphoreType.DMA((7,)),
+        ]
+        + line.scratch(),
         compiler_params=pltpu.CompilerParams(
-            collective_id=ident, has_side_effects=True, vmem_limit_bytes=32 << 20
+            collective_id=ident, has_side_effects=True, vmem_limit_bytes=56 << 20
         ),
-    )(*arrays)
+    )(hidden, tails, in_half, small, gains)
 
 
 piece = 32
@@ -595,7 +777,7 @@
     return parts[0]
 
 
-def scan_backward(size3, drive3, grad, b_row, c_row, rate, kept, enter, seqs, ident, partial, epilogue, extras, chunk):
+def scan_backward(size3, drive3, grad, b_row, c_row, rate, kept, enter, seqs, ident, partial, epilogue, extras, chunk, scatters):
     rows, channels = grad.shape
     local = rows // seqs
     states = rate.shape[0]
@@ -604,14 +786,27 @@
     early = 2
     unroll_b = 2
     line = Line(partial.shape, chunk, epilogue, extras, bf16)
-    n_line, n_ex = len(line.scratch()), len(extras)
+    share = Halving(scatters, 64)
+    n_line, n_ex, n_sc = len(line.scratch()), len(extras), len(scatters)
 
     def kernel(*refs):
-        size_ref, drive_ref, grad_ref, b_ref, c_ref, rate_ref, kept_ref, enter_ref, p_ref = refs[:9]
-        tb_ref, sd_ref, bg_ref, cg_ref, dec_ref, sum_ref = refs[9 + n_ex : 15 + n_ex]
-        grad3, tb3, sd3, ends, got, held, bpart, cpart, prior, send, recv, in_sem = refs[15 + n_ex : 27 + n_ex]
-        line.bind(p_ref, refs[9 : 9 + n_ex], sum_ref, [], refs[27 + n_ex :])
-        line.begin(ctx_greet(width), width - 1)
+        refs = list(refs)
+
+        def take_refs(n):
+            taken = refs[:n]
+            del refs[:n]
+            return taken
+
+        size_ref, drive_ref, grad_ref, b_ref, c_ref, rate_ref, kept_ref, enter_ref, p_ref = take_refs(9)
+        ins, full = take_refs(n_ex), take_refs(n_sc)
+        tb_ref, sd_ref, bg_ref, cg_ref, dec_ref, sum_ref = take_refs(6)
+        shares = take_refs(n_sc)
+        grad3, tb3, sd3, ends, got, held, bpart, cpart, prior, send, recv, in_sem = take_refs(12)
+        line.bind(p_ref, ins, sum_ref, [], take_refs(n_line))
+        share.bind(full, shares, refs)
+        barrier = ctx_greet(width)
+        line.begin(barrier, width - 1 + share.greet(barrier))
+        share.start()
 
         def lay(i, _):
             first = pl.multiple_of(i * 8, 8)
@@ -717,6 +912,7 @@
                     sums = outer_cols(ones, part[...].astype(bf16))
                     out[pl.ds(seq * pieces + k, 1)] = sums[None]
                 line.tick(seqs * early + seq * pieces + back_k)
+                share.tick(seq * pieces + back_k)
                 return tuple(adjoint) + tuple(decays)
 
             zero = tuple(jnp.zeros((8, 128), f32) for _ in range(states))
@@ -733,16 +929,19 @@
         lax.fori_loop(0, rows // 8, back, 0)
         for c in range(seqs * (early + pieces), line.ticks()):
             line.tick(c)
+        for i in range(seqs * pieces, share.turns):
+            share.tick(i)
         line.finish()
+        share.finish()
 
     nat = jax.ShapeDtypeStruct((rows, channels), f32)
     sums = jax.ShapeDtypeStruct((rows // piece, 8, piece * states), f32)
     return pl.pallas_call(
         kernel,
         out_shape=[nat, nat, sums, sums, jax.ShapeDtypeStruct((states, 8, 128), f32),
-                   jax.ShapeDtypeStruct(partial.shape, bf16)],
-        in_specs=[VMEM] * 6 + [HBM, VMEM] + [HBM] * (1 + n_ex),
-        out_specs=[VMEM] * 6,
+                   jax.ShapeDtypeStruct(partial.shape, bf16)] + share.results(),
+        in_specs=[VMEM] * 6 + [HBM, VMEM] + [HBM] * (1 + n_ex + n_sc),
+        out_specs=[VMEM] * (6 + n_sc),
         scratch_shapes=[pltpu.VMEM((rows * 8, 128), f32)] * 3
         + [
             pltpu.VMEM((seqs, states + 1, 8, 128), f32),
@@ -755,11 +954,12 @@
             pltpu.SemaphoreType.DMA((seqs, width)),
             pltpu.SemaphoreType.DMA((2,)),
         ]
-        + line.scratch(),
+        + line.scratch()
+        + share.scratch(),
         compiler_params=pltpu.CompilerParams(
-            collective_id=ident, has_side_effects=True, vmem_limit_bytes=58 << 20
+            collective_id=ident, has_side_effects=True, vmem_limit_bytes=62 << 20
         ),
-    )(size3, drive3, grad, b_row, c_row, rate, kept, enter, partial, *extras)
+    )(size3, drive3, grad, b_row, c_row, rate, kept, enter, partial, *extras, *share.folded)
 
 
 def body(
@@ -778,11 +978,14 @@
     small = jnp.concatenate(
         [low_weight, step_weight, decay_log, conv_weight, conv_bias[None], step_bias[None], skip_gain[None]], axis=0
     )
+    hidden_rows = hidden_in.reshape(rows, width)
     small = jnp.pad(small, ((0, -small.shape[0] % 16), (0, 0)))
     gains = jnp.stack([norm_gain, ffn_gain])
     gains = jnp.pad(gains, ((0, 14), (0, 0)))
     in_half = in_weight.transpose(1, 0, 2)
-    small, gains, in_w = shard_gather([small, gains, in_half], [1, 1, 1], 0)
+    in_w, small, gains, normed_one, gate_z, padded, pre_act, act_half, low_all = front(
+        hidden_rows, in_half, small, gains, seqs, low_len + rank + states, taps, low_len, 0
+    )
     out_parts = lax.all_gather(out_weight, "shard")
     gate_half = gate_up.transpose(1, 0, 2)
     gate_w = [lax.all_gather(gate_half[c], "shard", axis=0, tiled=True) for c in range(2)]
@@ -803,25 +1006,9 @@
     positions = first_slot + jnp.arange(local, dtype=jnp.int32)
     pad_mask = (positions[None, :] < lengths[:, None]).astype(f32)
 
-    ahead = lax.ppermute(hidden_in[:, local - taps + 1 :], "ctx", [(k, k + 1) for k in range(pieces - 1)])
-    longer = jnp.concatenate([ahead, hidden_in], axis=1).astype(f32)
-    normed_all = (longer * rms_scale(longer) * gain_one).astype(bf16)
-    source = hidden_in.reshape(rows, width).astype(f32)
-    normed_one = normed_all[:, taps - 1 :].reshape(rows, width)
-    normed_edge = normed_all[:, : taps - 1].reshape(seqs * (taps - 1), width)
-    edge_in = jnp.dot(normed_edge, in_w[0], preferred_element_type=f32).astype(bf16)
-    conv_in = jnp.dot(normed_one, in_w[0], preferred_element_type=f32).astype(bf16)
-    gate_z = jnp.dot(normed_one, in_w[1], preferred_element_type=f32)
-    padded = jnp.concatenate(
-        [edge_in.reshape(seqs, taps - 1, inner), conv_in.reshape(seqs, local, inner)], axis=1
-    ).astype(f32)
-    pre_act = conv_b + sum(kernel[k] * padded[:, k : k + local] for k in range(taps))
-    pre_act = pre_act.reshape(rows, inner)
-    act_half = jax.nn.silu(pre_act).astype(bf16)
+    source = hidden_rows.astype(f32)
+    padded = padded.reshape(seqs, halo + local, inner)[:, halo - taps + 1 :].astype(f32)
     act_full = act_half.astype(f32)
-
-    low_part = outer_cols(low_w, act_half).astype(bf16)
-    low_all = tp_sum(low_part, plain_end, [], [], 80, 1, f32)[0]
     step_low = low_all[:rank].astype(bf16)
     b_in, c_out = low_all[rank : rank + states], low_all[rank + states :]
     b_row, c_row = (
@@ -839,7 +1026,6 @@
         [jnp.dot(gated_out, out_parts[k], preferred_element_type=f32) for k in range(shards)], axis=1
     ).astype(bf16)
     wide = jax.ShapeDtypeStruct((rows, width), f32)
-    hidden_rows = hidden_in.reshape(rows, width)
     normed_two, middle = tp_sum(mixed_part, norm_end, [hidden_rows, gain_two], [wide], 32, 3)
     gate_lin, up_lin = (jnp.dot(normed_two, gate_w[c], preferred_element_type=f32) for c in range(2))
     hidden_ffn = (jax.nn.silu(gate_lin) * up_lin).astype(bf16)
@@ -865,8 +1051,9 @@
     scan_grad = gated_grad * gate_act
     z_grad = gated_grad * scan_out * silu_grad(gate_z)
     skip_gain_grad = jnp.sum(scan_grad * act_full, axis=0)
-    through_b, through_decay, b_sums, c_sums, decay_sum, mixed_out = scan_backward(
-        size3, drive3, scan_grad, b_row, c_row, rate, kept, enter, seqs, 6, ffn_part, add_end, [middle], 32
+    through_b, through_decay, b_sums, c_sums, decay_sum, mixed_out, out_share = scan_backward(
+        size3, drive3, scan_grad, b_row, c_row, rate, kept, enter, seqs, 6, ffn_part, add_end, [middle], 32,
+        [out_weight_grad],
     )
     mixed_out = mixed_out.reshape(hidden_in.shape)
     decay_log_grad = decay_sum.reshape(states, inner) * decay_rate
@@ -903,26 +1090,30 @@
          step_bias_grad[None], skip_gain_grad[None]], axis=0,
     )
     places = shards * pieces
-    lines, lane = small_grads.shape[0], inner // places
+    lines, lane, share = small_grads.shape[0], inner // places, width // places
+    small_rows = -(-(lines * lane) // (16 * inner)) * 16
+    if small_rows * inner - lines * lane < 8 * inner:
+        small_rows += 16
     small_blocks = small_grads.reshape(lines, places, lane).transpose(1, 0, 2).reshape(places, lines * lane)
-    small_rows = -(-lines * lane // (16 * inner)) * 16
-    small_blocks = jnp.pad(small_blocks, ((0, 0), (0, small_rows * inner - lines * lane)))
+    gain_blocks = jnp.concatenate([norm_gain_grad.reshape(places, share), ffn_gain_grad.reshape(places, share)], axis=1)
+    fill = (small_rows - 8) * inner - lines * lane
+    small_blocks = jnp.concatenate(
+        [small_blocks, jnp.zeros((places, fill), f32), gain_blocks, jnp.zeros((places, 8 * inner - 2 * share), f32)],
+        axis=1,
+    )
     small_blocks = small_blocks.reshape(places * small_rows, inner).astype(bf16)
-    share = width // places
-    gain_blocks = jnp.concatenate([norm_gain_grad.reshape(places, share), ffn_gain_grad.reshape(places, share)], axis=1)
-    gain_blocks = jnp.pad(gain_blocks[:, None], ((0, 0), (0, 15), (0, inner - 2 * share))).astype(bf16)
-    input_grad, in_share, z_share, out_share, small_share, gain_share = tp_sum(
+    input_grad, in_share, z_share, small_share = tp_sum(
         first_part, norm_back_end, [hidden_rows, gain_one, middle_grad], [], 32, 8,
-        scatters=in_weight_grad + [out_weight_grad, small_blocks, gain_blocks.reshape(places * 16, inner)],
-        line_too=True,
+        scatters=in_weight_grad + [small_blocks], line_too=True,
     )
+    gain_share = small_share[small_rows - 8]
     input_grad = input_grad.astype(f32).reshape(hidden_in.shape)
     small_out = small_share.reshape(-1)[: lines * lane].reshape(lines, lane)
     at = low_len + rank
     return (
         mixed_out,
         input_grad,
-        gain_share[0, :share],
+        gain_share[:share],
         jnp.stack([in_share, z_share], axis=1),
         small_out[at + states : at + states + taps],
         small_out[at + states + taps],
@@ -932,7 +1123,7 @@
         small_out[at : at + states],
         small_out[at + states + taps + 2],
         out_share.T,
-        gain_share[0, share : 2 * share],
+        gain_share[share : 2 * share],
         jnp.stack(ffn_shares[:2], axis=1),
         ffn_shares[2].T,
     )

time: 585 us -> 567 us (0.969)
  local copies, waits for them, and re-layouts: 73.6 us -> 51.8 us
  Pallas kernels: 357 us -> 366 us
  matrix products: 102 us -> 95.4 us
    dot_general x3 -> x0, matrix products: 14.7 us -> none  [the longest x1 6.04 us: body(): jnp.dot(normed_one, in_w[0], preferred_element_type=f32).astype(bf16)]
    unnamed x152 -> x145, local copies, waits for them, and re-layouts: 43.2 us -> 30.5 us
    pallas_call x6 -> x5, Pallas kernels: 248 us -> 255 us  [the longest x4 217 us: tp_sum(): pl.pallas_call(kernel, out_shape=[jax.ShapeDtypeStruct(partial.shape, out...]
    dot_general x10 -> x9, matrix products: 29.4 us -> 32.4 us  [outer_cols(): lax.dot_general(left, right, (((1,), (1,)), ((), ())), preferred_element_...]
  transfers between devices with their start and end apart: 6 -> 5, of which waited for: 0 -> 0; matrix products, arithmetic and copies ran while one was open for 16% -> 15% of each run, Pallas kernels for 21% -> 24%
where the time goes in v3:
time: 567 us; the launch traced here: 560 us
  Pallas kernels  366 us (65%)
  matrix products  95.4 us (17%)
  local copies, waits for them, and re-layouts  51.8 us (9%)
  other arithmetic  28.3 us (5%)
  between operations  14.8 us (3%)
    pallas_call x4, Pallas kernels, tp_sum(): pl.pallas_call(kernel, out_shape=[jax.ShapeDtypeStruct(partial.shape, out...  217 us
    pallas_call x1, Pallas kernels, scan_backward(): pl.pallas_call(kernel, out_shape=[nat, nat, sums, sums, jax.ShapeDtypeStr...  75.7 us
    dot_general x8, matrix products, inner_rows(): lax.dot_general(left, right, (((0,), (0,)), ((), ())), preferred_element_...  40.7 us
    pallas_call x1, Pallas kernels, front(): pl.pallas_call(kernel, out_shape=[sds((2, shards * part, inner), bf16), s...  37.9 us
    pallas_call x1, Pallas kernels, scan_forward(): pl.pallas_call(kernel, out_shape=[jax.ShapeDtypeStruct((rows, channels),...  35.6 us
    dot_general x9, matrix products, outer_cols(): lax.dot_general(left, right, (((1,), (1,)), ((), ())), preferred_element_...  32.4 us
    unnamed x145, local copies, waits for them, and re-layouts  30.5 us
    dot_general x2, matrix products, body(): jnp.dot(normed_two, gate_w[c], preferred_element_type=f32)  13.7 us
  transfers between devices with their start and end apart: 5, of which 0 were waited for; matrix products, arithmetic and copies ran while one was open for 15% of the time, Pallas kernels for 24%

profile of v3, /device:TPU:0, one launch (start us, length us, event | category | flops | bytes accessed | tf_op | source)
XLA Modules:
  0.0 560.1 jit_solution(5224819620097938010)
XLA Ops:
  17.5 6.2 %copy.61 = bf16[1024,2,1024]{2,0,1:T(8,128)(2,1)} copy(bf16[1024,2,1024]{2,1,0:T(2,128)(2,1)} %param.20) | data formatting | bytes 8388608 | tf_op args[4]
  25.2 37.9 %shard_map.271 = (bf16[2,2048,1024]{2,1,0:T(8,128)(2,1)}, bf16[320,1024]{1,0:T(8,128)(2,1)}, bf16[16,2048]{1,0:T(8,128)(2,1)}, bf16[512,2048]{1,0:T(8,128)(2,1)}...) custom-call(bf16[512,2048]{1,0:T(8,128)(2,1)} %bitcast.150, ...), custom_call_target="tpu_custom_call" | custom-call | tf_op jit(solution)/shard_map/pallas_call | solution.py:547
  73.4 4.2 compare_select_fusion
  82.9 35.6 %shard_map.272 = (f32[512,1024]{1,0:T(8,128)S(1)}, f32[512,16,8,128]{3,2,1,0:T(8,128)}, f32[2,16,8,128]{3,2,1,0:T(8,128)S(1)}, f32[4096,128]{1,0:T(8,128)S(1)}, f32[4096,128]{1,0:T(8,128)}) custom-call(f32[512,1024]{1,0:T(8,128)} %get-tuple-element.138.size_ref, f32[512,1024]{1,0:T(8,128)} %convert_element_type.122.act_ref, ...), custom_call_target="tpu_custom_call" | custom-call | tf_op jit(solution)/shard_map/pallas_call | solution.py:740
  130.5 62.7 %shard_map.273 = (bf16[512,2048]{1,0:T(8,128)(2,1)}, f32[512,2048]{1,0:T(8,128)}) custom-call(bf16[512,2048]{1,0:T(8,128)(2,1)} %pad_maximum_fusion.1.refs_0_, bf16[512,2048]{1,0:T(8,128)(2,1)} %bitcast.151, f32[1,2048]{1,0:T(1,128)} %get-tuple-element.133.refs_2_), custom_call_target="tpu_custom_call" | custom-call | tf_op jit(solution)/shard_map/pallas_call | solution.py:360
  199.7 6.5 %fusion.7 = f32[512,1024]{1,0:T(8,128)} fusion(bf16[512,2048]{1,0:T(8,128)(2,1)} %get-tuple-element.55, bf16[1,2048,1024]{2,1,0:T(8,128)(2,1)} %all-gather.15.cloned.1.call-done), kind=kOutput, calls=%fused_computation.9 | convolution fusion | flops 2147483648 | bytes 8388608 | tf_op jit(solution)/shard_map/dot_general | solution.py:1030
  206.2 7.2 %multiply_convert_fusion.2 = (bf16[512,1024]{1,0:T(8,128)(2,1)S(1)}, bf16[512,1024]{1,0:T(8,128)(2,1)S(1)}, bf16[512,1024]{1,0:T(8,128)(2,1)S(1)}) fusion(f32[512,1024]{1,0:T(8,128)} %fusion.7, f32[512,1024]{1,0:T(8,128)} %fusion.50, bf16[512,2048]{1,0:T(8,128)(2,1)} %get-tuple-element.55, bf16[1,2048,1024]{2,1,0:T(8,128)(2,1)} %all-gather.13.cloned.1.call-done), kind=kOutput, calls=%fused_computation.58 | convolution fusion | flops 2155347968 | bytes 13631488 | tf_op jit(solution)/shard_map/dot_general | solution.py:1030
  213.4 4.4 convolution_convert_fusion.3
  217.8 4.3 convolution_convert_fusion.4
  222.1 4.5 convolution_convert_fusion.5
  229.0 4.0 multiply_reduce_fusion
  233.0 68.3 %shard_map.274 = (bf16[512,2048]{1,0:T(8,128)(2,1)}, f32[512,2048]{1,0:T(8,128)}, f32[256,1024]{1,0:T(8,128)}, f32[256,1024]{1,0:T(8,128)}, f32[256,1024]{1,0:T(8,128)}) custom-call(bf16[512,2048]{1,0:T(8,128)(2,1)} %get-tuple-element.144.refs_0_, f32[512,2048]{1,0:T(8,128)} %get-tuple-element.56.refs_1_.refs_9_, f32[1,2048]{1,0:T(1,128)} %get-tuple-element.133.refs_2_, ...), custom_call_target="tpu_custom_call" | custom-call | tf_op jit(solution)/shard_map/pallas_call | solution.py:360
  301.4 6.3 %convolution_convert_fusion.2 = bf16[2048,1024]{1,0:T(8,128)(2,1)} fusion(bf16[512,2048]{1,0:T(8,128)(2,1)} %get-tuple-element.57, bf16[512,1024]{1,0:T(8,128)(2,1)S(1)} %copy-done.18), kind=kOutput, calls=%fused_computation.26 | convolution fusion | flops 2149580800 | bytes 7340032 | tf_op jit(solution)/shard_map/dot_general | solution.py:20
  314.9 4.2 multiply_reduce_fusion.3
  319.0 75.7 %shard_map.275 = (f32[512,1024]{1,0:T(8,128)}, f32[512,1024]{1,0:T(8,128)}, f32[16,8,512]{2,1,0:T(8,128)}, f32[16,8,512]{2,1,0:T(8,128)}, f32[16,8,128]{2,1,0:T(...) custom-call(f32[4096,128]{1,0:T(8,128)} %copy-done, f32[4096,128]{1,0:T(8,128)} %get-tuple-element.51.refs_1_, ...), custom_call_target="tpu_custom_call" | custom-call | tf_op jit(solution)/shard_map/pallas_call | solution.py:939
  394.7 3.8 fusion.89
  403.4 12.5 %shard_map.276 = bf16[160,512]{1,0:T(8,128)(2,1)} custom-call(bf16[160,512]{1,0:T(8,128)(2,1)} %pad_maximum_fusion.5.refs_0_), custom_call_target="tpu_custom_call" | custom-call | tf_op jit(solution)/shard_map/pallas_call | solution.py:360
  417.3 6.9 %fusion.27 = (bf16[1024]{0:T(1024)(128)(2,1)S(1)}, bf16[1024]{0:T(1024)(128)(2,1)S(1)}, bf16[1024]{0:T(1024)(128)(2,1)S(1)}, bf16[1024]{0:T(1024)(128)(2,1)S(1)}, f32[512,1024]{1,0:T(8,128)S(1)}) fusion(f32[2,259,1024]{2,1,0:T(8,128)} %slice_convert_fusion, f32[512,1024]{1,0:T(8,128)S(1)} %copy-done.52, bf16[160,512]{1,0:T(8,128)(2,1)S(1)} %copy-done.19, ...), kind=kOutput, calls=%fused_computation.41 | convolution fusion | flops 178253824 | bytes 19378176 | tf_op jit(solution)/shard_map/dot_general | solution.py:20
  426.5 5.6 %convolution_convert_fusion = bf16[2048,1024]{1,0:T(8,128)(2,1)} fusion(bf16[512,2048]{1,0:T(8,128)(2,1)S(1)} %copy-done.50, bf16[512,1024]{1,0:T(8,128)(2,1)} %get-tuple-element.117), kind=kOutput, calls=%fused_computation.24 | convolution fusion | flops 2149580800 | bytes 7340032 | tf_op jit(solution)/shard_map/dot_general | solution.py:20
  432.2 6.7 %fusion.1 = f32[512,2048]{1,0:T(8,128)} fusion(bf16[512,1024]{1,0:T(8,128)(2,1)S(1)} %copy-done.56, bf16[2,2048,1024]{2,1,0:T(8,128)(2,1)} %get-tuple-element.66), kind=kOutput, calls=%fused_computation.3 | convolution fusion | flops 2147483648 | bytes 9437184 | tf_op jit(solution)/shard_map/dot_general | solution.py:24
  440.5 4.5 copy.44
  451.7 4.4 convolution_convert_fusion.1
  456.1 6.4 %multiply_reduce_fusion.1 = (bf16[2048]{0:T(1024)(128)(2,1)S(1)}, bf16[512,2048]{1,0:T(8,128)(2,1)}) fusion(f32[512]{0:T(512)S(1)} %bitcast.194, bf16[2,256,2048]{2,1,0:T(8,128)(2,1)S(1)} %copy-done.4, f32[512,2048]{1,0:T(8,128)S(1)} %copy-done.55, bf16[512,1024]{1,0:T(8,128)(2,1)S(1)} %bitcast.171, bf16[2,2048,1024]{2,1,0:T(8,128)(2,1)} %get-tuple-element.66), kind=kOutput, calls=%fused_computation.18 | convolution fusion | flops 2154821632 | bytes 13637632 | tf_op jit(solution)/shard_map/dot_general | solution.py:24
  463.9 73.0 %shard_map.277 = (bf16[512,2048]{1,0:T(8,128)(2,1)}, f32[256,1024]{1,0:T(8,128)}, f32[256,1024]{1,0:T(8,128)}, f32[48,1024]{1,0:T(8,128)}) custom-call(bf16[512,2048]{1,0:T(8,128)(2,1)} %get-tuple-element.142.refs_0_, bf16[512,2048]{1,0:T(8,128)(2,1)} %bitcast.152, f32[1,2048]{1,0:T(1,128)} %get-tuple-element.132.refs_2_, ...), custom_call_target="tpu_custom_call" | custom-call | tf_op jit(solution)/shard_map/pallas_call | solution.py:360
  (230 shorter events, 89.3 us)
Async XLA Ops:
  7.2 117.0 %all-gather.11.cloned.1.call-start = ((), (), s32[]{:S(2)}) async-start(), calls=%async_computation.1 | async-start | bytes 6291456 | tf_op jit(solution)/shard_map/all_gather | solution.py:989
  7.9 185.3 %all-gather.9.cloned.1.call-start = ((), (), s32[]{:S(2)}) async-start(), calls=%async_computation | async-start | bytes 6291456 | tf_op jit(solution)/shard_map/all_gather | solution.py:992
  8.7 191.0 %all-gather.15.cloned.1.call-start = ((), (), s32[]{:S(2)}) async-start(), calls=%async_computation.3 | async-start | bytes 6291456 | tf_op jit(solution)/shard_map/all_gather | solution.py:991
  14.7 191.5 %all-gather.13.cloned.1.call-start = ((), (), s32[]{:S(2)}) async-start(), calls=%async_computation.2 | async-start | bytes 6291456 | tf_op jit(solution)/shard_map/all_gather | solution.py:991
  17.5 6.9 %copy-start.21 = (bf16[160,512]{1,0:T(8,128)(2,1)S(1)}, bf16[160,512]{1,0:T(8,128)(2,1)}, u32[]{:S(2)}) copy-start(bf16[160,512]{1,0:T(8,128)(2,1)} %param.23) | copy-start | bytes 491524
  17.5 6.9 %copy-start.22 = (bf16[128,512]{1,0:T(8,128)(2,1)S(1)}, bf16[128,512]{1,0:T(8,128)(2,1)}, u32[]{:S(2)}) copy-start(bf16[128,512]{1,0:T(8,128)(2,1)} %param.24) | copy-start | bytes 393220
  17.5 6.9 %copy-start.31 = (bf16[16,512]{1,0:T(8,128)(2,1)S(1)}, bf16[16,512]{1,0:T(8,128)(2,1)}, u32[]{:S(2)}) copy-start(bf16[16,512]{1,0:T(8,128)(2,1)} %param.26) | copy-start | bytes 49156
  17.5 6.9 %copy-start.35 = (bf16[4,512]{1,0:T(4,128)(2,1)S(1)}, bf16[4,512]{1,0:T(4,128)(2,1)}, u32[]{:S(2)}) copy-start(bf16[4,512]{1,0:T(4,128)(2,1)} %param.21) | copy-start | bytes 12292
  25.2 40.9 %copy-start.43 = (s32[2]{0:T(128)S(1)}, s32[2]{0:T(128)}, u32[]{:S(2)}) copy-start(s32[2]{0:T(128)} %param.17) | copy-start | bytes 28
  63.2 7.0 %copy-start.14 = (bf16[544,1024]{1,0:T(8,128)(2,1)S(1)}, bf16[544,1024]{1,0:T(8,128)(2,1)}, u32[]{:S(2)}) copy-start(bf16[544,1024]{1,0:T(8,128)(2,1)} %get-tuple-element.70) | copy-start | bytes 3342340
  64.6 8.8 %copy-start.25 = (f32[1,1024]{1,0:T(1,128)}, f32[1,1024]{1,0:T(1,128)S(1)}, u32[]{:S(2)}) copy-start(f32[1,1024]{1,0:T(1,128)S(1)} %get-tuple-element.124) | copy-start | bytes 12292
  68.8 14.1 %copy-start.1 = (f32[2,8,8,128]{3,2,1,0:T(8,128)}, f32[2,8,8,128]{3,2,1,0:T(8,128)S(1)}, u32[]{:S(2)}) copy-start(f32[2,8,8,128]{3,2,1,0:T(8,128)S(1)} %copy.46) | copy-start | bytes 196612
  82.9 37.8 %copy-start.11 = (f32[512,1024]{1,0:T(8,128)S(1)}, f32[512,1024]{1,0:T(8,128)}, u32[]{:S(2)}) copy-start(f32[512,1024]{1,0:T(8,128)} %get-tuple-element.53) | copy-start | bytes 6291460
  82.9 37.8 %copy-start.32 = (f32[1,1024]{1,0:T(1,128)S(1)}, f32[1,1024]{1,0:T(1,128)}, u32[]{:S(2)}) copy-start(f32[1,1024]{1,0:T(1,128)} %get-tuple-element.123) | copy-start | bytes 12292
  206.2 7.2 %copy-start.7 = (bf16[512,2048]{1,0:T(8,128)(2,1)S(1)}, bf16[512,2048]{1,0:T(8,128)(2,1)}, u32[]{:S(2)}) copy-start(bf16[512,2048]{1,0:T(8,128)(2,1)} %fusion.refs_3_) | copy-start | bytes 6291460
  233.0 68.3 %copy-start.18 = (bf16[512,1024]{1,0:T(8,128)(2,1)S(1)}, bf16[512,1024]{1,0:T(8,128)(2,1)}, u32[]{:S(2)}) copy-start(bf16[512,1024]{1,0:T(8,128)(2,1)} %multiply_convert_fusion.5) | copy-start | bytes 3145732
  301.4 6.3 %copy-start.47 = (bf16[2048,1024]{1,0:T(8,128)(2,1)S(1)}, bf16[2048,1024]{1,0:T(8,128)(2,1)}, u32[]{:S(2)}) copy-start(bf16[2048,1024]{1,0:T(8,128)(2,1)} %all-gather.9.cloned.1.call-done) | copy-start | bytes 12582916
  301.4 6.3 %copy-start.58 = (bf16[512,1024]{1,0:T(8,128)(2,1)S(1)}, bf16[512,1024]{1,0:T(8,128)(2,1)}, u32[]{:S(2)}) copy-start(bf16[512,1024]{1,0:T(8,128)(2,1)} %copy-done.57) | copy-start | bytes 3145732
  319.0 75.7 %copy-start.26 = (f32[1,1024]{1,0:T(1,128)S(1)}, f32[1,1024]{1,0:T(1,128)}, u32[]{:S(2)}) copy-start(f32[1,1024]{1,0:T(1,128)} %copy-done.25) | copy-start | bytes 12292
  402.7 14.6 %copy-start.52 = (f32[512,1024]{1,0:T(8,128)S(1)}, f32[512,1024]{1,0:T(8,128)}, u32[]{:S(2)}) copy-start(f32[512,1024]{1,0:T(8,128)} %get-tuple-element.65) | copy-start | bytes 6291460
  424.4 25.7 %collective-permute-start = (f32[2,3,1024]{2,1,0:T(4,128)S(1)}, f32[2,3,1024]{2,1,0:T(4,128)S(1)}, u32[]{:S(2)}, u32[]{:S(2)}) collective-permute-start(f32[2,3,1024]{2,1,0:T(4,128)S(1)} %slice.264), channel_id=1, source_target_pairs={{4,0},{8,4},{12,8},{5,1},{9,5},{13,9},{6,2},{10,6},{14,10},{7,3},{... | collective-permute-start | bytes 73736 | tf_op jit(solution)/shard_map/ppermute | solution.py:1080
  432.2 6.7 %copy-start.15 = (f32[256,1024]{1,0:T(8,128)S(1)}, f32[256,1024]{1,0:T(8,128)}, u32[]{:S(2)}) copy-start(f32[256,1024]{1,0:T(8,128)} %get-tuple-element.76) | copy-start | bytes 3145732
  432.2 6.7 %copy-start.16 = (f32[256,1024]{1,0:T(8,128)S(1)}, f32[256,1024]{1,0:T(8,128)}, u32[]{:S(2)}) copy-start(f32[256,1024]{1,0:T(8,128)} %get-tuple-element.77) | copy-start | bytes 3145732
  456.1 6.5 %copy-start.24 = (f32[8,256]{1,0:T(8,128)S(1)}, f32[8,256]{1,0:T(8,128)}, u32[]{:S(2)}) copy-start(f32[8,256]{1,0:T(8,128)} %squeeze.45) | copy-start | bytes 24580
  (40 other events, 130.3 us)
Sparse Core Ops, SparseCore 0:
  9.6 16.3 all-gather.10
  27.5 14.8 all-gather.8
  43.9 14.8 all-gather.14
  60.2 14.8 all-gather.12

commit v4 on v3

--- a/solution.py
+++ b/solution.py
@@ -177,7 +177,8 @@
 
 class Halving:
     def __init__(self, arrays, step_rows=16):
-        self.step_rows = step_rows
+        steps = [step_rows] * len(arrays) if isinstance(step_rows, int) else list(step_rows)
+        self.steps = steps
         shards, pieces = lax.axis_size("shard"), lax.axis_size("ctx")
         self.n = len(arrays)
         self.bits = [
@@ -189,8 +190,10 @@
         head = shards.bit_length() - 1
         self.dims = list(range(self.depth))
         self.orders = (self.dims, self.dims[:head] + self.dims[head:][::-1])
-        self.parts = [g.shape[0] // (shards * pieces) // step_rows for g in arrays]
-        self.folded = [g.reshape((2,) * self.depth + (p * step_rows, g.shape[1])) for g, p in zip(arrays, self.parts)]
+        self.parts = [g.shape[0] // (shards * pieces) // k for g, k in zip(arrays, steps)]
+        self.folded = [
+            g.reshape((2,) * self.depth + (p * k, g.shape[1])) for g, p, k in zip(arrays, self.parts, steps)
+        ]
         self.tails = [g.shape[self.depth :] for g in self.folded]
         self.pairs = (max(self.parts, default=0) + 1) // 2
         self.turns = self.pairs + share_lag * (self.depth - 1)
@@ -225,11 +228,11 @@
             pl.semaphore_signal(barrier, inc=1, device_id=who, device_id_type=MESH)
         return len(self.partner)
 
-    def spot(self, c):
-        return pl.ds(pl.multiple_of(c * self.step_rows, self.step_rows), self.step_rows)
-
-    def pick(self, remaining, dim, index, c):
-        return tuple(index if d == dim else slice(None) for d in remaining) + (self.spot(c), slice(None))
+    def spot(self, a, c):
+        return pl.ds(pl.multiple_of(c * self.steps[a], self.steps[a]), self.steps[a])
+
+    def pick(self, remaining, dim, index, a, c):
+        return tuple(index if d == dim else slice(None) for d in remaining) + (self.spot(a, c), slice(None))
 
     def rest(self, order, j):
         return [d for d in self.dims if d not in order[:j]]
@@ -238,8 +241,8 @@
         source = self.full[a] if j == 0 else self.landed[j - 1][a]
         d = order[j]
         return pltpu.make_async_remote_copy(
-            source.at[self.pick(self.rest(order, j), d, 1 - self.mine[d], c)],
-            self.landed[j][a].at[self.pick(self.rest(order, j + 1), None, None, c)],
+            source.at[self.pick(self.rest(order, j), d, 1 - self.mine[d], a, c)],
+            self.landed[j][a].at[self.pick(self.rest(order, j + 1), None, None, a, c)],
             self.send.at[j, a, c],
             self.recv.at[j, a, c],
             device_id=self.partner[d],
@@ -248,8 +251,8 @@
 
     def own_copy(self, a, c, order):
         return pltpu.make_async_copy(
-            self.full[a].at[self.pick(self.dims, order[0], self.mine[order[0]], c)],
-            self.own[a].at[self.pick(self.rest(order, 1), None, None, c)],
+            self.full[a].at[self.pick(self.dims, order[0], self.mine[order[0]], a, c)],
+            self.own[a].at[self.pick(self.rest(order, 1), None, None, a, c)],
             self.own_sem.at[a, c],
         )
 
@@ -259,16 +262,16 @@
 
     def step(self, j, a, c, order):
         self.copy(j, a, c, order).wait_recv()
-        where = self.pick(self.rest(order, j + 1), None, None, c)
+        where = self.pick(self.rest(order, j + 1), None, None, a, c)
         d = order[j]
         if j == 0:
             self.own_copy(a, c, order).wait()
             kept = self.own[a][where]
         else:
-            kept = self.landed[j - 1][a][self.pick(self.rest(order, j), d, self.mine[d], c)]
+            kept = self.landed[j - 1][a][self.pick(self.rest(order, j), d, self.mine[d], a, c)]
         total = kept.astype(f32) + self.landed[j][a][where].astype(f32)
         if j == self.depth - 1:
-            self.shares[a][self.spot(c), :] = total
+            self.shares[a][self.spot(a, c), :] = total
         else:
             self.landed[j][a][where] = total.astype(bf16)
             self.copy(j + 1, a, c, order).start()
@@ -302,9 +305,9 @@
             lax.fori_loop(0, self.pairs, sent, 0)
 
 
-def tp_sum(partial, epilogue, extras, extra_outs, chunk, ident, out_dtype=bf16, scatters=(), line_too=False):
+def tp_sum(partial, epilogue, extras, extra_outs, chunk, ident, out_dtype=bf16, scatters=(), line_too=False, steps=16):
     line = Line(partial.shape, chunk, epilogue, extras, out_dtype)
-    share = Halving(scatters)
+    share = Halving(scatters, steps)
     n_ex, n_out, n_sc = len(extras), len(extra_outs), len(scatters)
     n_line, n_share = len(line.scratch()), len(share.scratch())
 
@@ -646,27 +649,56 @@
     return result
 
 
-def scan_forward(size, act, b_row, c_row, rate, seqs, ident):
-    rows, channels = size.shape
+def spread_rows(low_ref, first, out_ref):
+    states, slots = 16, low_ref.shape[1]
+
+    def lanes(k, _):
+        block = low_ref[first : first + states, pl.ds(pl.multiple_of(k * 128, 128), 128)]
+        for i in range(128):
+            to = pl.ds(pl.multiple_of((k * 128 + i) * states, states), states)
+            out_ref[to, :] = jnp.broadcast_to(block[:, i : i + 1], (states, 128))
+        return 0
+
+    lax.fori_loop(0, slots // 128, lanes, 0)
+
+
+def scan_forward(low_all, act, gate_z, small, rate, out_parts, seqs, rank, at_step, at_bias, at_skip, ident):
+    rows, channels = act.shape
+    shards, _, part = out_parts.shape
     local = rows // seqs
     states = rate.shape[0]
     width = lax.axis_size("ctx")
     pieces = local // piece
 
     def kernel(
-        size_ref, act_ref, b_ref, c_ref, rate_ref, y_ref, kept_ref, enter_ref, size3, drive3,
-        y3, ends, got, held, send, recv, out_sem,
+        low_ref, act_ref, z_ref, small_ref, rate_ref, w_ref,
+        scan_ref, gated_ref, mixed_ref, pre_ref, kept_ref, enter_ref, size3, drive3,
+        y3, ends, got, held, b_ref, c_ref, low_t, w_own, send, recv, out_sem, w_sem,
     ):
-        pl.semaphore_wait(ctx_greet(width), width - 1)
+        barrier = ctx_greet(width)
+        load = pltpu.make_async_copy(w_ref, w_own, w_sem)
+        load.start()
+        low_t[...] = low_ref[0:rank, :].T.astype(bf16)
+        bias = small_ref[at_bias : at_bias + 16, :].astype(f32)[0:1]
+        for j in range(channels // 256):
+            here = slice(j * 256, (j + 1) * 256)
+            value = jnp.dot(low_t[...], small_ref[at_step : at_step + rank, here], preferred_element_type=f32)
+            pre_ref[:, here] = value + bias[:, here]
+        spread_rows(low_ref, rank, b_ref)
+        spread_rows(low_ref, rank + states, c_ref)
 
         def lay(i, _):
-            first = pl.multiple_of(i * 8, 8)
-            block = size_ref[pl.ds(first, 8), :]
-            spread(size3, block, first)
-            spread(drive3, block * act_ref[pl.ds(first, 8), :], first)
+            first = pl.multiple_of(i * 16, 16)
+            act_block = act_ref[pl.ds(first, 16), :].astype(f32)
+            size = jax.nn.softplus(pre_ref[pl.ds(first, 16), :])
+            drive = size * act_block
+            for h in range(2):
+                spread(size3, size[h * 8 : h * 8 + 8], first + h * 8)
+                spread(drive3, drive[h * 8 : h * 8 + 8], first + h * 8)
             return 0
 
-        lax.fori_loop(0, rows // 8, lay, 0)
+        lax.fori_loop(0, rows // 16, lay, 0)
+        pl.semaphore_wait(barrier, width - 1)
         copies = []
         for seq in range(seqs):
 
@@ -729,38 +761,58 @@
             for k in (pieces - 2, pieces - 1):
                 save(k, k % 2).wait()
 
+        skip = small_ref[at_skip : at_skip + 16, :].astype(f32)[0:1]
+
         def back(i, _):
-            first = pl.multiple_of(i * 8, 8)
-            y_ref[pl.ds(first, 8), :] = unspread(y3, first)
+            first = pl.multiple_of(i * 16, 16)
+            here = pl.ds(first, 16)
+            value = jnp.concatenate([unspread(y3, first), unspread(y3, first + 8)], axis=0)
+            value = value + skip * act_ref[here, :].astype(f32)
+            scan_ref[here, :] = value
+            gated_ref[here, :] = (value * jax.nn.silu(z_ref[here, :])).astype(bf16)
             return 0
 
-        lax.fori_loop(0, rows // 8, back, 0)
+        lax.fori_loop(0, rows // 16, back, 0)
+        load.wait()
+        for k in range(shards):
+            for j in range(-(-part // 256)):
+                span = min(256, part)
+                value = jnp.dot(gated_ref[...], w_own[k, :, j * span : (j + 1) * span], preferred_element_type=f32)
+                mixed_ref[:, k * part + j * span : k * part + (j + 1) * span] = value.astype(bf16)
 
     flat = jax.ShapeDtypeStruct((rows * 8, 128), f32)
     return pl.pallas_call(
         kernel,
         out_shape=[
+            jax.ShapeDtypeStruct((rows, channels), f32),
+            jax.ShapeDtypeStruct((rows, channels), bf16),
+            jax.ShapeDtypeStruct((rows, shards * part), bf16),
             jax.ShapeDtypeStruct((rows, channels), f32),
             jax.ShapeDtypeStruct((rows, states, 8, 128), f32),
             jax.ShapeDtypeStruct((seqs, states, 8, 128), f32),
             flat,
             flat,
         ],
-        in_specs=[VMEM] * 5,
-        out_specs=[VMEM, HBM, VMEM, VMEM, VMEM],
+        in_specs=[VMEM] * 5 + [HBM],
+        out_specs=[VMEM] * 4 + [HBM, VMEM, VMEM, VMEM],
         scratch_shapes=[
             pltpu.VMEM((rows * 8, 128), f32),
             pltpu.VMEM((seqs, states + 1, 8, 128), f32),
             pltpu.VMEM((width, seqs, states + 1, 8, 128), f32),
             pltpu.VMEM((2, piece, states, 8, 128), f32),
+            pltpu.VMEM((rows * states, 128), f32),
+            pltpu.VMEM((rows * states, 128), f32),
+            pltpu.VMEM((rows, rank), bf16),
+            pltpu.VMEM(out_parts.shape, bf16),
             pltpu.SemaphoreType.DMA((seqs, width)),
             pltpu.SemaphoreType.DMA((seqs, width)),
             pltpu.SemaphoreType.DMA((2,)),
+            pltpu.SemaphoreType.DMA,
         ],
         compiler_params=pltpu.CompilerParams(
             collective_id=ident, has_side_effects=True, vmem_limit_bytes=48 << 20
         ),
-    )(size, act, b_row, c_row, rate)
+    )(low_all, act, gate_z, small, rate, out_parts)
 
 
 def sublane_sums(parts):
@@ -777,7 +829,7 @@
     return parts[0]
 
 
-def scan_backward(size3, drive3, grad, b_row, c_row, rate, kept, enter, seqs, ident, partial, epilogue, extras, chunk, scatters):
+def scan_backward(size3, drive3, grad, low_all, rank, rate, kept, enter, seqs, ident, partial, epilogue, extras, chunk, scatters):
     rows, channels = grad.shape
     local = rows // seqs
     states = rate.shape[0]
@@ -797,16 +849,18 @@
             del refs[:n]
             return taken
 
-        size_ref, drive_ref, grad_ref, b_ref, c_ref, rate_ref, kept_ref, enter_ref, p_ref = take_refs(9)
+        size_ref, drive_ref, grad_ref, low_ref, rate_ref, kept_ref, enter_ref, p_ref = take_refs(8)
         ins, full = take_refs(n_ex), take_refs(n_sc)
         tb_ref, sd_ref, bg_ref, cg_ref, dec_ref, sum_ref = take_refs(6)
         shares = take_refs(n_sc)
-        grad3, tb3, sd3, ends, got, held, bpart, cpart, prior, send, recv, in_sem = take_refs(12)
+        grad3, tb3, sd3, b_ref, c_ref, ends, got, held, bpart, cpart, prior, send, recv, in_sem = take_refs(14)
         line.bind(p_ref, ins, sum_ref, [], take_refs(n_line))
         share.bind(full, shares, refs)
         barrier = ctx_greet(width)
         line.begin(barrier, width - 1 + share.greet(barrier))
         share.start()
+        spread_rows(low_ref, rank, b_ref)
+        spread_rows(low_ref, rank + states, c_ref)
 
         def lay(i, _):
             first = pl.multiple_of(i * 8, 8)
@@ -940,9 +994,10 @@
         kernel,
         out_shape=[nat, nat, sums, sums, jax.ShapeDtypeStruct((states, 8, 128), f32),
                    jax.ShapeDtypeStruct(partial.shape, bf16)] + share.results(),
-        in_specs=[VMEM] * 6 + [HBM, VMEM] + [HBM] * (1 + n_ex + n_sc),
+        in_specs=[VMEM] * 5 + [HBM, VMEM] + [HBM] * (1 + n_ex + n_sc),
         out_specs=[VMEM] * (6 + n_sc),
         scratch_shapes=[pltpu.VMEM((rows * 8, 128), f32)] * 3
+        + [pltpu.VMEM((rows * states, 128), f32)] * 2
         + [
             pltpu.VMEM((seqs, states + 1, 8, 128), f32),
             pltpu.VMEM((width, seqs, states + 1, 8, 128), f32),
@@ -959,7 +1014,164 @@
         compiler_params=pltpu.CompilerParams(
             collective_id=ident, has_side_effects=True, vmem_limit_bytes=62 << 20
         ),
-    )(size3, drive3, grad, b_row, c_row, rate, kept, enter, partial, *extras, *share.folded)
+    )(size3, drive3, grad, low_all, rate, kept, enter, partial, *extras, *share.folded)
+
+
+def scan_tail(through_b, through_decay, sums, decay_grad, scan_grad, step_pre, pre_act, act, padded, low_all, small, ident,
+              seqs, low_len, rank, states, taps):
+    rows, inner = act.shape
+    local = rows // seqs
+    long = local + halo
+    shards, pieces = lax.axis_size("shard"), lax.axis_size("ctx")
+    places = shards * pieces
+    lane = inner // places
+    line = Line((low_len, rows), 80, plain_end, [], bf16)
+    tiles = inner // tile_cols
+    at = low_len + rank
+    lines = -(-(at + states + taps + 3) // 8) * 8
+    height = -(-(lines + 8) // 32) * 32
+    over = 8
+
+    def kernel(
+        tb_ref, sd_ref, sums_ref, dec_ref, sg_ref, sp_ref, pre_ref, act_ref, ext_ref, low_ref, small_ref,
+        conv_ref, blocks_ref,
+        low_out, low_t, step_g, low_acc, grads, pre_g, conv_f, edge, edge_out, edge_sem, *rest
+    ):
+        ctx = lax.axis_index("ctx")
+        barrier = pltpu.get_barrier_semaphore()
+        line.bind(rest[0], [], low_out, [], list(rest))
+        pl.semaphore_signal(barrier, inc=1, device_id={"ctx": lax.rem(ctx + 1, pieces)}, device_id_type=MESH)
+
+        def cols(j):
+            return pl.ds(pl.multiple_of(j * tile_cols, tile_cols), tile_cols)
+
+        low_acc[...] = jnp.zeros_like(low_acc)
+        grads[...] = jnp.zeros_like(grads)
+        low_t[...] = low_ref[0:rank, :].astype(bf16)
+
+        def size_tile(j, _):
+            here = cols(j)
+            bias_grad = jnp.zeros((8, tile_cols), f32)
+            skip_grad = jnp.zeros((8, tile_cols), f32)
+            for k in range(rows // 64):
+                to = slice(k * 64, (k + 1) * 64)
+                act_block = act_ref[to, here].astype(f32)
+                size_grad = act_block * tb_ref[to, here] + sd_ref[to, here] * (1.0 / log2e)
+                value = (size_grad * jax.nn.sigmoid(sp_ref[to, here])).astype(bf16)
+                step_g[to, here] = value
+                wide = value.astype(f32)
+                product = sg_ref[to, here] * act_block
+                for h in range(8):
+                    bias_grad = bias_grad + wide[h * 8 : h * 8 + 8]
+                    skip_grad = skip_grad + product[h * 8 : h * 8 + 8]
+            grads[at + states + taps + 1 : at + states + taps + 2, here] = jnp.sum(bias_grad, axis=0, keepdims=True)
+            grads[at + states + taps + 2 : at + states + taps + 3, here] = jnp.sum(skip_grad, axis=0, keepdims=True)
+            low_acc[...] = low_acc[...] + outer_cols(small_ref[low_len : low_len + rank, here], step_g[:, here])
+            return 0
+
+        lax.fori_loop(0, tiles, size_tile, 0)
+        line.p[0:rank, :] = low_acc[...].astype(bf16)
+        line.p[rank : rank + 2 * states, :] = sums_ref[...].astype(bf16)
+        line.greet(barrier, 1)
+        line.start()
+
+        def step_tile(j, _):
+            here = cols(j)
+            grads[low_len:at, here] = jnp.dot(low_t[...], step_g[:, here], preferred_element_type=f32)
+            return 0
+
+        lax.fori_loop(0, tiles, step_tile, 0)
+        grads[at : at + states, :] = dec_ref[...]
+        for c in range(line.ticks()):
+            line.tick(c)
+        line.finish()
+
+        def pre_tile(j, _):
+            here = cols(j)
+            grads[0:low_len, here] = jnp.dot(low_out[...], act_ref[:, here], preferred_element_type=f32)
+            for seq in range(seqs):
+                low = inner_rows(low_out[:, seq * local : (seq + 1) * local], small_ref[0:low_len, here])
+                conv_f[seq * long : (seq + 1) * long, :] = ext_ref[seq * long : (seq + 1) * long, here].astype(f32)
+                pre_g[seq * (local + over) : seq * (local + over) + local, here] = low
+            skip = small_ref[at + states + 32 : at + states + 48, here].astype(f32)[0:1]
+            bias_sum = jnp.zeros((8, tile_cols), f32)
+            tap_sums = [jnp.zeros((8, tile_cols), f32) for _ in range(taps)]
+            for seq in range(seqs):
+                for k in range(local // 64):
+                    to = slice(seq * local + k * 64, seq * local + (k + 1) * 64)
+                    where = slice(seq * (local + over) + k * 64, seq * (local + over) + (k + 1) * 64)
+                    act_grad = skip * sg_ref[to, here] + jax.nn.softplus(sp_ref[to, here]) * tb_ref[to, here]
+                    value = (act_grad + pre_g[where, here]) * silu_grad(pre_ref[to, here])
+                    pre_g[where, here] = value
+                    first = seq * long + halo + k * 64 - taps + 1
+                    products = [value * conv_f[first + tap : first + tap + 64, :] for tap in range(taps)]
+                    for h in range(8):
+                        bias_sum = bias_sum + value[h * 8 : h * 8 + 8]
+                        for tap in range(taps):
+                            tap_sums[tap] = tap_sums[tap] + products[tap][h * 8 : h * 8 + 8]
+            for tap in range(taps):
+                row = at + states + tap
+                grads[row : row + 1, here] = jnp.sum(tap_sums[tap], axis=0, keepdims=True)
+            row = at + states + taps
+            grads[row : row + 1, here] = jnp.sum(bias_sum, axis=0, keepdims=True)
+            return 0
+
+        lax.fori_loop(0, tiles, pre_tile, 0)
+        for seq in range(seqs):
+            edge_out[seq] = pre_g[seq * (local + over) : seq * (local + over) + over, :]
+        copy = pltpu.make_async_remote_copy(
+            edge_out, edge, edge_sem.at[0], edge_sem.at[1],
+            device_id={"ctx": lax.rem(ctx + pieces - 1, pieces)}, device_id_type=MESH,
+        )
+        copy.start()
+        for p in range(places):
+            blocks_ref[p * height : p * height + lines, :] = grads[:, p * lane : (p + 1) * lane].astype(bf16)
+            blocks_ref[p * height + lines : (p + 1) * height, :] = jnp.zeros((height - lines, lane), bf16)
+        copy.wait()
+        inside = (ctx < pieces - 1).astype(f32)
+        for seq in range(seqs):
+            first = seq * (local + over) + local
+            pre_g[first : first + over, :] = edge[seq] * inside
+
+        def conv_tile(j, _):
+            here = cols(j)
+            weights = small_ref[at + states : at + states + 16, here].astype(f32)
+            for seq in range(seqs):
+                for k in range(local // 64):
+                    first = seq * (local + over) + k * 64 + taps - 1
+                    total = weights[0:1] * pre_g[first : first + 64, here]
+                    for tap in range(1, taps):
+                        total = total + weights[tap : tap + 1] * pre_g[first - tap : first - tap + 64, here]
+                    conv_ref[seq * local + k * 64 : seq * local + (k + 1) * 64, here] = total.astype(bf16)
+            return 0
+
+        lax.fori_loop(0, tiles, conv_tile, 0)
+
+    return pl.pallas_call(
+        kernel,
+        out_shape=[
+            jax.ShapeDtypeStruct((rows, inner), bf16),
+            jax.ShapeDtypeStruct((places * height, lane), bf16),
+        ],
+        in_specs=[VMEM] * 11,
+        out_specs=[VMEM] * 2,
+        scratch_shapes=[
+            pltpu.VMEM((low_len, rows), bf16),
+            pltpu.VMEM((rank, rows), bf16),
+            pltpu.VMEM((rows, inner), bf16),
+            pltpu.VMEM((rank, rows), f32),
+            pltpu.VMEM((lines, inner), f32),
+            pltpu.VMEM((seqs * (local + over), inner), f32),
+            pltpu.VMEM((seqs * long, tile_cols), f32),
+            pltpu.VMEM((seqs, over, inner), f32),
+            pltpu.VMEM((seqs, over, inner), f32),
+            pltpu.SemaphoreType.DMA((2,)),
+        ]
+        + line.scratch(),
+        compiler_params=pltpu.CompilerParams(
+            collective_id=ident, has_side_effects=True, vmem_limit_bytes=56 << 20
+        ),
+    )(through_b, through_decay, sums, decay_grad, scan_grad, step_pre, pre_act, act, padded, low_all, small), height
 
 
 def body(
@@ -975,9 +1187,15 @@
     states = decay_log.shape[0]
     low_len = low_weight.shape[0]
 
+    def rows16(v):
+        return jnp.pad(v, ((0, 16 - v.shape[0]), (0, 0)))
+
     small = jnp.concatenate(
-        [low_weight, step_weight, decay_log, conv_weight, conv_bias[None], step_bias[None], skip_gain[None]], axis=0
+        [low_weight, step_weight, decay_log, rows16(jnp.concatenate([conv_weight, conv_bias[None]], axis=0)),
+         rows16(step_bias[None]), rows16(skip_gain[None])], axis=0,
     )
+    at_bias = low_len + rank + states + 16
+    at_skip = at_bias + 16
     hidden_rows = hidden_in.reshape(rows, width)
     small = jnp.pad(small, ((0, -small.shape[0] % 16), (0, 0)))
     gains = jnp.stack([norm_gain, ffn_gain])
@@ -997,9 +1215,7 @@
     at = low_len + rank
     decay_w = small[at : at + states].astype(f32)
     kernel = small[at + states : at + states + taps].astype(f32)
-    conv_b = small[at + states + taps].astype(f32)
-    step_b = small[at + states + taps + 1].astype(f32)
-    skip_full = small[at + states + taps + 2].astype(f32)
+    skip_full = small[at_skip].astype(f32)
     gain_one, gain_two = gains[0:1].astype(f32), gains[1:2].astype(f32)
 
     first_slot = lax.axis_index("ctx") * local
@@ -1007,24 +1223,15 @@
     pad_mask = (positions[None, :] < lengths[:, None]).astype(f32)
 
     source = hidden_rows.astype(f32)
-    padded = padded.reshape(seqs, halo + local, inner)[:, halo - taps + 1 :].astype(f32)
     act_full = act_half.astype(f32)
     step_low = low_all[:rank].astype(bf16)
-    b_in, c_out = low_all[rank : rank + states], low_all[rank + states :]
-    b_row, c_row = (
-        jnp.broadcast_to(v.T[:, :, None], (rows, states, 128)).reshape(rows * states, 128) for v in (b_in, c_out)
-    )
-    step_pre = inner_rows(step_low, step_w) + step_b
-    step_size = jax.nn.softplus(step_pre)
     decay_rate = -jnp.exp(decay_w)
     rate = (decay_rate * log2e).reshape(states, 8, 128)
-    scan_y, kept, enter, size3, drive3 = scan_forward(step_size, act_full, b_row, c_row, rate, seqs, 2)
-    scan_out = scan_y + skip_full * act_full
+    scan_out, gated_out, mixed_part, step_pre, kept, enter, size3, drive3 = scan_forward(
+        low_all, act_half, gate_z, small, rate, out_parts, seqs, rank, low_len, at_bias, at_skip, 2
+    )
+    step_size = jax.nn.softplus(step_pre)
     gate_act = jax.nn.silu(gate_z)
-    gated_out = (scan_out * gate_act).astype(bf16)
-    mixed_part = jnp.concatenate(
-        [jnp.dot(gated_out, out_parts[k], preferred_element_type=f32) for k in range(shards)], axis=1
-    ).astype(bf16)
     wide = jax.ShapeDtypeStruct((rows, width), f32)
     normed_two, middle = tp_sum(mixed_part, norm_end, [hidden_rows, gain_two], [wide], 32, 3)
     gate_lin, up_lin = (jnp.dot(normed_two, gate_w[c], preferred_element_type=f32) for c in range(2))
@@ -1050,65 +1257,36 @@
     gated_grad = sum(outer_cols(mix_grad[:, k * part : (k + 1) * part], out_parts[k]) for k in range(shards))
     scan_grad = gated_grad * gate_act
     z_grad = gated_grad * scan_out * silu_grad(gate_z)
-    skip_gain_grad = jnp.sum(scan_grad * act_full, axis=0)
     through_b, through_decay, b_sums, c_sums, decay_sum, mixed_out, out_share = scan_backward(
-        size3, drive3, scan_grad, b_row, c_row, rate, kept, enter, seqs, 6, ffn_part, add_end, [middle], 32,
+        size3, drive3, scan_grad, low_all, rank, rate, kept, enter, seqs, 6, ffn_part, add_end, [middle], 32,
         [out_weight_grad],
     )
     mixed_out = mixed_out.reshape(hidden_in.shape)
     decay_log_grad = decay_sum.reshape(states, inner) * decay_rate
-    size_grad = act_full * through_b + through_decay * (1.0 / log2e)
-    step_grad = (size_grad * jax.nn.sigmoid(step_pre)).astype(bf16)
-    step_bias_grad = jnp.sum(step_grad.astype(f32), axis=0)
-    step_weight_grad = jnp.dot(step_low, step_grad, preferred_element_type=f32)
-    low_back = jnp.concatenate(
-        [
-            outer_cols(step_w, step_grad),
-            b_sums[:, 0].reshape(rows, states).T,
-            c_sums[:, 0].reshape(rows, states).T,
-        ],
-        axis=0,
-    ).astype(bf16)
-    low_grad = tp_sum(low_back, plain_end, [], [], 80, 7)[0]
-    low_weight_grad = jnp.dot(low_grad, act_half, preferred_element_type=f32)
-    act_grad = skip_full * scan_grad + step_size * through_b + inner_rows(low_grad, low_w)
-    pre_grad = (act_grad * silu_grad(pre_act)).reshape(seqs, local, inner)
-    conv_bias_grad = jnp.sum(pre_grad, axis=(0, 1))
-    conv_weight_grad = jnp.stack(
-        [jnp.sum(pre_grad * padded[:, k : k + local], axis=(0, 1)) for k in range(taps)]
+    sums = jnp.concatenate([v[:, 0].reshape(rows, states).T for v in (b_sums, c_sums)], axis=0)
+    (conv_grad, small_blocks), small_height = scan_tail(
+        through_b, through_decay, sums, decay_log_grad, scan_grad, step_pre, pre_act, act_half, padded, low_all, small, 7,
+        seqs, low_len, rank, states, taps,
     )
-    behind = lax.ppermute(pre_grad[:, : taps - 1], "ctx", [(k + 1, k) for k in range(pieces - 1)])
-    pre_long = jnp.concatenate([pre_grad, behind], axis=1)
-    conv_grad = sum(kernel[k] * pre_long[:, taps - 1 - k : taps - 1 - k + local] for k in range(taps))
-    conv_grad = conv_grad.reshape(rows, inner).astype(bf16)
     z_half = z_grad.astype(bf16)
     in_weight_grad = [inner_rows(normed_one, g).astype(bf16) for g in (conv_grad, z_half)]
     first_part = (outer_cols(conv_grad, in_w[0]) + outer_cols(z_half, in_w[1])).astype(bf16)
     norm_gain_grad = jnp.sum(first_part.astype(f32) * source * rms_scale(source), axis=0)
-    small_grads = jnp.concatenate(
-        [low_weight_grad, step_weight_grad, decay_log_grad, conv_weight_grad, conv_bias_grad[None],
-         step_bias_grad[None], skip_gain_grad[None]], axis=0,
+    places, share = shards * pieces, width // (shards * pieces)
+    lane = inner // places
+    gain_rows = -(-2 * share // lane)
+    gain_blocks = jnp.concatenate([norm_gain_grad.reshape(places, share), ffn_gain_grad.reshape(places, share)], axis=1)
+    gain_blocks = jnp.pad(gain_blocks, ((0, 0), (0, gain_rows * lane - 2 * share))).reshape(places, gain_rows, lane)
+    gain_height = 16 * -(-gain_rows // 16)
+    gain_blocks = jnp.pad(gain_blocks, ((0, 0), (gain_height - gain_rows, 0), (0, 0)))
+    gain_blocks = gain_blocks.reshape(places * gain_height, lane).astype(bf16)
+    input_grad, in_share, z_share, small_out, gain_share = tp_sum(
+        first_part, norm_back_end, [hidden_rows, gain_one, middle_grad], [], 32, 8,
+        scatters=in_weight_grad + [small_blocks, gain_blocks], line_too=True,
+        steps=[16, 16, small_height // 2, gain_height],
     )
-    places = shards * pieces
-    lines, lane, share = small_grads.shape[0], inner // places, width // places
-    small_rows = -(-(lines * lane) // (16 * inner)) * 16
-    if small_rows * inner - lines * lane < 8 * inner:
-        small_rows += 16
-    small_blocks = small_grads.reshape(lines, places, lane).transpose(1, 0, 2).reshape(places, lines * lane)
-    gain_blocks = jnp.concatenate([norm_gain_grad.reshape(places, share), ffn_gain_grad.reshape(places, share)], axis=1)
-    fill = (small_rows - 8) * inner - lines * lane
-    small_blocks = jnp.concatenate(
-        [small_blocks, jnp.zeros((places, fill), f32), gain_blocks, jnp.zeros((places, 8 * inner - 2 * share), f32)],
-        axis=1,
-    )
-    small_blocks = small_blocks.reshape(places * small_rows, inner).astype(bf16)
-    input_grad, in_share, z_share, small_share = tp_sum(
-        first_part, norm_back_end, [hidden_rows, gain_one, middle_grad], [], 32, 8,
-        scatters=in_weight_grad + [small_blocks], line_too=True,
-    )
-    gain_share = small_share[small_rows - 8]
+    gain_share = gain_share[gain_height - gain_rows :].reshape(-1)
     input_grad = input_grad.astype(f32).reshape(hidden_in.shape)
-    small_out = small_share.reshape(-1)[: lines * lane].reshape(lines, lane)
     at = low_len + rank
     return (
         mixed_out,

time: 567 us -> 530 us (0.935)
  matrix products: 95.4 us -> 69.4 us
  Pallas kernels: 366 us -> 384 us
  other arithmetic: 28.3 us -> 12.5 us
  local copies, waits for them, and re-layouts: 51.8 us -> 38.9 us
    pallas_call x0 -> x1, Pallas kernels: none -> 27.5 us  [scan_tail(): pl.pallas_call(kernel, out_shape=[jax.ShapeDtypeStruct((rows, inner), bf1...]
    pallas_call x4 -> x3, Pallas kernels: 217 us -> 203 us  [tp_sum(): pl.pallas_call(kernel, out_shape=[jax.ShapeDtypeStruct(partial.shape, out...]
    dot_general x8 -> x6, matrix products: 40.7 us -> 29.9 us  [inner_rows(): lax.dot_general(left, right, (((0,), (0,)), ((), ())), preferred_element_...]
    dot_general x9 -> x8, matrix products: 32.4 us -> 23.3 us  [outer_cols(): lax.dot_general(left, right, (((1,), (1,)), ((), ())), preferred_element_...]
    convert_element_type x5 -> x0, other arithmetic: 6.57 us -> none  [the longest x1 1.67 us: body(): padded.reshape(seqs, halo + local, inner)[:, halo - taps + 1:].astype(f32)]
    dot_general x4 -> x0, matrix products: 6.2 us -> none  [the longest x2 4.57 us: body(): jnp.dot(gated_out, out_parts[k], preferred_element_type=f32)]
    unnamed x145 -> x100, local copies, waits for them, and re-layouts: 30.5 us -> 25.9 us
  transfers between devices with their start and end apart: 5 -> 4, of which waited for: 0 -> 0; matrix products, arithmetic and copies ran while one was open for 15% -> 6% of each run, Pallas kernels for 24% -> 27%
where the time goes in v4:
time: 530 us; the launch traced here: 522 us
  Pallas kernels  384 us (72%)
  matrix products  69.4 us (13%)
  local copies, waits for them, and re-layouts  38.9 us (7%)
  between operations  14.8 us (3%)
  other arithmetic  12.5 us (2%)
    pallas_call x3, Pallas kernels, tp_sum(): pl.pallas_call(kernel, out_shape=[jax.ShapeDtypeStruct(partial.shape, out...  203 us
    pallas_call x1, Pallas kernels, scan_backward(): pl.pallas_call(kernel, out_shape=[nat, nat, sums, sums, jax.ShapeDtypeStr...  75.1 us
    pallas_call x1, Pallas kernels, scan_forward(): pl.pallas_call(kernel, out_shape=[jax.ShapeDtypeStruct((rows, channels),...  40.9 us
    pallas_call x1, Pallas kernels, front(): pl.pallas_call(kernel, out_shape=[sds((2, shards * part, inner), bf16), s...  37.8 us
    dot_general x6, matrix products, inner_rows(): lax.dot_general(left, right, (((0,), (0,)), ((), ())), preferred_element_...  29.9 us
    pallas_call x1, Pallas kernels, scan_tail(): pl.pallas_call(kernel, out_shape=[jax.ShapeDtypeStruct((rows, inner), bf1...  27.5 us
    unnamed x100, local copies, waits for them, and re-layouts  25.9 us
    dot_general x8, matrix products, outer_cols(): lax.dot_general(left, right, (((1,), (1,)), ((), ())), preferred_element_...  23.3 us
  transfers between devices with their start and end apart: 4, of which 0 were waited for; matrix products, arithmetic and copies ran while one was open for 6% of the time, Pallas kernels for 27%

profile of v4, /device:TPU:0, one launch (start us, length us, event | category | flops | bytes accessed | tf_op | source)
XLA Modules:
  0.0 522.1 jit_solution(10232290821840661488)
XLA Ops:
  8.7 3.5 copy.51
  17.6 6.2 %copy.52 = bf16[1024,2,1024]{2,0,1:T(8,128)(2,1)} copy(bf16[1024,2,1024]{2,1,0:T(2,128)(2,1)} %param.20) | data formatting | bytes 8388608 | tf_op args[4]
  24.7 37.8 %shard_map.271 = (bf16[2,2048,1024]{2,1,0:T(8,128)(2,1)}, bf16[352,1024]{1,0:T(8,128)(2,1)}, bf16[16,2048]{1,0:T(8,128)(2,1)}, bf16[512,2048]{1,0:T(8,128)(2,1)}...) custom-call(bf16[512,2048]{1,0:T(8,128)(2,1)} %bitcast.104, ...), custom_call_target="tpu_custom_call" | custom-call | tf_op jit(solution)/shard_map/pallas_call | solution.py:550
  66.6 40.9 %shard_map.272 = (f32[512,1024]{1,0:T(8,128)S(1)}, bf16[512,1024]{1,0:T(8,128)(2,1)S(1)}, bf16[512,2048]{1,0:T(8,128)(2,1)}, f32[512,1024]{1,0:T(8,128)}, f32[51...) custom-call(f32[160,512]{1,0:T(8,128)S(1)} %copy-done.2, ...), custom_call_target="tpu_custom_call" | custom-call | tf_op jit(solution)/shard_map/pallas_call | solution.py:784
  108.9 62.1 %shard_map.273 = (bf16[512,2048]{1,0:T(8,128)(2,1)}, f32[512,2048]{1,0:T(8,128)}) custom-call(bf16[512,2048]{1,0:T(8,128)(2,1)} %get-tuple-element.59.refs_0_, bf16[512,2048]{1,0:T(8,128)(2,1)} %bitcast.105, f32[1,2048]{1,0:T(1,128)} %get-tuple-element.132.refs_2_), custom_call_target="tpu_custom_call" | custom-call | tf_op jit(solution)/shard_map/pallas_call | solution.py:363
  171.0 3.3 fusion.24
  174.7 2.6 fusion.32
  177.4 6.5 %fusion.7 = f32[512,1024]{1,0:T(8,128)} fusion(bf16[512,2048]{1,0:T(8,128)(2,1)} %get-tuple-element.61, bf16[1,2048,1024]{2,1,0:T(8,128)(2,1)} %all-gather.15.cloned.1.call-done), kind=kOutput, calls=%fused_computation.8 | convolution fusion | flops 2147483648 | bytes 8388608 | tf_op jit(solution)/shard_map/dot_general | solution.py:1237
  183.8 7.2 %multiply_convert_fusion.1 = (bf16[512,1024]{1,0:T(8,128)(2,1)S(1)}, bf16[512,1024]{1,0:T(8,128)(2,1)S(1)}, bf16[512,1024]{1,0:T(8,128)(2,1)S(1)}) fusion(f32[512,1024]{1,0:T(8,128)} %fusion.7, f32[512,1024]{1,0:T(8,128)} %fusion.32, bf16[512,2048]{1,0:T(8,128)(2,1)} %get-tuple-element.61, bf16[1,2048,1024]{2,1,0:T(8,128)(2,1)} %all-gather.13.cloned.1.call-done), kind=kOutput, calls=%fused_computation.39 | convolution fusion | flops 2155347968 | bytes 13631488 | tf_op jit(solution)/shard_map/dot_general | solution.py:1237
  191.1 4.4 convolution_convert_fusion.3
  195.4 4.4 convolution_convert_fusion.4
  199.9 4.8 convolution_convert_fusion.5
  212.6 3.9 multiply_reduce_fusion
  216.4 69.0 %shard_map.274 = (bf16[512,2048]{1,0:T(8,128)(2,1)}, f32[512,2048]{1,0:T(8,128)}, f32[256,1024]{1,0:T(8,128)}, f32[256,1024]{1,0:T(8,128)}, f32[256,1024]{1,0:T(8,128)}) custom-call(bf16[512,2048]{1,0:T(8,128)(2,1)} %get-tuple-element.136.refs_0_, f32[512,2048]{1,0:T(8,128)} %get-tuple-element.62.refs_1_.refs_8_, f32[1,2048]{1,0:T(1,128)} %get-tuple-element.132.refs_2_, ...), custom_call_target="tpu_custom_call" | custom-call | tf_op jit(solution)/shard_map/pallas_call | solution.py:363
  285.4 6.1 %convolution_convert_fusion.2 = bf16[2048,1024]{1,0:T(8,128)(2,1)} fusion(bf16[512,2048]{1,0:T(8,128)(2,1)} %get-tuple-element.63, bf16[512,1024]{1,0:T(8,128)(2,1)S(1)} %get-tuple-element.66), kind=kOutput, calls=%fused_computation.25 | convolution fusion | flops 2149580800 | bytes 7340032 | tf_op jit(solution)/shard_map/dot_general | solution.py:20
  293.8 3.2 multiply_convert_fusion
  297.0 75.1 %shard_map.275 = (f32[512,1024]{1,0:T(8,128)}, f32[512,1024]{1,0:T(8,128)}, f32[16,8,512]{2,1,0:T(8,128)}, f32[16,8,512]{2,1,0:T(8,128)}, f32[16,8,128]{2,1,0:T(...) custom-call(f32[4096,128]{1,0:T(8,128)} %get-tuple-element.57.refs_0_, f32[4096,128]{1,0:T(8,128)} %get-tuple-element.58.refs_1_, ...), custom_call_target="tpu_custom_call" | custom-call | tf_op jit(solution)/shard_map/pallas_call | solution.py:993
  375.9 27.5 %shard_map.276 = (bf16[512,1024]{1,0:T(8,128)(2,1)}, bf16[2560,128]{1,0:T(8,128)(2,1)}) custom-call(f32[512,1024]{1,0:T(8,128)} %get-tuple-element.68.tb_ref, f32[512,1024]{1,0:T(8,128)} %get-tuple-element.69.sd_ref, f32[32,512]{1,0:T(8,128)} %pad_maximum_fusion.3.sums_ref, f32[16,1024]{1,0:T(8,128)} %bitcast_multiply_fusion.dec_ref, ...), custom_call_target="tpu_custom_call" | custom-call | tf_op jit(solution)/shard_map/pallas_call | solution.py:1150
  403.4 5.8 %convolution_convert_fusion.1 = bf16[2048,1024]{1,0:T(8,128)(2,1)} fusion(bf16[512,2048]{1,0:T(8,128)(2,1)S(1)} %copy-done.37, bf16[512,1024]{1,0:T(8,128)(2,1)} %get-tuple-element.76), kind=kOutput, calls=%fused_computation.24 | convolution fusion | flops 2149580800 | bytes 7340032 | tf_op jit(solution)/shard_map/dot_general | solution.py:20
  409.2 4.4 convolution_convert_fusion
  416.0 4.2 multiply_reduce_fusion.1
  420.9 72.0 %shard_map.277 = (bf16[512,2048]{1,0:T(8,128)(2,1)}, f32[256,1024]{1,0:T(8,128)}, f32[256,1024]{1,0:T(8,128)}, f32[320,128]{1,0:T(8,128)}, f32[16,128]{1,0:T(8,128)}) custom-call(bf16[512,2048]{1,0:T(8,128)(2,1)} %get-tuple-element.138.refs_0_, bf16[512,2048]{1,0:T(8,128)(2,1)} %bitcast.106, f32[1,2048]{1,0:T(1,128)} %get-tuple-element.131.refs_2_, ...), custom_call_target="tpu_custom_call" | custom-call | tf_op jit(solution)/shard_map/pallas_call | solution.py:363
  500.1 2.9 copy.42
  510.9 2.9 copy.40
  (150 shorter events, 46.5 us)
Async XLA Ops:
  7.2 59.4 %all-gather.9.cloned.1.call-start = ((), (), s32[]{:S(2)}) async-start(), calls=%async_computation | async-start | bytes 6291456 | tf_op jit(solution)/shard_map/all_gather | solution.py:1207
  7.9 163.1 %all-gather.11.cloned.1.call-start = ((), (), s32[]{:S(2)}) async-start(), calls=%async_computation.1 | async-start | bytes 6291456 | tf_op jit(solution)/shard_map/all_gather | solution.py:1210
  8.7 168.7 %all-gather.15.cloned.1.call-start = ((), (), s32[]{:S(2)}) async-start(), calls=%async_computation.3 | async-start | bytes 6291456 | tf_op jit(solution)/shard_map/all_gather | solution.py:1209
  14.7 169.1 %all-gather.13.cloned.1.call-start = ((), (), s32[]{:S(2)}) async-start(), calls=%async_computation.2 | async-start | bytes 6291456 | tf_op jit(solution)/shard_map/all_gather | solution.py:1209
  17.5 6.3 %copy-start.22 = (bf16[160,512]{1,0:T(8,128)(2,1)S(1)}, bf16[160,512]{1,0:T(8,128)(2,1)}, u32[]{:S(2)}) copy-start(bf16[160,512]{1,0:T(8,128)(2,1)} %param.23) | copy-start | bytes 491524
  17.5 6.3 %copy-start.24 = (bf16[128,512]{1,0:T(8,128)(2,1)S(1)}, bf16[128,512]{1,0:T(8,128)(2,1)}, u32[]{:S(2)}) copy-start(bf16[128,512]{1,0:T(8,128)(2,1)} %param.24) | copy-start | bytes 393220
  17.5 6.3 %copy-start.25 = (bf16[16,512]{1,0:T(8,128)(2,1)S(1)}, bf16[16,512]{1,0:T(8,128)(2,1)}, u32[]{:S(2)}) copy-start(bf16[16,512]{1,0:T(8,128)(2,1)} %param.26) | copy-start | bytes 49156
  17.6 6.3 %copy-start.26 = (bf16[4,512]{1,0:T(4,128)(2,1)S(1)}, bf16[4,512]{1,0:T(4,128)(2,1)}, u32[]{:S(2)}) copy-start(bf16[4,512]{1,0:T(4,128)(2,1)} %param.21) | copy-start | bytes 12292
  24.6 40.1 %copy-start.14 = (bf16[2,256,2048]{2,1,0:T(8,128)(2,1)S(1)}, bf16[2,256,2048]{2,1,0:T(8,128)(2,1)}, u32[]{:S(2)}) copy-start(bf16[2,256,2048]{2,1,0:T(8,128)(2,1)} %param.18) | copy-start | bytes 6291460
  63.3 3.3 copy-start.3
  108.9 62.1 %copy-start.4 = (f32[2,16,8,128]{3,2,1,0:T(8,128)}, f32[2,16,8,128]{3,2,1,0:T(8,128)S(1)}, u32[]{:S(2)}) copy-start(f32[2,16,8,128]{3,2,1,0:T(8,128)S(1)} %get-tuple-element.65.refs_6_) | copy-start | bytes 393220
  171.0 3.4 copy-start.9
  171.0 3.8 copy-start.33
  183.8 7.2 %copy-start.10 = (bf16[512,2048]{1,0:T(8,128)(2,1)S(1)}, bf16[512,2048]{1,0:T(8,128)(2,1)}, u32[]{:S(2)}) copy-start(bf16[512,2048]{1,0:T(8,128)(2,1)} %fusion.refs_3_) | copy-start | bytes 6291460
  191.1 4.4 copy-start.38
  199.8 4.9 copy-start.34
  285.4 6.2 %copy-start.11 = (bf16[2048,1024]{1,0:T(8,128)(2,1)S(1)}, bf16[2048,1024]{1,0:T(8,128)(2,1)}, u32[]{:S(2)}) copy-start(bf16[2048,1024]{1,0:T(8,128)(2,1)} %all-gather.9.cloned.1.call-done) | copy-start | bytes 12582916
  285.4 6.2 %copy-start.39 = (bf16[512,2048]{1,0:T(8,128)(2,1)S(1)}, bf16[512,2048]{1,0:T(8,128)(2,1)}, u32[]{:S(2)}) copy-start(bf16[512,2048]{1,0:T(8,128)(2,1)} %get-tuple-element.63) | copy-start | bytes 6291460
  375.9 27.5 %copy-start.37 = (bf16[512,2048]{1,0:T(8,128)(2,1)S(1)}, bf16[512,2048]{1,0:T(8,128)(2,1)}, u32[]{:S(2)}) copy-start(bf16[512,2048]{1,0:T(8,128)(2,1)} %get-tuple-element.80) | copy-start | bytes 6291460
  403.4 10.2 %slice-start = ((s8[8388608]{0:T(1024)(128)(4,1)}), s8[4194304]{0:T(1024)(128)(4,1)S(1)}, s32[]{:S(2)}) async-start(s8[8388608]{0:T(1024)(128)(4,1)} %bitcast.134), calls=%async_computation.4 | async-start | bytes 8388608
  409.2 4.4 slice-start.1
  420.9 78.9 %copy-start.17 = (f32[256,1024]{1,0:T(8,128)S(1)}, f32[256,1024]{1,0:T(8,128)}, u32[]{:S(2)}) copy-start(f32[256,1024]{1,0:T(8,128)} %get-tuple-element.88) | copy-start | bytes 3145732
  420.9 78.9 %copy-start.18 = (f32[256,1024]{1,0:T(8,128)S(1)}, f32[256,1024]{1,0:T(8,128)}, u32[]{:S(2)}) copy-start(f32[256,1024]{1,0:T(8,128)} %get-tuple-element.89) | copy-start | bytes 3145732
  503.0 5.2 copy-start.12
  (23 other events, 45.0 us)
Sparse Core Ops, SparseCore 0:
  9.6 16.3 all-gather.8
  27.5 14.8 all-gather.10
  44.5 14.8 all-gather.14
  61.4 14.8 all-gather.12

commit v5 on v4

--- a/solution.py
+++ b/solution.py
@@ -148,10 +148,21 @@
         def _():
             self.copy_a(c + self.ahead).start()
 
+    def quiet_tick(self, c):
+        lag = min(self.lag, self.count)
+
+        @pl.when(jnp.logical_and(self.middle, jnp.logical_and(c >= 0, c < self.count)))
+        def _():
+            self.first(c)
+
+        @pl.when(jnp.logical_and(self.middle, jnp.logical_and(c >= lag, c < self.count + lag)))
+        def _():
+            self.second(c - lag)
+
     def ticks(self):
         return self.count + min(self.lag, self.count)
 
-    def finish(self):
+    def finish(self, take_result=True):
         @pl.when(self.middle)
         def _():
             def drain(c, _):
@@ -164,7 +175,8 @@
         @pl.when(jnp.logical_not(self.middle))
         def _():
             def take(c, _):
-                self.copy_c(c).wait_recv()
+                if take_result:
+                    self.copy_c(c).wait_recv()
                 self.copy_a(c).wait_send()
                 return 0
 
@@ -176,7 +188,8 @@
 
 
 class Halving:
-    def __init__(self, arrays, step_rows=16):
+    def __init__(self, arrays, step_rows=16, lag=share_lag):
+        self.lag = lag
         steps = [step_rows] * len(arrays) if isinstance(step_rows, int) else list(step_rows)
         self.steps = steps
         shards, pieces = lax.axis_size("shard"), lax.axis_size("ctx")
@@ -196,7 +209,7 @@
         ]
         self.tails = [g.shape[self.depth :] for g in self.folded]
         self.pairs = (max(self.parts, default=0) + 1) // 2
-        self.turns = self.pairs + share_lag * (self.depth - 1)
+        self.turns = self.pairs + lag * (self.depth - 1)
 
     def results(self):
         return [jax.ShapeDtypeStruct(tail, f32) for tail in self.tails]
@@ -293,7 +306,7 @@
         if self.n:
             self.each(i + share_ahead, self.begin)
             for j in range(self.depth):
-                self.each(i - share_lag * j, functools.partial(self.step, j))
+                self.each(i - self.lag * j, functools.partial(self.step, j))
 
     def finish(self):
         def sent(i, _):
@@ -590,7 +603,8 @@
     )(hidden, tails, in_half, small, gains)
 
 
-piece = 32
+piece = 16
+slots_held = 4
 unroll = 4
 
 
@@ -838,7 +852,7 @@
     early = 2
     unroll_b = 2
     line = Line(partial.shape, chunk, epilogue, extras, bf16)
-    share = Halving(scatters, 64)
+    share = Halving(scatters, 16, 1)
     n_line, n_ex, n_sc = len(line.scratch()), len(extras), len(scatters)
 
     def kernel(*refs):
@@ -851,9 +865,9 @@
 
         size_ref, drive_ref, grad_ref, low_ref, rate_ref, kept_ref, enter_ref, p_ref = take_refs(8)
         ins, full = take_refs(n_ex), take_refs(n_sc)
-        tb_ref, sd_ref, bg_ref, cg_ref, dec_ref, sum_ref = take_refs(6)
+        tb3, sd3, bg_ref, cg_ref, dec_ref, sum_ref = take_refs(6)
         shares = take_refs(n_sc)
-        grad3, tb3, sd3, b_ref, c_ref, ends, got, held, bpart, cpart, prior, send, recv, in_sem = take_refs(14)
+        grad3, b_ref, c_ref, ends, got, held, bpart, cpart, prior, send, recv, in_sem = take_refs(12)
         line.bind(p_ref, ins, sum_ref, [], take_refs(n_line))
         share.bind(full, shares, refs)
         barrier = ctx_greet(width)
@@ -861,6 +875,7 @@
         share.start()
         spread_rows(low_ref, rank, b_ref)
         spread_rows(low_ref, rank + states, c_ref)
+        share.tick(0)
 
         def lay(i, _):
             first = pl.multiple_of(i * 8, 8)
@@ -869,10 +884,13 @@
 
         lax.fori_loop(0, rows // 8, lay, 0)
 
-        def fetch(seq, k, slot):
-            return pltpu.make_async_copy(
-                kept_ref.at[pl.ds(seq * local + k * piece, piece)], held.at[slot], in_sem.at[slot]
-            )
+        def fetch(g):
+            first = (g // pieces) * local + (pieces - 1 - g % pieces) * piece
+            slot = g % slots_held
+            return pltpu.make_async_copy(kept_ref.at[pl.ds(first, piece)], held.at[slot], in_sem.at[slot])
+
+        for g in range(slots_held - 1):
+            fetch(g).start()
 
         copies = []
         for seq in range(seqs):
@@ -896,16 +914,16 @@
             for n in range(states + 1):
                 ends[seq, n] = done[n]
             copies.append(exchange(ends, got, send, recv, seq, width))
+            share.tick(1 + seq)
         me = lax.axis_index("ctx")
         for n in range(states):
             dec_ref[n] = jnp.zeros((8, 128), f32)
         for seq in range(seqs):
-            fetch(seq, pieces - 1, (pieces - 1) % 2).start()
             for copy in copies[seq]:
                 copy.wait()
             got[me, seq] = ends[seq]
             start = entering(got, seq, rate_ref, states, width, True)
-            fetch(seq, pieces - 1, (pieces - 1) % 2).wait()
+            fetch(seq * pieces).wait()
 
             def one_slot(slot, k, inside, adjoint, decays, prior_at):
                 t = seq * local + k * piece + inside
@@ -933,11 +951,12 @@
 
             def one_piece(back_k, carried):
                 k = pieces - 1 - back_k
-                slot = lax.rem(k, 2)
-
-                @pl.when(k > 0)
+                place = seq * pieces + back_k
+                slot = place % slots_held
+
+                @pl.when(place + slots_held - 1 < seqs * pieces)
                 def _():
-                    fetch(seq, k - 1, 1 - slot).start()
+                    fetch(place + slots_held - 1).start()
 
                 def slots(i, carried):
                     adjoint, decays = list(carried[:states]), list(carried[states:])
@@ -953,8 +972,8 @@
 
                 @pl.when(k > 0)
                 def _():
-                    fetch(seq, k - 1, 1 - slot).wait()
-                    prior[...] = held[1 - slot, piece - 1]
+                    fetch(place + 1).wait()
+                    prior[...] = held[(place + 1) % slots_held, piece - 1]
 
                 @pl.when(k == 0)
                 def _():
@@ -965,8 +984,14 @@
                 for part, out in ((bpart, bg_ref), (cpart, cg_ref)):
                     sums = outer_cols(ones, part[...].astype(bf16))
                     out[pl.ds(seq * pieces + k, 1)] = sums[None]
-                line.tick(seqs * early + seq * pieces + back_k)
-                share.tick(seq * pieces + back_k)
+                @pl.when(place % 2 == 0)
+                def _():
+                    line.tick(seqs * early + place // 2)
+
+                @pl.when(place % 5 == 0)
+                def _():
+                    share.tick(1 + seqs + place // 5)
+
                 return tuple(adjoint) + tuple(decays)
 
             zero = tuple(jnp.zeros((8, 128), f32) for _ in range(states))
@@ -974,40 +999,33 @@
             for n in range(states):
                 dec_ref[n] = dec_ref[n] + carried[states + n]
 
-        def back(i, _):
-            first = pl.multiple_of(i * 8, 8)
-            tb_ref[pl.ds(first, 8), :] = unspread(tb3, first)
-            sd_ref[pl.ds(first, 8), :] = unspread(sd3, first)
-            return 0
-
-        lax.fori_loop(0, rows // 8, back, 0)
-        for c in range(seqs * (early + pieces), line.ticks()):
+        for c in range(seqs * early + (seqs * pieces + 1) // 2, line.ticks()):
             line.tick(c)
-        for i in range(seqs * pieces, share.turns):
+        for i in range(1 + seqs + (seqs * pieces + 4) // 5, share.turns):
             share.tick(i)
         line.finish()
         share.finish()
 
-    nat = jax.ShapeDtypeStruct((rows, channels), f32)
+    flat = jax.ShapeDtypeStruct((rows * 8, 128), f32)
     sums = jax.ShapeDtypeStruct((rows // piece, 8, piece * states), f32)
     return pl.pallas_call(
         kernel,
-        out_shape=[nat, nat, sums, sums, jax.ShapeDtypeStruct((states, 8, 128), f32),
+        out_shape=[flat, flat, sums, sums, jax.ShapeDtypeStruct((states, 8, 128), f32),
                    jax.ShapeDtypeStruct(partial.shape, bf16)] + share.results(),
         in_specs=[VMEM] * 5 + [HBM, VMEM] + [HBM] * (1 + n_ex + n_sc),
         out_specs=[VMEM] * (6 + n_sc),
-        scratch_shapes=[pltpu.VMEM((rows * 8, 128), f32)] * 3
+        scratch_shapes=[pltpu.VMEM((rows * 8, 128), f32)]
         + [pltpu.VMEM((rows * states, 128), f32)] * 2
         + [
             pltpu.VMEM((seqs, states + 1, 8, 128), f32),
             pltpu.VMEM((width, seqs, states + 1, 8, 128), f32),
-            pltpu.VMEM((2, piece, states, 8, 128), f32),
+            pltpu.VMEM((slots_held, piece, states, 8, 128), f32),
             pltpu.VMEM((piece * states, 128), f32),
             pltpu.VMEM((piece * states, 128), f32),
             pltpu.VMEM((states, 8, 128), f32),
             pltpu.SemaphoreType.DMA((seqs, width)),
             pltpu.SemaphoreType.DMA((seqs, width)),
-            pltpu.SemaphoreType.DMA((2,)),
+            pltpu.SemaphoreType.DMA((slots_held,)),
         ]
         + line.scratch()
         + share.scratch(),
@@ -1017,7 +1035,177 @@
     )(size3, drive3, grad, low_all, rate, kept, enter, partial, *extras, *share.folded)
 
 
-def scan_tail(through_b, through_decay, sums, decay_grad, scan_grad, step_pre, pre_act, act, padded, low_all, small, ident,
+def feed_forward(mixed_part, hidden, gain, ffn_grad, gate_w, down_parts, ident):
+    rows, width = hidden.shape
+    shards, ffn, part = down_parts.shape
+    chunk = 32
+    block = 4 * chunk
+    tile = ffn // 4
+    blocks = rows // block
+    fore = Line(mixed_part.shape, chunk, norm_end, [], bf16)
+    after = Line(mixed_part.shape, chunk, norm_back_end, [], bf16)
+    n_line = len(fore.scratch())
+    behind = 6
+    wtile = 256
+
+    def kernel(
+        p_ref, hid_ref, gain_ref, fg_ref, gate_ref, up_ref, down_ref,
+        ffn_out, mid_out, mix_ref, midg_ref, gsum_ref, both_out, dw_out,
+        normed, middle, hid_v, gg_v, ug_v, ffn_v, ffn_acc, back_acc, gate_v, up_v, down_v, stage, stage_d, load_sem, save_sem, *rest
+    ):
+        barrier = pltpu.get_barrier_semaphore()
+        fore.bind(p_ref, [], normed, [middle], rest[:n_line])
+        after.bind(rest[n_line], [], mix_ref, [midg_ref], rest[n_line:])
+        fore.ins = [hid_ref, gain_ref]
+        after.ins = [middle, gain_ref, fg_ref]
+        loads = [
+            pltpu.make_async_copy(a, b, load_sem.at[i])
+            for i, (a, b) in enumerate(((gate_ref, gate_v), (up_ref, up_v), (down_ref, down_v)))
+        ]
+        fore.begin(barrier, 0)
+        for load in loads:
+            load.start()
+        gsum_ref[...] = jnp.zeros_like(gsum_ref)
+        lead = 4 + fore.lag
+
+        def warm(c, _):
+            fore.tick(c)
+            return 0
+
+        lax.fori_loop(0, lead, warm, 0)
+        for load in loads:
+            load.wait()
+        outer = jnp.logical_not(fore.middle)
+
+        def step(s, _):
+            b, j = s // 4, s % 4
+            fore.tick(s + lead)
+            at = pl.ds(pl.multiple_of(b * block, block), block)
+            here = pl.ds(pl.multiple_of(j * tile, tile), tile)
+
+            @pl.when(j == 0)
+            def _():
+                ffn_acc[...] = jnp.zeros_like(ffn_acc)
+                back_acc[...] = jnp.zeros_like(back_acc)
+
+                @pl.when(outer)
+                def _():
+                    for k in range(4):
+                        fore.copy_c(4 * b + k).wait_recv()
+
+            source, grad = normed[at, :], fg_ref[at, :]
+            gate = jnp.dot(source, gate_v[:, here], preferred_element_type=f32)
+            up = jnp.dot(source, up_v[:, here], preferred_element_type=f32)
+            sig = jax.nn.sigmoid(gate)
+            silu = gate * sig
+            hidden_val = (silu * up).astype(bf16)
+            back = sum(
+                outer_cols(grad[:, k * part : (k + 1) * part], down_v[k, here, :]) for k in range(shards)
+            )
+            gate_back = (back * up * (sig * (1.0 + gate * (1.0 - sig)))).astype(bf16)
+            up_back = (back * silu).astype(bf16)
+            hid_v[at, here] = hidden_val
+            gg_v[at, here] = gate_back
+            ug_v[at, here] = up_back
+
+            after.quiet_tick(s - behind)
+
+            for k in range(shards):
+                to = slice(k * part, (k + 1) * part)
+                ffn_acc[:, to] += jnp.dot(hidden_val, down_v[k, here, :], preferred_element_type=f32)
+            for k in range(width // 512):
+                to = slice(k * 512, (k + 1) * 512)
+                back_acc[:, to] += outer_cols(gate_back, gate_v[to, here]) + outer_cols(up_back, up_v[to, here])
+
+            @pl.when(j == 3)
+            def _():
+                ffn_v[at, :] = ffn_acc[...].astype(bf16)
+                after.p[at, :] = back_acc[...].astype(bf16)
+                for k in range(block // 16):
+                    product = after.p[pl.ds(pl.multiple_of(b * block + k * 16, 16), 16), :].astype(f32)
+                    product = product * normed[pl.ds(pl.multiple_of(b * block + k * 16, 16), 16), :].astype(f32)
+                    gsum_ref[...] += product[:8] + product[8:]
+
+                @pl.when(outer)
+                def _():
+                    for k in range(4):
+                        after.copy_a(4 * b + k).start()
+
+            return 0
+
+        steps = 4 * blocks
+        lax.fori_loop(0, steps, step, 0)
+        ffn_save = pltpu.make_async_copy(ffn_v, ffn_out, save_sem.at[3])
+        ffn_save.start()
+        mid_save = pltpu.make_async_copy(middle, mid_out, save_sem.at[4])
+        mid_save.start()
+
+        def saves(i):
+            to = pl.ds(pl.multiple_of(i * wtile, wtile), wtile)
+            return [
+                pltpu.make_async_copy(held, out.at[to], save_sem.at[a])
+                for a, (held, out) in enumerate(((stage, both_out), (stage_d, dw_out)))
+            ]
+
+        def weights(i, _):
+            after.quiet_tick(steps - behind + i)
+            here = pl.ds(pl.multiple_of(i * wtile, wtile), wtile)
+
+            @pl.when(i > 0)
+            def _():
+                for save in saves(i - 1):
+                    save.wait()
+
+            source, grad = normed[:, here], fg_ref[:, here]
+            stage[:, :ffn] = inner_rows(source, gg_v[...]).astype(bf16)
+            stage[:, ffn:] = inner_rows(source, ug_v[...]).astype(bf16)
+            stage_d[...] = inner_rows(grad, hid_v[...]).astype(bf16)
+            for save in saves(i):
+                save.start()
+            return 0
+
+        lax.fori_loop(0, width // wtile, weights, 0)
+        for c in range(steps - behind + width // wtile, after.ticks()):
+            after.quiet_tick(c)
+        for save in saves(width // wtile - 1) + [ffn_save, mid_save]:
+            save.wait()
+        fore.finish(False)
+        after.finish()
+
+    sds = jax.ShapeDtypeStruct
+    wide, half = sds((rows, width), f32), sds((rows, width), bf16)
+    both, down = sds((width, 2 * ffn), bf16), sds((width, ffn), bf16)
+    return pl.pallas_call(
+        kernel,
+        out_shape=[half, wide, half, wide, sds((8, width), f32), both, down],
+        in_specs=[HBM, VMEM, VMEM, VMEM, HBM, HBM, HBM],
+        out_specs=[HBM, HBM, VMEM, VMEM, VMEM, HBM, HBM],
+        scratch_shapes=[
+            pltpu.VMEM((rows, width), bf16),
+            pltpu.VMEM((rows, width), f32),
+            pltpu.VMEM((rows, ffn), bf16),
+            pltpu.VMEM((rows, ffn), bf16),
+            pltpu.VMEM((rows, ffn), bf16),
+            pltpu.VMEM((rows, width), bf16),
+            pltpu.VMEM((block, width), f32),
+            pltpu.VMEM((block, width), f32),
+            pltpu.VMEM((width, ffn), bf16),
+            pltpu.VMEM((width, ffn), bf16),
+            pltpu.VMEM(down_parts.shape, bf16),
+            pltpu.VMEM((wtile, 2 * ffn), bf16),
+            pltpu.VMEM((wtile, ffn), bf16),
+            pltpu.SemaphoreType.DMA((3,)),
+            pltpu.SemaphoreType.DMA((5,)),
+        ]
+        + fore.scratch()
+        + after.scratch(),
+        compiler_params=pltpu.CompilerParams(
+            collective_id=ident, has_side_effects=True, vmem_limit_bytes=62 << 20
+        ),
+    )(mixed_part, hidden, gain, ffn_grad, gate_w[0], gate_w[1], down_parts)
+
+
+def scan_tail(through_b, through_decay, sums, decay_grad, scan_grad, step_pre, pre_act, act, padded, z_half, low_all, small, ident,
               seqs, low_len, rank, states, taps):
     rows, inner = act.shape
     local = rows // seqs
@@ -1033,7 +1221,7 @@
     over = 8
 
     def kernel(
-        tb_ref, sd_ref, sums_ref, dec_ref, sg_ref, sp_ref, pre_ref, act_ref, ext_ref, low_ref, small_ref,
+        tb_ref, sd_ref, sums_ref, dec_ref, sg_ref, sp_ref, pre_ref, act_ref, ext_ref, zg_ref, low_ref, small_ref,
         conv_ref, blocks_ref,
         low_out, low_t, step_g, low_acc, grads, pre_g, conv_f, edge, edge_out, edge_sem, *rest
     ):
@@ -1042,6 +1230,10 @@
         line.bind(rest[0], [], low_out, [], list(rest))
         pl.semaphore_signal(barrier, inc=1, device_id={"ctx": lax.rem(ctx + 1, pieces)}, device_id_type=MESH)
 
+        def flat(ref, j, first, count):
+            parts = [ref[pl.ds(first * 8 + j * (tile_cols // 128) + h, count, stride=8), :] for h in range(tile_cols // 128)]
+            return jnp.concatenate(parts, axis=1)
+
         def cols(j):
             return pl.ds(pl.multiple_of(j * tile_cols, tile_cols), tile_cols)
 
@@ -1056,7 +1248,7 @@
             for k in range(rows // 64):
                 to = slice(k * 64, (k + 1) * 64)
                 act_block = act_ref[to, here].astype(f32)
-                size_grad = act_block * tb_ref[to, here] + sd_ref[to, here] * (1.0 / log2e)
+                size_grad = act_block * flat(tb_ref, j, k * 64, 64) + flat(sd_ref, j, k * 64, 64) * (1.0 / log2e)
                 value = (size_grad * jax.nn.sigmoid(sp_ref[to, here])).astype(bf16)
                 step_g[to, here] = value
                 wide = value.astype(f32)
@@ -1100,7 +1292,7 @@
                 for k in range(local // 64):
                     to = slice(seq * local + k * 64, seq * local + (k + 1) * 64)
                     where = slice(seq * (local + over) + k * 64, seq * (local + over) + (k + 1) * 64)
-                    act_grad = skip * sg_ref[to, here] + jax.nn.softplus(sp_ref[to, here]) * tb_ref[to, here]
+                    act_grad = skip * sg_ref[to, here] + jax.nn.softplus(sp_ref[to, here]) * flat(tb_ref, j, seq * local + k * 64, 64)
                     value = (act_grad + pre_g[where, here]) * silu_grad(pre_ref[to, here])
                     pre_g[where, here] = value
                     first = seq * long + halo + k * 64 - taps + 1
@@ -1146,14 +1338,15 @@
             return 0
 
         lax.fori_loop(0, tiles, conv_tile, 0)
+        conv_ref[:, inner:] = zg_ref[...]
 
     return pl.pallas_call(
         kernel,
         out_shape=[
-            jax.ShapeDtypeStruct((rows, inner), bf16),
+            jax.ShapeDtypeStruct((rows, 2 * inner), bf16),
             jax.ShapeDtypeStruct((places * height, lane), bf16),
         ],
-        in_specs=[VMEM] * 11,
+        in_specs=[VMEM] * 12,
         out_specs=[VMEM] * 2,
         scratch_shapes=[
             pltpu.VMEM((low_len, rows), bf16),
@@ -1171,7 +1364,7 @@
         compiler_params=pltpu.CompilerParams(
             collective_id=ident, has_side_effects=True, vmem_limit_bytes=56 << 20
         ),
-    )(through_b, through_decay, sums, decay_grad, scan_grad, step_pre, pre_act, act, padded, low_all, small), height
+    )(through_b, through_decay, sums, decay_grad, scan_grad, step_pre, pre_act, act, padded, z_half, low_all, small), height
 
 
 def body(
@@ -1232,45 +1425,31 @@
     )
     step_size = jax.nn.softplus(step_pre)
     gate_act = jax.nn.silu(gate_z)
-    wide = jax.ShapeDtypeStruct((rows, width), f32)
-    normed_two, middle = tp_sum(mixed_part, norm_end, [hidden_rows, gain_two], [wide], 32, 3)
-    gate_lin, up_lin = (jnp.dot(normed_two, gate_w[c], preferred_element_type=f32) for c in range(2))
-    hidden_ffn = (jax.nn.silu(gate_lin) * up_lin).astype(bf16)
-    ffn_part = jnp.concatenate(
-        [jnp.dot(hidden_ffn, down_parts[k], preferred_element_type=f32) for k in range(shards)], axis=1
-    ).astype(bf16)
-
     upstream = cotangent.reshape(rows, width).astype(f32) * pad_mask.reshape(rows, 1)
     ffn_grad = upstream.astype(bf16)
-    down_grad = inner_rows(ffn_grad, hidden_ffn).astype(bf16)
-    hidden_grad = sum(outer_cols(ffn_grad[:, k * part : (k + 1) * part], down_parts[k]) for k in range(shards))
-    gate_grad = (hidden_grad * up_lin * silu_grad(gate_lin)).astype(bf16)
-    up_grad = (hidden_grad * jax.nn.silu(gate_lin)).astype(bf16)
-    gate_up_grad = [inner_rows(normed_two, g).astype(bf16) for g in (gate_grad, up_grad)]
-    back_part = (outer_cols(gate_grad, gate_w[0]) + outer_cols(up_grad, gate_w[1])).astype(bf16)
-    mix_grad, middle_grad, *ffn_shares = tp_sum(
-        back_part, norm_back_end, [middle, gain_two, ffn_grad], [wide], 32, 5, scatters=gate_up_grad + [down_grad]
+    ffn_part, middle, mix_grad, middle_grad, gain_sum, both_grad, down_grad = feed_forward(
+        mixed_part, hidden_rows, gain_two, ffn_grad, gate_w, down_parts, 3
     )
-    ffn_gain_grad = jnp.sum(back_part.astype(f32) * normed_two.astype(f32), axis=0) / gain_two[0]
+    ffn_gain_grad = jnp.sum(gain_sum, axis=0) / gain_two[0]
 
     out_weight_grad = inner_rows(mix_grad, gated_out).astype(bf16)
     gated_grad = sum(outer_cols(mix_grad[:, k * part : (k + 1) * part], out_parts[k]) for k in range(shards))
     scan_grad = gated_grad * gate_act
     z_grad = gated_grad * scan_out * silu_grad(gate_z)
-    through_b, through_decay, b_sums, c_sums, decay_sum, mixed_out, out_share = scan_backward(
+    through_b, through_decay, b_sums, c_sums, decay_sum, mixed_out, *ffn_shares = scan_backward(
         size3, drive3, scan_grad, low_all, rank, rate, kept, enter, seqs, 6, ffn_part, add_end, [middle], 32,
-        [out_weight_grad],
+        [both_grad, down_grad],
     )
     mixed_out = mixed_out.reshape(hidden_in.shape)
     decay_log_grad = decay_sum.reshape(states, inner) * decay_rate
     sums = jnp.concatenate([v[:, 0].reshape(rows, states).T for v in (b_sums, c_sums)], axis=0)
-    (conv_grad, small_blocks), small_height = scan_tail(
-        through_b, through_decay, sums, decay_log_grad, scan_grad, step_pre, pre_act, act_half, padded, low_all, small, 7,
+    z_half = z_grad.astype(bf16)
+    (project_grad, small_blocks), small_height = scan_tail(
+        through_b, through_decay, sums, decay_log_grad, scan_grad, step_pre, pre_act, act_half, padded, z_half, low_all, small, 7,
         seqs, low_len, rank, states, taps,
     )
-    z_half = z_grad.astype(bf16)
-    in_weight_grad = [inner_rows(normed_one, g).astype(bf16) for g in (conv_grad, z_half)]
-    first_part = (outer_cols(conv_grad, in_w[0]) + outer_cols(z_half, in_w[1])).astype(bf16)
+    in_weight_grad = inner_rows(normed_one, project_grad).astype(bf16)
+    first_part = sum(outer_cols(project_grad[:, c * inner : (c + 1) * inner], in_w[c]) for c in range(2)).astype(bf16)
     norm_gain_grad = jnp.sum(first_part.astype(f32) * source * rms_scale(source), axis=0)
     places, share = shards * pieces, width // (shards * pieces)
     lane = inner // places
@@ -1280,9 +1459,9 @@
     gain_height = 16 * -(-gain_rows // 16)
     gain_blocks = jnp.pad(gain_blocks, ((0, 0), (gain_height - gain_rows, 0), (0, 0)))
     gain_blocks = gain_blocks.reshape(places * gain_height, lane).astype(bf16)
-    input_grad, in_share, z_share, small_out, gain_share = tp_sum(
+    input_grad, in_share, out_share, small_out, gain_share = tp_sum(
         first_part, norm_back_end, [hidden_rows, gain_one, middle_grad], [], 32, 8,
-        scatters=in_weight_grad + [small_blocks, gain_blocks], line_too=True,
+        scatters=[in_weight_grad, out_weight_grad, small_blocks, gain_blocks], line_too=True,
         steps=[16, 16, small_height // 2, gain_height],
     )
     gain_share = gain_share[gain_height - gain_rows :].reshape(-1)
@@ -1292,7 +1471,7 @@
         mixed_out,
         input_grad,
         gain_share[:share],
-        jnp.stack([in_share, z_share], axis=1),
+        in_share.reshape((-1,) + in_weight.shape[1:]),
         small_out[at + states : at + states + taps],
         small_out[at + states + taps],
         small_out[:low_len],
@@ -1302,8 +1481,8 @@
         small_out[at + states + taps + 2],
         out_share.T,
         gain_share[share : 2 * share],
-        jnp.stack(ffn_shares[:2], axis=1),
-        ffn_shares[2].T,
+        ffn_shares[0].reshape((-1,) + gate_up.shape[1:]),
+        ffn_shares[1].T,
     )
 
 

time: 530 us -> 498 us (0.940)
  matrix products: 69.4 us -> 28.5 us
  Pallas kernels: 384 us -> 395 us
    pallas_call x2 -> x3, Pallas kernels: 103 us -> 231 us  [the longest x1 121 us: feed_forward(): pl.pallas_call(kernel, out_shape=[half, wide, half, wide, sds((8, width),...]
    pallas_call x3 -> x1, Pallas kernels: 203 us -> 80.3 us  [tp_sum(): pl.pallas_call(kernel, out_shape=[jax.ShapeDtypeStruct(partial.shape, out...]
    dot_general x6 -> x2, matrix products: 29.9 us -> 11.3 us  [inner_rows(): lax.dot_general(left, right, (((0,), (0,)), ((), ())), preferred_element_...]
    dot_general x4 -> x0, matrix products: 16.2 us -> none  [the longest x2 13.7 us: body(): jnp.dot(normed_two, gate_w[c], preferred_element_type=f32)]
    unnamed x100 -> x86, local copies, waits for them, and re-layouts: 25.9 us -> 17.9 us
    dot_general x8 -> x4, matrix products: 23.3 us -> 17.2 us  [outer_cols(): lax.dot_general(left, right, (((1,), (1,)), ((), ())), preferred_element_...]
    reshape x0 -> x2, local copies, waits for them, and re-layouts: none -> 5.53 us  [the longest x1 2.77 us: body(): ffn_shares[0].reshape((-1,) + gate_up.shape[1:])]
  transfers between devices with their start and end apart: 4 -> 4, of which waited for: 0 -> 0; matrix products, arithmetic and copies ran while one was open for 6% -> 4% of each run, Pallas kernels for 27% -> 17%
where the time goes in v5:
time: 498 us; the launch traced here: 490 us
  Pallas kernels  395 us (79%)
  local copies, waits for them, and re-layouts  37.3 us (7%)
  matrix products  28.5 us (6%)
  between operations  14.8 us (3%)
  other arithmetic  12.4 us (2%)
    pallas_call x1, Pallas kernels, feed_forward(): pl.pallas_call(kernel, out_shape=[half, wide, half, wide, sds((8, width),...  121 us
    pallas_call x1, Pallas kernels, scan_backward(): pl.pallas_call(kernel, out_shape=[flat, flat, sums, sums, jax.ShapeDtypeS...  83.3 us
    pallas_call x1, Pallas kernels, tp_sum(): pl.pallas_call(kernel, out_shape=[jax.ShapeDtypeStruct(partial.shape, out...  80.3 us
    pallas_call x1, Pallas kernels, scan_forward(): pl.pallas_call(kernel, out_shape=[jax.ShapeDtypeStruct((rows, channels),...  45.5 us
    pallas_call x1, Pallas kernels, front(): pl.pallas_call(kernel, out_shape=[sds((2, shards * part, inner), bf16), s...  38 us
    pallas_call x1, Pallas kernels, scan_tail(): pl.pallas_call(kernel, out_shape=[jax.ShapeDtypeStruct((rows, 2 * inner),...  26.7 us
    unnamed x86, local copies, waits for them, and re-layouts  17.9 us
    dot_general x4, matrix products, outer_cols(): lax.dot_general(left, right, (((1,), (1,)), ((), ())), preferred_element_...  17.2 us
  transfers between devices with their start and end apart: 4, of which 0 were waited for; matrix products, arithmetic and copies ran while one was open for 4% of the time, Pallas kernels for 17%

profile of v5, /device:TPU:0, one launch (start us, length us, event | category | flops | bytes accessed | tf_op | source)
XLA Modules:
  0.0 489.7 jit_solution(13925578118818740374)
XLA Ops:
  8.0 3.5 copy.48
  11.5 2.5 fusion.31
  15.4 5.7 %copy.49 = bf16[1024,2,1024]{2,0,1:T(8,128)(2,1)} copy(bf16[1024,2,1024]{2,1,0:T(2,128)(2,1)} %param.20) | data formatting | bytes 8388608 | tf_op args[4]
  21.1 1.6 slice.84.tail_ref
  23.6 38.0 %shard_map.271 = (bf16[2,2048,1024]{2,1,0:T(8,128)(2,1)}, bf16[352,1024]{1,0:T(8,128)(2,1)}, bf16[16,2048]{1,0:T(8,128)(2,1)}, bf16[512,2048]{1,0:T(8,128)(2,1)}...) custom-call(bf16[512,2048]{1,0:T(8,128)(2,1)} %bitcast.69, ...), custom_call_target="tpu_custom_call" | custom-call | tf_op jit(solution)/shard_map/pallas_call | solution.py:563
  63.0 1.4 slice_convert_fusion
  64.5 1.8 fusion.fg_ref
  66.3 45.5 %shard_map.272 = (f32[512,1024]{1,0:T(8,128)S(1)}, bf16[512,1024]{1,0:T(8,128)(2,1)S(1)}, bf16[512,2048]{1,0:T(8,128)(2,1)}, f32[512,1024]{1,0:T(8,128)}, f32[51...) custom-call(f32[160,512]{1,0:T(8,128)S(1)} %copy-done.2, ...), custom_call_target="tpu_custom_call" | custom-call | tf_op jit(solution)/shard_map/pallas_call | solution.py:798
  114.8 120.8 %shard_map.273 = (bf16[512,2048]{1,0:T(8,128)(2,1)}, f32[512,2048]{1,0:T(8,128)}, bf16[512,2048]{1,0:T(8,128)(2,1)}, f32[512,2048]{1,0:T(8,128)}, f32[8,2048]{1,...) custom-call(bf16[512,2048]{1,0:T(8,128)(2,1)} %get-tuple-element.60.p_ref, ...), custom_call_target="tpu_custom_call" | custom-call | tf_op jit(solution)/shard_map/pallas_call | solution.py:1178
  235.7 3.3 fusion.9
  240.0 4.8 multiply_convert_fusion
  244.8 83.3 %shard_map.274 = (f32[4096,128]{1,0:T(8,128)}, f32[4096,128]{1,0:T(8,128)}, f32[32,8,256]{2,1,0:T(8,128)}, f32[32,8,256]{2,1,0:T(8,128)}, f32[16,8,128]{2,1,0:T(...) custom-call(f32[4096,128]{1,0:T(8,128)} %get-tuple-element.58.refs_0_, ...), custom_call_target="tpu_custom_call" | custom-call | tf_op jit(solution)/shard_map/pallas_call | solution.py:1011
  328.1 1.5 bitcast_multiply_fusion.dec_ref
  331.9 26.7 %shard_map.275 = (bf16[512,2048]{1,0:T(8,128)(2,1)}, bf16[2560,128]{1,0:T(8,128)(2,1)}) custom-call(f32[4096,128]{1,0:T(8,128)} %get-tuple-element.70.tb_ref, f32[4096,128]{1,0:T(8,128)} %get-tuple-element.71.sd_ref, f32[32,512]{1,0:T(8,128)} %pad_maximum_fusion.sums_ref, f32[16,1024]{1,0:T(8,128)} %bitcast_multiply_fusion.dec_ref, ...), custom_call_target="tpu_custom_call" | custom-call | tf_op jit(solution)/shard_map/pallas_call | solution.py:1343
  358.6 5.0 %fusion.1 = f32[512,2048]{1,0:T(8,128)S(1)} fusion(bf16[2,2048,1024]{2,1,0:T(8,128)(2,1)} %get-tuple-element.80, bf16[512,2048]{1,0:T(8,128)(2,1)} %get-tuple-element.79), kind=kOutput, calls=%fused_computation.3 | convolution fusion | flops 2147483648 | bytes 9437184 | tf_op jit(solution)/shard_map/dot_general | solution.py:24
  363.7 6.9 %convolution_convert_fusion = bf16[2048,2048]{1,0:T(8,128)(2,1)} fusion(bf16[512,2048]{1,0:T(8,128)(2,1)S(1)} %copy-done.32, bf16[512,2048]{1,0:T(8,128)(2,1)S(1)} %copy-done.34), kind=kOutput, calls=%fused_computation | convolution fusion | flops 4299161600 | bytes 12582912 | tf_op jit(solution)/shard_map/dot_general | solution.py:20
  370.6 4.4 convolution_convert_fusion.1
  375.0 4.1 multiply_reduce_fusion
  379.8 80.3 %shard_map.276 = (bf16[512,2048]{1,0:T(8,128)(2,1)}, f32[256,2048]{1,0:T(8,128)}, f32[256,1024]{1,0:T(8,128)}, f32[320,128]{1,0:T(8,128)}, f32[16,128]{1,0:T(8,128)}) custom-call(bf16[512,2048]{1,0:T(8,128)(2,1)} %get-tuple-element.135.refs_0_, bf16[512,2048]{1,0:T(8,128)(2,1)} %bitcast.71, f32[1,2048]{1,0:T(1,128)} %get-tuple-element.130.refs_2_, ...), custom_call_target="tpu_custom_call" | custom-call | tf_op jit(solution)/shard_map/pallas_call | solution.py:376
  460.1 1.5 slice.104
  461.7 1.5 slice.105
  467.0 4.3 convert.15
  471.3 2.8 reshape.141
  476.7 2.8 reshape.142
  (123 shorter events, 21.0 us)
Async XLA Ops:
  7.2 59.1 %all-gather.9.cloned.1.call-start = ((), (), s32[]{:S(2)}) async-start(), calls=%async_computation | async-start | bytes 6291456 | tf_op jit(solution)/shard_map/all_gather | solution.py:1400
  7.9 106.9 %all-gather.11.cloned.1.call-start = ((), (), s32[]{:S(2)}) async-start(), calls=%async_computation.1 | async-start | bytes 6291456 | tf_op jit(solution)/shard_map/all_gather | solution.py:1402
  14.0 100.9 %all-gather.13.cloned.1.call-start = ((), (), s32[]{:S(2)}) async-start(), calls=%async_computation.2 | async-start | bytes 6291456 | tf_op jit(solution)/shard_map/all_gather | solution.py:1402
  14.7 100.1 %all-gather.15.cloned.1.call-start = ((), (), s32[]{:S(2)}) async-start(), calls=%async_computation.3 | async-start | bytes 6291456 | tf_op jit(solution)/shard_map/all_gather | solution.py:1403
  15.3 5.8 %copy-start.28 = (bf16[512]{0:T(512)(128)(2,1)S(1)}, bf16[512]{0:T(512)(128)(2,1)}, u32[]{:S(2)}) copy-start(bf16[512]{0:T(512)(128)(2,1)} %param.22) | copy-start | bytes 3076
  15.3 5.8 %copy-start.29 = (bf16[512]{0:T(512)(128)(2,1)S(1)}, bf16[512]{0:T(512)(128)(2,1)}, u32[]{:S(2)}) copy-start(bf16[512]{0:T(512)(128)(2,1)} %param.25) | copy-start | bytes 3076
  15.3 5.8 %copy-start.30 = (bf16[512]{0:T(512)(128)(2,1)S(1)}, bf16[512]{0:T(512)(128)(2,1)}, u32[]{:S(2)}) copy-start(bf16[512]{0:T(512)(128)(2,1)} %param.27) | copy-start | bytes 3076
  15.3 7.4 %copy-start.26 = (bf16[1024]{0:T(1024)(128)(2,1)S(1)}, bf16[1024]{0:T(1024)(128)(2,1)}, u32[]{:S(2)}) copy-start(bf16[1024]{0:T(1024)(128)(2,1)} %param.29) | copy-start | bytes 6148
  15.3 7.4 %copy-start.27 = (bf16[1024]{0:T(1024)(128)(2,1)S(1)}, bf16[1024]{0:T(1024)(128)(2,1)}, u32[]{:S(2)}) copy-start(bf16[1024]{0:T(1024)(128)(2,1)} %param.19) | copy-start | bytes 6148
  15.3 7.4 %copy-start.20 = (bf16[160,512]{1,0:T(8,128)(2,1)S(1)}, bf16[160,512]{1,0:T(8,128)(2,1)}, u32[]{:S(2)}) copy-start(bf16[160,512]{1,0:T(8,128)(2,1)} %param.23) | copy-start | bytes 491524
  15.4 7.4 %copy-start.21 = (bf16[128,512]{1,0:T(8,128)(2,1)S(1)}, bf16[128,512]{1,0:T(8,128)(2,1)}, u32[]{:S(2)}) copy-start(bf16[128,512]{1,0:T(8,128)(2,1)} %param.24) | copy-start | bytes 393220
  15.4 7.4 %copy-start.24 = (bf16[16,512]{1,0:T(8,128)(2,1)S(1)}, bf16[16,512]{1,0:T(8,128)(2,1)}, u32[]{:S(2)}) copy-start(bf16[16,512]{1,0:T(8,128)(2,1)} %param.26) | copy-start | bytes 49156
  15.4 7.4 %copy-start.25 = (bf16[4,512]{1,0:T(4,128)(2,1)S(1)}, bf16[4,512]{1,0:T(4,128)(2,1)}, u32[]{:S(2)}) copy-start(bf16[4,512]{1,0:T(4,128)(2,1)} %param.21) | copy-start | bytes 12292
  23.6 38.9 %copy-start.31 = (s32[2]{0:T(128)S(1)}, s32[2]{0:T(128)}, u32[]{:S(2)}) copy-start(s32[2]{0:T(128)} %param.17) | copy-start | bytes 28
  23.6 38.9 %copy-start.9 = (bf16[2,256,2048]{2,1,0:T(8,128)(2,1)S(1)}, bf16[2,256,2048]{2,1,0:T(8,128)(2,1)}, u32[]{:S(2)}) copy-start(bf16[2,256,2048]{2,1,0:T(8,128)(2,1)} %param.16) | copy-start | bytes 6291460
  235.7 4.4 copy-start.16
  358.6 5.1 %copy-start.32 = (bf16[512,2048]{1,0:T(8,128)(2,1)S(1)}, bf16[512,2048]{1,0:T(8,128)(2,1)}, u32[]{:S(2)}) copy-start(bf16[512,2048]{1,0:T(8,128)(2,1)} %get-tuple-element.82) | copy-start | bytes 6291460
  358.6 5.1 %copy-start.34 = (bf16[512,2048]{1,0:T(8,128)(2,1)S(1)}, bf16[512,2048]{1,0:T(8,128)(2,1)}, u32[]{:S(2)}) copy-start(bf16[512,2048]{1,0:T(8,128)(2,1)} %get-tuple-element.79) | copy-start | bytes 6291460
  358.6 16.4 %slice-start = ((s8[8388608]{0:T(1024)(128)(4,1)}), s8[4194304]{0:T(1024)(128)(4,1)S(1)}, s32[]{:S(2)}) async-start(s8[8388608]{0:T(1024)(128)(4,1)} %bitcast.96), calls=%async_computation.4 | async-start | bytes 8388608
  363.7 6.9 %copy-start.8 = (bf16[512,1024]{1,0:T(8,128)(2,1)S(1)}, bf16[512,1024]{1,0:T(8,128)(2,1)}, u32[]{:S(2)}) copy-start(bf16[512,1024]{1,0:T(8,128)(2,1)} %copy-done.7) | copy-start | bytes 3145732
  363.7 6.9 %copy-start.33 = (bf16[512,2048]{1,0:T(8,128)(2,1)S(1)}, bf16[512,2048]{1,0:T(8,128)(2,1)}, u32[]{:S(2)}) copy-start(bf16[512,2048]{1,0:T(8,128)(2,1)} %get-tuple-element.62) | copy-start | bytes 6291460
  363.7 11.3 %slice-start.1 = ((s8[8388608]{0:T(1024)(128)(4,1)}), s8[4194304]{0:T(1024)(128)(4,1)S(1)}, s32[]{:S(2)}) async-start(s8[8388608]{0:T(1024)(128)(4,1)} %bitcast.96), calls=%async_computation.5 | async-start | bytes 8388608
  370.6 4.4 copy-start.10
  467.0 4.3 copy-start.14
  (17 other events, 40.6 us)
Sparse Core Ops, SparseCore 0:
  9.6 16.3 all-gather.8
  27.5 14.8 all-gather.10
  44.5 14.8 all-gather.12
  60.8 14.8 all-gather.14

commit v6 on v5

--- a/solution.py
+++ b/solution.py
@@ -34,7 +34,7 @@
 
 
 class Line:
-    lag = 3
+    lag = 2
     ahead = 4
 
     def __init__(self, shape, chunk, epilogue, extras, out_dtype):
@@ -123,7 +123,7 @@
     def first(self, c):
         at = self.at(c)
         self.copy_a(c).wait_recv()
-        self.pair[at, :] = (self.p[at, :].astype(f32) + self.got_a[at, :].astype(f32)).astype(bf16)
+        self.pair[at, :] = self.p[at, :] + self.got_a[at, :]
         self.copy_b(c).start()
 
     def second(self, c):
@@ -282,11 +282,10 @@
             kept = self.own[a][where]
         else:
             kept = self.landed[j - 1][a][self.pick(self.rest(order, j), d, self.mine[d], a, c)]
-        total = kept.astype(f32) + self.landed[j][a][where].astype(f32)
         if j == self.depth - 1:
-            self.shares[a][self.spot(a, c), :] = total
+            self.shares[a][self.spot(a, c), :] = kept.astype(f32) + self.landed[j][a][where].astype(f32)
         else:
-            self.landed[j][a][where] = total.astype(bf16)
+            self.landed[j][a][where] = kept + self.landed[j][a][where]
             self.copy(j + 1, a, c, order).start()
 
     def each(self, i, fn):
@@ -345,27 +344,40 @@
         line.begin(barrier, share.greet(barrier), line_too)
         share.start()
 
+        def tail_copy(k):
+            to = (line.mate, line.across)[k]
+            source = shares[-1].at[pl.ds(shares[-1].shape[0] - 8, 8)] if k == 0 else tail.at[2]
+            return pltpu.make_async_remote_copy(
+                source, tail.at[k], tail_send.at[k], tail_recv.at[k], device_id={"tp": to}, device_id_type=MESH
+            )
+
+        def tail_step(k):
+            last = pl.ds(shares[-1].shape[0] - 8, 8)
+            if k > 0:
+                tail_copy(k - 1).wait()
+            if k == 1:
+                tail[2] = shares[-1][last, :] + tail[0]
+            if k == 2:
+                shares[-1][last, :] = tail[2] + tail[1]
+            else:
+                tail_copy(k).start()
+
+        ready = (share.parts[-1] + 1) // 2 + share.lag * (share.depth - 1) if n_sc else 0
+
         def turn(i, _):
             for parity in (0, 1):
                 line.tick(2 * i + parity)
             share.tick(i)
+            for k in range(3 if line_too else 0):
+
+                @pl.when(i == ready + k)
+                def _():
+                    tail_step(k)
+
             return 0
 
-        turns = (line.ticks() + 1) // 2
-        lax.fori_loop(0, max(turns, share.turns) if n_sc else turns, turn, 0)
-        if line_too:
-            height = shares[-1].shape[0]
-            last = pl.ds(height - 8, 8)
-            for k, to in enumerate((line.mate, line.across)):
-                copy = pltpu.make_async_remote_copy(
-                    shares[-1].at[last] if k == 0 else tail.at[2], tail.at[k], tail_send.at[k], tail_recv.at[k],
-                    device_id={"tp": to}, device_id_type=MESH,
-                )
-                copy.start()
-                copy.wait()
-                if k == 0:
-                    tail[2] = shares[-1][last, :] + tail[0]
-            shares[-1][last, :] = tail[2] + tail[1]
+        turns = max((line.ticks() + 1) // 2, share.turns if n_sc else 0, ready + 3 if line_too else 0)
+        lax.fori_loop(0, turns, turn, 0)
         line.finish()
         share.finish()
 
@@ -1045,7 +1057,7 @@
     fore = Line(mixed_part.shape, chunk, norm_end, [], bf16)
     after = Line(mixed_part.shape, chunk, norm_back_end, [], bf16)
     n_line = len(fore.scratch())
-    behind = 6
+    behind = 5
     wtile = 256
 
     def kernel(
@@ -1205,7 +1217,7 @@
     )(mixed_part, hidden, gain, ffn_grad, gate_w[0], gate_w[1], down_parts)
 
 
-def scan_tail(through_b, through_decay, sums, decay_grad, scan_grad, step_pre, pre_act, act, padded, z_half, low_all, small, ident,
+def scan_tail(through_b, through_decay, sums, decay_grad, scan_grad, step_pre, pre_act, act, padded, z_half, low_all, small, normed, in_w, scatters, ident,
               seqs, low_len, rank, states, taps):
     rows, inner = act.shape
     local = rows // seqs
@@ -1219,15 +1231,28 @@
     lines = -(-(at + states + taps + 3) // 8) * 8
     height = -(-(lines + 8) // 32) * 32
     over = 8
-
-    def kernel(
-        tb_ref, sd_ref, sums_ref, dec_ref, sg_ref, sp_ref, pre_ref, act_ref, ext_ref, zg_ref, low_ref, small_ref,
-        conv_ref, blocks_ref,
-        low_out, low_t, step_g, low_acc, grads, pre_g, conv_f, edge, edge_out, edge_sem, *rest
+    width = normed.shape[1]
+    dtile = width // 8
+    share = Halving(scatters, 32, 1)
+    n_sc, n_share = len(scatters), len(share.scratch())
+
+    def kernel(*refs):
+        n_in = 14 + n_sc
+        main(*refs[:14], *refs[n_in : n_in + 4], refs[14:n_in], refs[n_in + 4 : n_in + 4 + n_sc],
+             refs[n_in + 4 + n_sc : n_in + 4 + n_sc + n_share], *refs[n_in + 4 + n_sc + n_share :])
+
+    def main(
+        tb_ref, sd_ref, sums_ref, dec_ref, sg_ref, sp_ref, pre_ref, act_ref, ext_ref, zg_ref, low_ref, small_ref, n_ref, w_ref,
+        iw_out, first_ref, gsum_ref, blocks_ref, full, shares, share_scratch,
+        conv_ref, w_v, acc, stage, w_sem, stage_sem, low_out, low_t, step_g, low_acc, grads, pre_g, conv_f, edge, edge_out, edge_sem, *rest
     ):
         ctx = lax.axis_index("ctx")
         barrier = pltpu.get_barrier_semaphore()
         line.bind(rest[0], [], low_out, [], list(rest))
+        share.bind(full, shares, share_scratch)
+        w_load = pltpu.make_async_copy(w_ref, w_v, w_sem)
+        w_load.start()
+        met = share.greet(barrier)
         pl.semaphore_signal(barrier, inc=1, device_id={"ctx": lax.rem(ctx + 1, pieces)}, device_id_type=MESH)
 
         def flat(ref, j, first, count):
@@ -1264,8 +1289,30 @@
         lax.fori_loop(0, tiles, size_tile, 0)
         line.p[0:rank, :] = low_acc[...].astype(bf16)
         line.p[rank : rank + 2 * states, :] = sums_ref[...].astype(bf16)
-        line.greet(barrier, 1)
+        line.greet(barrier, 1 + met)
         line.start()
+        share.start()
+
+        def save(i):
+            c, d = 1 - i // 8, i % 8
+            return pltpu.make_async_copy(
+                stage.at[i % 2], iw_out.at[pl.ds(d * dtile, dtile), pl.ds(c * inner, inner)], stage_sem.at[i % 2]
+            )
+
+        def weight_piece(i, right):
+            c, here = 1 - i // 8, slice((i % 8) * dtile, (i % 8 + 1) * dtile)
+            if i >= 2:
+                save(i - 2).wait()
+            stage[i % 2] = inner_rows(n_ref[:, here], right[...]).astype(bf16)
+            save(i).start()
+            value = outer_cols(right[...], w_v[c, here, :])
+            if i < 8:
+                acc[:, here] = value
+            else:
+                value = (acc[:, here] + value).astype(bf16)
+                first_ref[:, here] = value
+                product = value.astype(f32) * n_ref[:, here].astype(f32)
+                gsum_ref[:, here] = jnp.sum(product.reshape(rows // 8, 8, dtile), axis=0)
 
         def step_tile(j, _):
             here = cols(j)
@@ -1274,8 +1321,15 @@
 
         lax.fori_loop(0, tiles, step_tile, 0)
         grads[at : at + states, :] = dec_ref[...]
+        w_load.wait()
+        early = 8 // line.ticks()
         for c in range(line.ticks()):
+            for i in range(early):
+                weight_piece(c * early + i, zg_ref)
             line.tick(c)
+            share.tick(c)
+        for i in range(early * line.ticks(), 8):
+            weight_piece(i, zg_ref)
         line.finish()
 
         def pre_tile(j, _):
@@ -1309,6 +1363,7 @@
             return 0
 
         lax.fori_loop(0, tiles, pre_tile, 0)
+        share.tick(line.ticks())
         for seq in range(seqs):
             edge_out[seq] = pre_g[seq * (local + over) : seq * (local + over) + over, :]
         copy = pltpu.make_async_remote_copy(
@@ -1338,17 +1393,35 @@
             return 0
 
         lax.fori_loop(0, tiles, conv_tile, 0)
-        conv_ref[:, inner:] = zg_ref[...]
+        for i in range(8, 16):
+            if line.ticks() + i - 7 < share.turns:
+                share.tick(line.ticks() + i - 7)
+            weight_piece(i, conv_ref)
+        for i in range(line.ticks() + 9, share.turns):
+            share.tick(i)
+        save(14).wait()
+        save(15).wait()
+        share.finish()
 
     return pl.pallas_call(
         kernel,
         out_shape=[
-            jax.ShapeDtypeStruct((rows, 2 * inner), bf16),
+            jax.ShapeDtypeStruct((width, 2 * inner), bf16),
+            jax.ShapeDtypeStruct((rows, width), bf16),
+            jax.ShapeDtypeStruct((8, width), f32),
             jax.ShapeDtypeStruct((places * height, lane), bf16),
-        ],
-        in_specs=[VMEM] * 12,
-        out_specs=[VMEM] * 2,
-        scratch_shapes=[
+        ]
+        + share.results(),
+        in_specs=[VMEM] * 13 + [HBM] * (1 + n_sc),
+        out_specs=[HBM] + [VMEM] * (3 + n_sc),
+        scratch_shapes=share.scratch()
+        + [
+            pltpu.VMEM((rows, inner), bf16),
+            pltpu.VMEM(in_w.shape, bf16),
+            pltpu.VMEM((rows, width), f32),
+            pltpu.VMEM((2, dtile, inner), bf16),
+            pltpu.SemaphoreType.DMA,
+            pltpu.SemaphoreType.DMA((2,)),
             pltpu.VMEM((low_len, rows), bf16),
             pltpu.VMEM((rank, rows), bf16),
             pltpu.VMEM((rows, inner), bf16),
@@ -1362,9 +1435,9 @@
         ]
         + line.scratch(),
         compiler_params=pltpu.CompilerParams(
-            collective_id=ident, has_side_effects=True, vmem_limit_bytes=56 << 20
+            collective_id=ident, has_side_effects=True, vmem_limit_bytes=60 << 20
         ),
-    )(through_b, through_decay, sums, decay_grad, scan_grad, step_pre, pre_act, act, padded, z_half, low_all, small), height
+    )(through_b, through_decay, sums, decay_grad, scan_grad, step_pre, pre_act, act, padded, z_half, low_all, small, normed, in_w, *share.folded), height
 
 
 def body(
@@ -1444,13 +1517,12 @@
     decay_log_grad = decay_sum.reshape(states, inner) * decay_rate
     sums = jnp.concatenate([v[:, 0].reshape(rows, states).T for v in (b_sums, c_sums)], axis=0)
     z_half = z_grad.astype(bf16)
-    (project_grad, small_blocks), small_height = scan_tail(
-        through_b, through_decay, sums, decay_log_grad, scan_grad, step_pre, pre_act, act_half, padded, z_half, low_all, small, 7,
+    (in_weight_grad, first_part, gain_one_sum, small_blocks), small_height = scan_tail(
+        through_b, through_decay, sums, decay_log_grad, scan_grad, step_pre, pre_act, act_half, padded, z_half, low_all, small, normed_one, in_w,
+        [], 7,
         seqs, low_len, rank, states, taps,
     )
-    in_weight_grad = inner_rows(normed_one, project_grad).astype(bf16)
-    first_part = sum(outer_cols(project_grad[:, c * inner : (c + 1) * inner], in_w[c]) for c in range(2)).astype(bf16)
-    norm_gain_grad = jnp.sum(first_part.astype(f32) * source * rms_scale(source), axis=0)
+    norm_gain_grad = jnp.sum(gain_one_sum, axis=0) / gain_one[0]
     places, share = shards * pieces, width // (shards * pieces)
     lane = inner // places
     gain_rows = -(-2 * share // lane)

time: 498 us -> 484 us (0.972)
  matrix products: 28.5 us -> 14.1 us
    pallas_call x1, Pallas kernels: 26.7 us -> 48.4 us  [scan_tail(): pl.pallas_call(kernel, out_shape=[jax.ShapeDtypeStruct((width, 2 * inner)...]
    pallas_call x1, Pallas kernels: 80.3 us -> 67.7 us  [tp_sum(): pl.pallas_call(kernel, out_shape=[jax.ShapeDtypeStruct(partial.shape, out...]
    dot_general x4 -> x2, matrix products: 17.2 us -> 8.11 us  [outer_cols(): lax.dot_general(left, right, (((1,), (1,)), ((), ())), preferred_element_...]
    pallas_call x1, Pallas kernels: 121 us -> 115 us  [feed_forward(): pl.pallas_call(kernel, out_shape=[half, wide, half, wide, sds((8, width),...]
    dot_general x2 -> x1, matrix products: 11.3 us -> 5.99 us  [inner_rows(): lax.dot_general(left, right, (((0,), (0,)), ((), ())), preferred_element_...]
    unnamed x86 -> x69, local copies, waits for them, and re-layouts: 17.9 us -> 19.2 us
where the time goes in v6:
time: 484 us; the launch traced here: 478 us
  Pallas kernels  395 us (82%)
  local copies, waits for them, and re-layouts  41.2 us (9%)
  between operations  14.4 us (3%)
  matrix products  14.1 us (3%)
  other arithmetic  11 us (2%)
    pallas_call x1, Pallas kernels, feed_forward(): pl.pallas_call(kernel, out_shape=[half, wide, half, wide, sds((8, width),...  115 us
    pallas_call x1, Pallas kernels, scan_backward(): pl.pallas_call(kernel, out_shape=[flat, flat, sums, sums, jax.ShapeDtypeS...  80.6 us
    pallas_call x1, Pallas kernels, tp_sum(): pl.pallas_call(kernel, out_shape=[jax.ShapeDtypeStruct(partial.shape, out...  67.7 us
    pallas_call x1, Pallas kernels, scan_tail(): pl.pallas_call(kernel, out_shape=[jax.ShapeDtypeStruct((width, 2 * inner)...  48.4 us
    pallas_call x1, Pallas kernels, scan_forward(): pl.pallas_call(kernel, out_shape=[jax.ShapeDtypeStruct((rows, channels),...  45.9 us
    pallas_call x1, Pallas kernels, front(): pl.pallas_call(kernel, out_shape=[sds((2, shards * part, inner), bf16), s...  37.5 us
    unnamed x69, local copies, waits for them, and re-layouts  19.2 us
  transfers between devices with their start and end apart: 4, of which 0 were waited for; matrix products, arithmetic and copies ran while one was open for 4% of the time, Pallas kernels for 17%

profile of v6, /device:TPU:0, one launch (start us, length us, event | category | flops | bytes accessed | tf_op | source)
XLA Modules:
  0.0 477.7 jit_solution(4210679859987429696)
XLA Ops:
  8.7 3.5 copy.47
  12.2 2.5 fusion.21
  15.5 1.6 slice.72.tail_ref
  17.1 6.3 %copy.48 = bf16[1024,2,1024]{2,0,1:T(8,128)(2,1)} copy(bf16[1024,2,1024]{2,1,0:T(2,128)(2,1)} %param.20) | data formatting | bytes 8388608 | tf_op args[4]
  24.3 37.5 %shard_map.271 = (bf16[2,2048,1024]{2,1,0:T(8,128)(2,1)}, bf16[352,1024]{1,0:T(8,128)(2,1)}, bf16[16,2048]{1,0:T(8,128)(2,1)}, bf16[512,2048]{1,0:T(8,128)(2,1)}...) custom-call(bf16[512,2048]{1,0:T(8,128)(2,1)} %bitcast.54, ...), custom_call_target="tpu_custom_call" | custom-call | tf_op jit(solution)/shard_map/pallas_call | solution.py:575
  62.6 1.4 slice_convert_fusion
  64.1 1.7 fusion.fg_ref
  66.0 45.9 %shard_map.272 = (f32[512,1024]{1,0:T(8,128)S(1)}, bf16[512,1024]{1,0:T(8,128)(2,1)S(1)}, bf16[512,2048]{1,0:T(8,128)(2,1)}, f32[512,1024]{1,0:T(8,128)}, f32[51...) custom-call(f32[160,512]{1,0:T(8,128)S(1)} %copy-done.2, ...), custom_call_target="tpu_custom_call" | custom-call | tf_op jit(solution)/shard_map/pallas_call | solution.py:810
  114.8 114.8 %shard_map.273 = (bf16[512,2048]{1,0:T(8,128)(2,1)}, f32[512,2048]{1,0:T(8,128)}, bf16[512,2048]{1,0:T(8,128)(2,1)}, f32[512,2048]{1,0:T(8,128)}, f32[8,2048]{1,...) custom-call(bf16[512,2048]{1,0:T(8,128)(2,1)} %get-tuple-element.62.p_ref, ...), custom_call_target="tpu_custom_call" | custom-call | tf_op jit(solution)/shard_map/pallas_call | solution.py:1190
  229.7 3.3 fusion.1
  234.0 4.8 multiply_convert_fusion
  238.8 80.6 %shard_map.274 = (f32[4096,128]{1,0:T(8,128)}, f32[4096,128]{1,0:T(8,128)}, f32[32,8,256]{2,1,0:T(8,128)}, f32[32,8,256]{2,1,0:T(8,128)}, f32[16,8,128]{2,1,0:T(...) custom-call(f32[4096,128]{1,0:T(8,128)} %get-tuple-element.60.refs_0_, ...), custom_call_target="tpu_custom_call" | custom-call | tf_op jit(solution)/shard_map/pallas_call | solution.py:1023
  319.4 1.5 bitcast_multiply_fusion.refs_3_
  323.2 48.4 %shard_map.275 = (bf16[2048,2048]{1,0:T(8,128)(2,1)}, bf16[512,2048]{1,0:T(8,128)(2,1)}, f32[8,2048]{1,0:T(8,128)}, bf16[2560,128]{1,0:T(8,128)(2,1)}) custom-call(f32[4096,128]{1,0:T(8,128)} %get-tuple-element.72.refs_0_, f32[4096,128]{1,0:T(8,128)} %get-tuple-element.73.refs_1_, f32[32,512]{1,0:T(8,128)} %pad_maximum_fusion.refs_2_, ...), custom_call_target="tpu_custom_call" | custom-call | tf_op jit(solution)/shard_map/pallas_call | solution.py:1406
  372.5 6.0 %convolution_convert_fusion = bf16[2048,1024]{1,0:T(8,128)(2,1)} fusion(bf16[512,2048]{1,0:T(8,128)(2,1)} %get-tuple-element.64, bf16[512,1024]{1,0:T(8,128)(2,1)S(1)} %copy-done.8), kind=kOutput, calls=%fused_computation.4 | convolution fusion | flops 2149580800 | bytes 7340032 | tf_op jit(solution)/shard_map/dot_general | solution.py:20
  379.2 67.7 %shard_map.276 = (bf16[512,2048]{1,0:T(8,128)(2,1)}, f32[256,2048]{1,0:T(8,128)}, f32[256,1024]{1,0:T(8,128)}, f32[320,128]{1,0:T(8,128)}, f32[16,128]{1,0:T(8,128)}) custom-call(bf16[512,2048]{1,0:T(8,128)(2,1)} %get-tuple-element.83.refs_0_, bf16[512,2048]{1,0:T(8,128)(2,1)} %bitcast.56, f32[1,2048]{1,0:T(1,128)} %copy-done.18, ...), custom_call_target="tpu_custom_call" | custom-call | tf_op jit(solution)/shard_map/pallas_call | solution.py:388
  450.8 1.5 slice.89
  452.2 1.5 slice.88
  455.1 1.3 slice_bitcast_fusion
  456.4 2.5 copy.39
  458.9 2.5 convert.14
  461.5 4.0 reshape.126
  465.4 4.1 reshape.127
  469.6 1.3 copy.55
  (102 shorter events, 16.9 us)
Async XLA Ops:
  7.2 58.6 %all-gather.9.cloned.1.call-start = ((), (), s32[]{:S(2)}) async-start(), calls=%async_computation | async-start | bytes 6291456 | tf_op jit(solution)/shard_map/all_gather | solution.py:1473
  7.9 106.9 %all-gather.15.cloned.1.call-start = ((), (), s32[]{:S(2)}) async-start(), calls=%async_computation.3 | async-start | bytes 6291456 | tf_op jit(solution)/shard_map/all_gather | solution.py:1476
  8.7 106.2 %all-gather.13.cloned.1.call-start = ((), (), s32[]{:S(2)}) async-start(), calls=%async_computation.2 | async-start | bytes 6291456 | tf_op jit(solution)/shard_map/all_gather | solution.py:1475
  14.8 100.1 %all-gather.11.cloned.1.call-start = ((), (), s32[]{:S(2)}) async-start(), calls=%async_computation.1 | async-start | bytes 6291456 | tf_op jit(solution)/shard_map/all_gather | solution.py:1475
  17.1 6.3 %copy-start.16 = (bf16[160,512]{1,0:T(8,128)(2,1)S(1)}, bf16[160,512]{1,0:T(8,128)(2,1)}, u32[]{:S(2)}) copy-start(bf16[160,512]{1,0:T(8,128)(2,1)} %param.23) | copy-start | bytes 491524
  17.1 6.3 %copy-start.17 = (bf16[128,512]{1,0:T(8,128)(2,1)S(1)}, bf16[128,512]{1,0:T(8,128)(2,1)}, u32[]{:S(2)}) copy-start(bf16[128,512]{1,0:T(8,128)(2,1)} %param.24) | copy-start | bytes 393220
  17.1 6.4 %copy-start.21 = (bf16[16,512]{1,0:T(8,128)(2,1)S(1)}, bf16[16,512]{1,0:T(8,128)(2,1)}, u32[]{:S(2)}) copy-start(bf16[16,512]{1,0:T(8,128)(2,1)} %param.26) | copy-start | bytes 49156
  17.1 6.4 %copy-start.22 = (bf16[4,512]{1,0:T(4,128)(2,1)S(1)}, bf16[4,512]{1,0:T(4,128)(2,1)}, u32[]{:S(2)}) copy-start(bf16[4,512]{1,0:T(4,128)(2,1)} %param.21) | copy-start | bytes 12292
  24.3 39.8 %copy-start.12 = (bf16[2,256,2048]{2,1,0:T(8,128)(2,1)S(1)}, bf16[2,256,2048]{2,1,0:T(8,128)(2,1)}, u32[]{:S(2)}) copy-start(bf16[2,256,2048]{2,1,0:T(8,128)(2,1)} %param.18) | copy-start | bytes 6291460
  62.6 3.2 copy-start.3
  64.0 314.5 %copy-start.18 = (f32[1,2048]{1,0:T(1,128)}, f32[1,2048]{1,0:T(1,128)S(1)}, u32[]{:S(2)}) copy-start(f32[1,2048]{1,0:T(1,128)S(1)} %get-tuple-element.134.refs_2_) | copy-start | bytes 24580
  64.1 1.8 copy-start
  64.1 1.8 copy-start.1
  64.1 1.9 copy-start.2
  112.5 1.3 copy-start.5
  229.6 3.4 copy-start.6
  229.6 3.8 copy-start.9
  229.6 4.4 copy-start.13
  238.8 83.8 %copy-start.20 = (f32[8,2048]{1,0:T(8,128)S(1)}, f32[8,2048]{1,0:T(8,128)}, u32[]{:S(2)}) copy-start(f32[8,2048]{1,0:T(8,128)} %get-tuple-element.89) | copy-start | bytes 196612
  323.2 49.3 %copy-start.8 = (bf16[512,1024]{1,0:T(8,128)(2,1)S(1)}, bf16[512,1024]{1,0:T(8,128)(2,1)}, u32[]{:S(2)}) copy-start(bf16[512,1024]{1,0:T(8,128)(2,1)} %copy-done.7) | copy-start | bytes 3145732
  372.5 6.0 %copy-start.19 = (f32[1,2048]{1,0:T(1,128)S(1)}, f32[1,2048]{1,0:T(1,128)}, u32[]{:S(2)}) copy-start(f32[1,2048]{1,0:T(1,128)} %get-tuple-element.135.gain_ref) | copy-start | bytes 24580
  379.2 74.6 %copy-start.14 = (f32[256,1024]{1,0:T(8,128)S(1)}, f32[256,1024]{1,0:T(8,128)}, u32[]{:S(2)}) copy-start(f32[256,1024]{1,0:T(8,128)} %get-tuple-element.96) | copy-start | bytes 3145732
  453.8 5.2 %copy-start.10 = (bf16[512,2048]{1,0:T(8,128)(2,1)S(1)}, bf16[512,2048]{1,0:T(8,128)(2,1)}, u32[]{:S(2)}) copy-start(bf16[512,2048]{1,0:T(8,128)(2,1)} %get-tuple-element.90) | copy-start | bytes 6291460
  465.4 4.1 copy-start.11
  (9 other events, 6.9 us)
Sparse Core Ops, SparseCore 0:
  9.6 16.3 all-gather.8
  27.5 14.8 all-gather.14
  44.5 14.8 all-gather.12
  60.8 14.8 all-gather.10

commit v7 on v6

--- a/solution.py
+++ b/solution.py
@@ -1293,20 +1293,27 @@
         line.start()
         share.start()
 
-        def save(i):
-            c, d = 1 - i // 8, i % 8
+        def save(i, c):
             return pltpu.make_async_copy(
-                stage.at[i % 2], iw_out.at[pl.ds(d * dtile, dtile), pl.ds(c * inner, inner)], stage_sem.at[i % 2]
+                stage.at[i % 2],
+                iw_out.at[pl.ds(pl.multiple_of(i * dtile, dtile), dtile), pl.ds(c * inner, inner)],
+                stage_sem.at[i % 2],
             )
 
-        def weight_piece(i, right):
-            c, here = 1 - i // 8, slice((i % 8) * dtile, (i % 8 + 1) * dtile)
-            if i >= 2:
-                save(i - 2).wait()
+        def weight_piece(i, right, c):
+            here = pl.ds(pl.multiple_of(i * dtile, dtile), dtile)
+            if c == 0:
+                save(i, c).wait()
+            else:
+
+                @pl.when(i >= 2)
+                def _():
+                    save(i, c).wait()
+
             stage[i % 2] = inner_rows(n_ref[:, here], right[...]).astype(bf16)
-            save(i).start()
+            save(i, c).start()
             value = outer_cols(right[...], w_v[c, here, :])
-            if i < 8:
+            if c == 1:
                 acc[:, here] = value
             else:
                 value = (acc[:, here] + value).astype(bf16)
@@ -1323,13 +1330,16 @@
         grads[at : at + states, :] = dec_ref[...]
         w_load.wait()
         early = 8 // line.ticks()
-        for c in range(line.ticks()):
+
+        def beside(c, _):
             for i in range(early):
-                weight_piece(c * early + i, zg_ref)
+                weight_piece(c * early + i, zg_ref, 1)
             line.tick(c)
-            share.tick(c)
+            return 0
+
+        lax.fori_loop(0, line.ticks(), beside, 0)
         for i in range(early * line.ticks(), 8):
-            weight_piece(i, zg_ref)
+            weight_piece(i, zg_ref, 1)
         line.finish()
 
         def pre_tile(j, _):
@@ -1363,7 +1373,6 @@
             return 0
 
         lax.fori_loop(0, tiles, pre_tile, 0)
-        share.tick(line.ticks())
         for seq in range(seqs):
             edge_out[seq] = pre_g[seq * (local + over) : seq * (local + over) + over, :]
         copy = pltpu.make_async_remote_copy(
@@ -1393,14 +1402,16 @@
             return 0
 
         lax.fori_loop(0, tiles, conv_tile, 0)
-        for i in range(8, 16):
-            if line.ticks() + i - 7 < share.turns:
-                share.tick(line.ticks() + i - 7)
-            weight_piece(i, conv_ref)
-        for i in range(line.ticks() + 9, share.turns):
+
+        def conv_piece(i, _):
+            weight_piece(i, conv_ref, 0)
+            return 0
+
+        lax.fori_loop(0, 8, conv_piece, 0)
+        for i in range(share.turns if n_sc else 0):
             share.tick(i)
-        save(14).wait()
-        save(15).wait()
+        save(6, 0).wait()
+        save(7, 0).wait()
         share.finish()
 
     return pl.pallas_call(

time: 484 us -> 472 us (0.975)
  Pallas kernels: 395 us -> 385 us
    pallas_call x1, Pallas kernels: 48.4 us -> 39.5 us  [scan_tail(): pl.pallas_call(kernel, out_shape=[jax.ShapeDtypeStruct((width, 2 * inner)...]
  transfers between devices with their start and end apart: 4 -> 4, of which waited for: 0 -> 0; matrix products, arithmetic and copies ran while one was open for 4% -> 4% of each run, Pallas kernels for 17% -> 18%
where the time goes in v7:
time: 472 us; the launch traced here: 467 us
  Pallas kernels  385 us (82%)
  local copies, waits for them, and re-layouts  41.3 us (9%)
  between operations  14.2 us (3%)
  matrix products  14.1 us (3%)
  other arithmetic  11 us (2%)
    pallas_call x1, Pallas kernels, feed_forward(): pl.pallas_call(kernel, out_shape=[half, wide, half, wide, sds((8, width),...  115 us
    pallas_call x1, Pallas kernels, scan_backward(): pl.pallas_call(kernel, out_shape=[flat, flat, sums, sums, jax.ShapeDtypeS...  80.2 us
    pallas_call x1, Pallas kernels, tp_sum(): pl.pallas_call(kernel, out_shape=[jax.ShapeDtypeStruct(partial.shape, out...  67 us
    pallas_call x1, Pallas kernels, scan_forward(): pl.pallas_call(kernel, out_shape=[jax.ShapeDtypeStruct((rows, channels),...  45.8 us
    pallas_call x1, Pallas kernels, scan_tail(): pl.pallas_call(kernel, out_shape=[jax.ShapeDtypeStruct((width, 2 * inner)...  39.5 us
    pallas_call x1, Pallas kernels, front(): pl.pallas_call(kernel, out_shape=[sds((2, shards * part, inner), bf16), s...  37.5 us
    unnamed x69, local copies, waits for them, and re-layouts  19.2 us
  transfers between devices with their start and end apart: 4, of which 0 were waited for; matrix products, arithmetic and copies ran while one was open for 4% of the time, Pallas kernels for 18%

profile of v7, /device:TPU:0, one launch (start us, length us, event | category | flops | bytes accessed | tf_op | source)
XLA Modules:
  0.0 467.4 jit_solution(826901685184186760)
XLA Ops:
  8.7 3.5 copy.47
  12.2 2.5 fusion.21
  15.5 1.6 slice.72.tail_ref
  17.1 6.3 %copy.48 = bf16[1024,2,1024]{2,0,1:T(8,128)(2,1)} copy(bf16[1024,2,1024]{2,1,0:T(2,128)(2,1)} %param.20) | data formatting | bytes 8388608 | tf_op args[4]
  24.3 37.5 %shard_map.271 = (bf16[2,2048,1024]{2,1,0:T(8,128)(2,1)}, bf16[352,1024]{1,0:T(8,128)(2,1)}, bf16[16,2048]{1,0:T(8,128)(2,1)}, bf16[512,2048]{1,0:T(8,128)(2,1)}...) custom-call(bf16[512,2048]{1,0:T(8,128)(2,1)} %bitcast.54, ...), custom_call_target="tpu_custom_call" | custom-call | tf_op jit(solution)/shard_map/pallas_call | solution.py:575
  62.6 1.4 slice_convert_fusion
  64.1 1.7 fusion.fg_ref
  66.0 45.8 %shard_map.272 = (f32[512,1024]{1,0:T(8,128)S(1)}, bf16[512,1024]{1,0:T(8,128)(2,1)S(1)}, bf16[512,2048]{1,0:T(8,128)(2,1)}, f32[512,1024]{1,0:T(8,128)}, f32[51...) custom-call(f32[160,512]{1,0:T(8,128)S(1)} %copy-done.2, ...), custom_call_target="tpu_custom_call" | custom-call | tf_op jit(solution)/shard_map/pallas_call | solution.py:810
  114.8 114.8 %shard_map.273 = (bf16[512,2048]{1,0:T(8,128)(2,1)}, f32[512,2048]{1,0:T(8,128)}, bf16[512,2048]{1,0:T(8,128)(2,1)}, f32[512,2048]{1,0:T(8,128)}, f32[8,2048]{1,...) custom-call(bf16[512,2048]{1,0:T(8,128)(2,1)} %get-tuple-element.62.p_ref, ...), custom_call_target="tpu_custom_call" | custom-call | tf_op jit(solution)/shard_map/pallas_call | solution.py:1190
  229.6 3.3 fusion.1
  234.0 4.8 %multiply_convert_fusion = (bf16[512,1024]{1,0:T(8,128)(2,1)}, f32[512,1024]{1,0:T(8,128)}) fusion(f32[512,1024]{1,0:T(8,128)S(1)} %copy-done.13, f32[512,1024]{1,0:T(8,128)S(1)} %copy-done.6, f32[512,1024]{1,0:T(8,128)S(1)} %fusion.1, bf16[2048,1024]{1,0:T(8,128)(2,1)S(1)} %copy-done.9, bf16[512,2048]{1,0:T(8,128)(2,1)} %get-tuple-element.64), kind=kOutput, calls=%fused_computation.9 | convolution fusion | flops 1080557568 | bytes 12582912 | tf_op jit(solution)/shard_map/dot_general | solution.py:24
  238.8 80.2 %shard_map.274 = (f32[4096,128]{1,0:T(8,128)}, f32[4096,128]{1,0:T(8,128)}, f32[32,8,256]{2,1,0:T(8,128)}, f32[32,8,256]{2,1,0:T(8,128)}, f32[16,8,128]{2,1,0:T(...) custom-call(f32[4096,128]{1,0:T(8,128)} %get-tuple-element.60.refs_0_, ...), custom_call_target="tpu_custom_call" | custom-call | tf_op jit(solution)/shard_map/pallas_call | solution.py:1023
  318.9 1.5 bitcast_multiply_fusion.refs_3_
  322.7 39.5 %shard_map.275 = (bf16[2048,2048]{1,0:T(8,128)(2,1)}, bf16[512,2048]{1,0:T(8,128)(2,1)}, f32[8,2048]{1,0:T(8,128)}, bf16[2560,128]{1,0:T(8,128)(2,1)}) custom-call(f32[4096,128]{1,0:T(8,128)} %get-tuple-element.72.refs_0_, f32[4096,128]{1,0:T(8,128)} %get-tuple-element.73.refs_1_, f32[32,512]{1,0:T(8,128)} %pad_maximum_fusion.refs_2_, ...), custom_call_target="tpu_custom_call" | custom-call | tf_op jit(solution)/shard_map/pallas_call | solution.py:1417
  363.2 6.0 %convolution_convert_fusion = bf16[2048,1024]{1,0:T(8,128)(2,1)} fusion(bf16[512,2048]{1,0:T(8,128)(2,1)} %get-tuple-element.64, bf16[512,1024]{1,0:T(8,128)(2,1)S(1)} %copy-done.8), kind=kOutput, calls=%fused_computation.4 | convolution fusion | flops 2149580800 | bytes 7340032 | tf_op jit(solution)/shard_map/dot_general | solution.py:20
  369.9 67.0 %shard_map.276 = (bf16[512,2048]{1,0:T(8,128)(2,1)}, f32[256,2048]{1,0:T(8,128)}, f32[256,1024]{1,0:T(8,128)}, f32[320,128]{1,0:T(8,128)}, f32[16,128]{1,0:T(8,128)}) custom-call(bf16[512,2048]{1,0:T(8,128)(2,1)} %get-tuple-element.83.refs_0_, bf16[512,2048]{1,0:T(8,128)(2,1)} %bitcast.56, f32[1,2048]{1,0:T(1,128)} %copy-done.18, ...), custom_call_target="tpu_custom_call" | custom-call | tf_op jit(solution)/shard_map/pallas_call | solution.py:388
  440.7 1.5 slice.89
  442.1 1.5 slice.88
  445.0 1.3 slice_bitcast_fusion
  446.3 2.5 copy.39
  448.8 2.5 convert.14
  451.4 4.0 reshape.126
  455.4 4.1 reshape.127
  459.5 1.3 copy.55
  (102 shorter events, 16.9 us)
Async XLA Ops:
  7.2 58.7 %all-gather.9.cloned.1.call-start = ((), (), s32[]{:S(2)}) async-start(), calls=%async_computation | async-start | bytes 6291456 | tf_op jit(solution)/shard_map/all_gather | solution.py:1484
  7.9 106.9 %all-gather.15.cloned.1.call-start = ((), (), s32[]{:S(2)}) async-start(), calls=%async_computation.3 | async-start | bytes 6291456 | tf_op jit(solution)/shard_map/all_gather | solution.py:1487
  8.7 106.1 %all-gather.13.cloned.1.call-start = ((), (), s32[]{:S(2)}) async-start(), calls=%async_computation.2 | async-start | bytes 6291456 | tf_op jit(solution)/shard_map/all_gather | solution.py:1486
  14.8 100.0 %all-gather.11.cloned.1.call-start = ((), (), s32[]{:S(2)}) async-start(), calls=%async_computation.1 | async-start | bytes 6291456 | tf_op jit(solution)/shard_map/all_gather | solution.py:1486
  17.1 6.3 %copy-start.16 = (bf16[160,512]{1,0:T(8,128)(2,1)S(1)}, bf16[160,512]{1,0:T(8,128)(2,1)}, u32[]{:S(2)}) copy-start(bf16[160,512]{1,0:T(8,128)(2,1)} %param.23) | copy-start | bytes 491524
  17.1 6.3 %copy-start.17 = (bf16[128,512]{1,0:T(8,128)(2,1)S(1)}, bf16[128,512]{1,0:T(8,128)(2,1)}, u32[]{:S(2)}) copy-start(bf16[128,512]{1,0:T(8,128)(2,1)} %param.24) | copy-start | bytes 393220
  17.1 6.4 %copy-start.21 = (bf16[16,512]{1,0:T(8,128)(2,1)S(1)}, bf16[16,512]{1,0:T(8,128)(2,1)}, u32[]{:S(2)}) copy-start(bf16[16,512]{1,0:T(8,128)(2,1)} %param.26) | copy-start | bytes 49156
  17.1 6.4 %copy-start.22 = (bf16[4,512]{1,0:T(4,128)(2,1)S(1)}, bf16[4,512]{1,0:T(4,128)(2,1)}, u32[]{:S(2)}) copy-start(bf16[4,512]{1,0:T(4,128)(2,1)} %param.21) | copy-start | bytes 12292
  24.3 39.8 %copy-start.12 = (bf16[2,256,2048]{2,1,0:T(8,128)(2,1)S(1)}, bf16[2,256,2048]{2,1,0:T(8,128)(2,1)}, u32[]{:S(2)}) copy-start(bf16[2,256,2048]{2,1,0:T(8,128)(2,1)} %param.18) | copy-start | bytes 6291460
  62.6 3.2 copy-start.3
  64.1 305.1 %copy-start.18 = (f32[1,2048]{1,0:T(1,128)}, f32[1,2048]{1,0:T(1,128)S(1)}, u32[]{:S(2)}) copy-start(f32[1,2048]{1,0:T(1,128)S(1)} %get-tuple-element.134.refs_2_) | copy-start | bytes 24580
  64.1 1.8 copy-start
  64.1 1.8 copy-start.1
  64.1 1.9 copy-start.2
  112.5 1.3 copy-start.5
  229.6 3.4 copy-start.6
  229.6 3.8 copy-start.9
  229.6 4.4 copy-start.13
  238.8 83.3 %copy-start.20 = (f32[8,2048]{1,0:T(8,128)S(1)}, f32[8,2048]{1,0:T(8,128)}, u32[]{:S(2)}) copy-start(f32[8,2048]{1,0:T(8,128)} %get-tuple-element.89) | copy-start | bytes 196612
  322.7 40.4 %copy-start.8 = (bf16[512,1024]{1,0:T(8,128)(2,1)S(1)}, bf16[512,1024]{1,0:T(8,128)(2,1)}, u32[]{:S(2)}) copy-start(bf16[512,1024]{1,0:T(8,128)(2,1)} %copy-done.7) | copy-start | bytes 3145732
  363.2 6.0 %copy-start.19 = (f32[1,2048]{1,0:T(1,128)S(1)}, f32[1,2048]{1,0:T(1,128)}, u32[]{:S(2)}) copy-start(f32[1,2048]{1,0:T(1,128)} %get-tuple-element.135.gain_ref) | copy-start | bytes 24580
  369.9 73.8 %copy-start.14 = (f32[256,1024]{1,0:T(8,128)S(1)}, f32[256,1024]{1,0:T(8,128)}, u32[]{:S(2)}) copy-start(f32[256,1024]{1,0:T(8,128)} %get-tuple-element.96) | copy-start | bytes 3145732
  443.7 5.2 %copy-start.10 = (bf16[512,2048]{1,0:T(8,128)(2,1)S(1)}, bf16[512,2048]{1,0:T(8,128)(2,1)}, u32[]{:S(2)}) copy-start(bf16[512,2048]{1,0:T(8,128)(2,1)} %get-tuple-element.90) | copy-start | bytes 6291460
  455.4 4.1 copy-start.11
  (9 other events, 6.9 us)
Sparse Core Ops, SparseCore 0:
  9.6 16.3 all-gather.8
  27.5 14.8 all-gather.14
  44.5 14.8 all-gather.12
  60.8 14.8 all-gather.10

commit v8 on v7

--- a/solution.py
+++ b/solution.py
@@ -616,6 +616,7 @@
 
 
 piece = 16
+forward_piece = 32
 slots_held = 4
 unroll = 4
 
@@ -694,7 +695,7 @@
     local = rows // seqs
     states = rate.shape[0]
     width = lax.axis_size("ctx")
-    pieces = local // piece
+    pieces = local // forward_piece
 
     def kernel(
         low_ref, act_ref, z_ref, small_ref, rate_ref, w_ref,
@@ -754,7 +755,7 @@
 
             def save(k, slot):
                 return pltpu.make_async_copy(
-                    held.at[slot], kept_ref.at[pl.ds(seq * local + k * piece, piece)], out_sem.at[slot]
+                    held.at[slot], kept_ref.at[pl.ds(seq * local + k * forward_piece, forward_piece)], out_sem.at[slot]
                 )
 
             def one_piece(k, carried):
@@ -768,7 +769,7 @@
                     values = list(values)
                     for u in range(unroll):
                         inside = i * unroll + u
-                        t = seq * local + k * piece + inside
+                        t = seq * local + k * forward_piece + inside
                         s, d = tile(size3, t), tile(drive3, t)
                         acc = [None] * 4
                         for n in range(states):
@@ -779,7 +780,7 @@
                         y3[pl.ds(pl.multiple_of(t * 8, 8), 8), :] = (acc[0] + acc[1]) + (acc[2] + acc[3])
                     return tuple(values)
 
-                carried = lax.fori_loop(0, piece // unroll, second_pass, carried)
+                carried = lax.fori_loop(0, forward_piece // unroll, second_pass, carried)
                 save(k, slot).start()
                 return carried
 
@@ -825,7 +826,7 @@
             pltpu.VMEM((rows * 8, 128), f32),
             pltpu.VMEM((seqs, states + 1, 8, 128), f32),
             pltpu.VMEM((width, seqs, states + 1, 8, 128), f32),
-            pltpu.VMEM((2, piece, states, 8, 128), f32),
+            pltpu.VMEM((2, forward_piece, states, 8, 128), f32),
             pltpu.VMEM((rows * states, 128), f32),
             pltpu.VMEM((rows * states, 128), f32),
             pltpu.VMEM((rows, rank), bf16),

time: 472 us -> 467 us (0.989)
  Pallas kernels: 385 us -> 380 us
  transfers between devices with their start and end apart: 4 -> 4, of which waited for: 0 -> 0; matrix products, arithmetic and copies ran while one was open for 4% -> 4% of each run, Pallas kernels for 18% -> 17%
where the time goes in v8:
time: 467 us; the launch traced here: 463 us
  Pallas kernels  380 us (81%)
  local copies, waits for them, and re-layouts  41.2 us (9%)
  between operations  14.2 us (3%)
  matrix products  14.1 us (3%)
  other arithmetic  11 us (2%)
    pallas_call x1, Pallas kernels, feed_forward(): pl.pallas_call(kernel, out_shape=[half, wide, half, wide, sds((8, width),...  115 us
    pallas_call x1, Pallas kernels, scan_backward(): pl.pallas_call(kernel, out_shape=[flat, flat, sums, sums, jax.ShapeDtypeS...  80.2 us
    pallas_call x1, Pallas kernels, tp_sum(): pl.pallas_call(kernel, out_shape=[jax.ShapeDtypeStruct(partial.shape, out...  67 us
    pallas_call x1, Pallas kernels, scan_forward(): pl.pallas_call(kernel, out_shape=[jax.ShapeDtypeStruct((rows, channels),...  41.2 us
    pallas_call x1, Pallas kernels, scan_tail(): pl.pallas_call(kernel, out_shape=[jax.ShapeDtypeStruct((width, 2 * inner)...  39.5 us
    pallas_call x1, Pallas kernels, front(): pl.pallas_call(kernel, out_shape=[sds((2, shards * part, inner), bf16), s...  37.5 us
    unnamed x69, local copies, waits for them, and re-layouts  19.2 us
  transfers between devices with their start and end apart: 4, of which 0 were waited for; matrix products, arithmetic and copies ran while one was open for 4% of the time, Pallas kernels for 17%

profile of v8, /device:TPU:0, one launch (start us, length us, event | category | flops | bytes accessed | tf_op | source)
XLA Modules:
  0.0 462.7 jit_solution(10803952542672867356)
XLA Ops:
  8.7 3.5 copy.47
  12.2 2.5 fusion.21
  15.5 1.6 slice.72.tail_ref
  17.1 6.3 %copy.48 = bf16[1024,2,1024]{2,0,1:T(8,128)(2,1)} copy(bf16[1024,2,1024]{2,1,0:T(2,128)(2,1)} %param.20) | data formatting | bytes 8388608 | tf_op args[4]
  24.3 37.5 %shard_map.271 = (bf16[2,2048,1024]{2,1,0:T(8,128)(2,1)}, bf16[352,1024]{1,0:T(8,128)(2,1)}, bf16[16,2048]{1,0:T(8,128)(2,1)}, bf16[512,2048]{1,0:T(8,128)(2,1)}...) custom-call(bf16[512,2048]{1,0:T(8,128)(2,1)} %bitcast.54, ...), custom_call_target="tpu_custom_call" | custom-call | tf_op jit(solution)/shard_map/pallas_call | solution.py:575
  62.6 1.4 slice_convert_fusion
  64.1 1.7 fusion.fg_ref
  66.0 41.2 %shard_map.272 = (f32[512,1024]{1,0:T(8,128)S(1)}, bf16[512,1024]{1,0:T(8,128)(2,1)S(1)}, bf16[512,2048]{1,0:T(8,128)(2,1)}, f32[512,1024]{1,0:T(8,128)}, f32[51...) custom-call(f32[160,512]{1,0:T(8,128)S(1)} %copy-done.2, ...), custom_call_target="tpu_custom_call" | custom-call | tf_op jit(solution)/shard_map/pallas_call | solution.py:811
  110.2 114.8 %shard_map.273 = (bf16[512,2048]{1,0:T(8,128)(2,1)}, f32[512,2048]{1,0:T(8,128)}, bf16[512,2048]{1,0:T(8,128)(2,1)}, f32[512,2048]{1,0:T(8,128)}, f32[8,2048]{1,...) custom-call(bf16[512,2048]{1,0:T(8,128)(2,1)} %get-tuple-element.62.p_ref, ...), custom_call_target="tpu_custom_call" | custom-call | tf_op jit(solution)/shard_map/pallas_call | solution.py:1191
  225.0 3.3 fusion.1
  229.3 4.8 %multiply_convert_fusion = (bf16[512,1024]{1,0:T(8,128)(2,1)}, f32[512,1024]{1,0:T(8,128)}) fusion(f32[512,1024]{1,0:T(8,128)S(1)} %copy-done.13, f32[512,1024]{1,0:T(8,128)S(1)} %copy-done.6, f32[512,1024]{1,0:T(8,128)S(1)} %fusion.1, bf16[2048,1024]{1,0:T(8,128)(2,1)S(1)} %copy-done.9, bf16[512,2048]{1,0:T(8,128)(2,1)} %get-tuple-element.64), kind=kOutput, calls=%fused_computation.9 | convolution fusion | flops 1080557568 | bytes 12582912 | tf_op jit(solution)/shard_map/dot_general | solution.py:24
  234.1 80.2 %shard_map.274 = (f32[4096,128]{1,0:T(8,128)}, f32[4096,128]{1,0:T(8,128)}, f32[32,8,256]{2,1,0:T(8,128)}, f32[32,8,256]{2,1,0:T(8,128)}, f32[16,8,128]{2,1,0:T(...) custom-call(f32[4096,128]{1,0:T(8,128)} %get-tuple-element.60.refs_0_, ...), custom_call_target="tpu_custom_call" | custom-call | tf_op jit(solution)/shard_map/pallas_call | solution.py:1024
  314.3 1.5 bitcast_multiply_fusion.refs_3_
  318.1 39.5 %shard_map.275 = (bf16[2048,2048]{1,0:T(8,128)(2,1)}, bf16[512,2048]{1,0:T(8,128)(2,1)}, f32[8,2048]{1,0:T(8,128)}, bf16[2560,128]{1,0:T(8,128)(2,1)}) custom-call(f32[4096,128]{1,0:T(8,128)} %get-tuple-element.72.refs_0_, f32[4096,128]{1,0:T(8,128)} %get-tuple-element.73.refs_1_, f32[32,512]{1,0:T(8,128)} %pad_maximum_fusion.refs_2_, ...), custom_call_target="tpu_custom_call" | custom-call | tf_op jit(solution)/shard_map/pallas_call | solution.py:1418
  358.5 6.0 %convolution_convert_fusion = bf16[2048,1024]{1,0:T(8,128)(2,1)} fusion(bf16[512,2048]{1,0:T(8,128)(2,1)} %get-tuple-element.64, bf16[512,1024]{1,0:T(8,128)(2,1)S(1)} %copy-done.8), kind=kOutput, calls=%fused_computation.4 | convolution fusion | flops 2149580800 | bytes 7340032 | tf_op jit(solution)/shard_map/dot_general | solution.py:20
  365.2 67.0 %shard_map.276 = (bf16[512,2048]{1,0:T(8,128)(2,1)}, f32[256,2048]{1,0:T(8,128)}, f32[256,1024]{1,0:T(8,128)}, f32[320,128]{1,0:T(8,128)}, f32[16,128]{1,0:T(8,128)}) custom-call(bf16[512,2048]{1,0:T(8,128)(2,1)} %get-tuple-element.83.refs_0_, bf16[512,2048]{1,0:T(8,128)(2,1)} %bitcast.56, f32[1,2048]{1,0:T(1,128)} %copy-done.18, ...), custom_call_target="tpu_custom_call" | custom-call | tf_op jit(solution)/shard_map/pallas_call | solution.py:388
  436.0 1.5 slice.89
  437.5 1.5 slice.88
  440.3 1.3 slice_bitcast_fusion
  441.7 2.5 copy.39
  444.2 2.5 convert.14
  446.7 4.0 reshape.126
  450.7 4.1 reshape.127
  454.9 1.3 copy.55
  (102 shorter events, 16.9 us)
Async XLA Ops:
  7.2 58.7 %all-gather.9.cloned.1.call-start = ((), (), s32[]{:S(2)}) async-start(), calls=%async_computation | async-start | bytes 6291456 | tf_op jit(solution)/shard_map/all_gather | solution.py:1485
  7.9 102.2 %all-gather.15.cloned.1.call-start = ((), (), s32[]{:S(2)}) async-start(), calls=%async_computation.3 | async-start | bytes 6291456 | tf_op jit(solution)/shard_map/all_gather | solution.py:1488
  8.7 101.5 %all-gather.13.cloned.1.call-start = ((), (), s32[]{:S(2)}) async-start(), calls=%async_computation.2 | async-start | bytes 6291456 | tf_op jit(solution)/shard_map/all_gather | solution.py:1487
  14.8 95.4 %all-gather.11.cloned.1.call-start = ((), (), s32[]{:S(2)}) async-start(), calls=%async_computation.1 | async-start | bytes 6291456 | tf_op jit(solution)/shard_map/all_gather | solution.py:1487
  17.1 6.3 %copy-start.16 = (bf16[160,512]{1,0:T(8,128)(2,1)S(1)}, bf16[160,512]{1,0:T(8,128)(2,1)}, u32[]{:S(2)}) copy-start(bf16[160,512]{1,0:T(8,128)(2,1)} %param.23) | copy-start | bytes 491524
  17.1 6.3 %copy-start.17 = (bf16[128,512]{1,0:T(8,128)(2,1)S(1)}, bf16[128,512]{1,0:T(8,128)(2,1)}, u32[]{:S(2)}) copy-start(bf16[128,512]{1,0:T(8,128)(2,1)} %param.24) | copy-start | bytes 393220
  17.1 6.4 %copy-start.21 = (bf16[16,512]{1,0:T(8,128)(2,1)S(1)}, bf16[16,512]{1,0:T(8,128)(2,1)}, u32[]{:S(2)}) copy-start(bf16[16,512]{1,0:T(8,128)(2,1)} %param.26) | copy-start | bytes 49156
  17.1 6.4 %copy-start.22 = (bf16[4,512]{1,0:T(4,128)(2,1)S(1)}, bf16[4,512]{1,0:T(4,128)(2,1)}, u32[]{:S(2)}) copy-start(bf16[4,512]{1,0:T(4,128)(2,1)} %param.21) | copy-start | bytes 12292
  24.3 39.8 %copy-start.12 = (bf16[2,256,2048]{2,1,0:T(8,128)(2,1)S(1)}, bf16[2,256,2048]{2,1,0:T(8,128)(2,1)}, u32[]{:S(2)}) copy-start(bf16[2,256,2048]{2,1,0:T(8,128)(2,1)} %param.18) | copy-start | bytes 6291460
  62.6 3.2 copy-start.3
  64.1 300.5 %copy-start.18 = (f32[1,2048]{1,0:T(1,128)}, f32[1,2048]{1,0:T(1,128)S(1)}, u32[]{:S(2)}) copy-start(f32[1,2048]{1,0:T(1,128)S(1)} %get-tuple-element.134.refs_2_) | copy-start | bytes 24580
  64.1 1.8 copy-start
  64.1 1.8 copy-start.1
  64.1 1.9 copy-start.2
  107.9 1.3 copy-start.5
  225.0 3.4 copy-start.6
  225.0 3.8 copy-start.9
  225.0 4.4 copy-start.13
  234.1 83.3 %copy-start.20 = (f32[8,2048]{1,0:T(8,128)S(1)}, f32[8,2048]{1,0:T(8,128)}, u32[]{:S(2)}) copy-start(f32[8,2048]{1,0:T(8,128)} %get-tuple-element.89) | copy-start | bytes 196612
  318.1 40.4 %copy-start.8 = (bf16[512,1024]{1,0:T(8,128)(2,1)S(1)}, bf16[512,1024]{1,0:T(8,128)(2,1)}, u32[]{:S(2)}) copy-start(bf16[512,1024]{1,0:T(8,128)(2,1)} %copy-done.7) | copy-start | bytes 3145732
  358.5 6.0 %copy-start.19 = (f32[1,2048]{1,0:T(1,128)S(1)}, f32[1,2048]{1,0:T(1,128)}, u32[]{:S(2)}) copy-start(f32[1,2048]{1,0:T(1,128)} %get-tuple-element.135.gain_ref) | copy-start | bytes 24580
  365.2 73.8 %copy-start.14 = (f32[256,1024]{1,0:T(8,128)S(1)}, f32[256,1024]{1,0:T(8,128)}, u32[]{:S(2)}) copy-start(f32[256,1024]{1,0:T(8,128)} %get-tuple-element.96) | copy-start | bytes 3145732
  439.0 5.2 %copy-start.10 = (bf16[512,2048]{1,0:T(8,128)(2,1)S(1)}, bf16[512,2048]{1,0:T(8,128)(2,1)}, u32[]{:S(2)}) copy-start(bf16[512,2048]{1,0:T(8,128)(2,1)} %get-tuple-element.90) | copy-start | bytes 6291460
  450.7 4.1 copy-start.11
  (9 other events, 6.9 us)
Sparse Core Ops, SparseCore 0:
  9.6 16.3 all-gather.8
  27.5 14.8 all-gather.14
  44.5 14.8 all-gather.12
  60.8 14.8 all-gather.10
